TPU v7x, 32 devices: a whole 2x2x4 slice. The times are simulated.
32 devices in a mesh: seg: 4 (over y, x), pitch: 4 (over z), span: 2 (over core).
Axes of the slice: x: 2, y: 2, z: 4, core: 2. Of those that a mesh axis runs over, the one named last changes fastest.
Arguments:
- states: float32 [4, 5, 1024, 512], P('seg', None, 'pitch', 'span'), may hold values from -6 to 6
- forcing: float32 [4, 5, 1024, 512], P('seg', None, 'pitch', 'span'), may hold values from -6 to 6
- adv_pitch: float32 [5, 5], replicated, may hold values from -2.5 to 2.5
- adv_span: float32 [5, 5], replicated, may hold values from -2.5 to 2.5
- diffusion: float32 [5], replicated, may hold values from 0.1 to 0.4
Outputs:
- mismatch: float32 [4, 5, 1024, 512], P('seg', None, 'pitch', 'span')
- gradient: float32 [4, 5, 1024, 512], P('seg', None, 'pitch', 'span')
All inputs are finite; a program needn't handle non-finite values.
Results may differ from a plain program's by a relative error of at most 0.0001.
Values sent between devices are 32-bit elements; how exact they have to be, the bound alone decides.
No kernel may reach another device: no remote copies, remote signals or barrier semaphores. Data moves between devices by JAX's collectives and lax.ppermute only.
A program may use at most 64 MiB of HBM per device.

v0:
```python
import functools

import jax
import jax.numpy as jnp
from jax import lax
from jax.experimental import pallas as pl
from jax.experimental.pallas import tpu as pltpu
from jax.sharding import PartitionSpec as P

TIME_STEP = 0.25
SUBSTEPS = 2
TILE = 8
LANES = 128
STRIP = 24
MARGIN = 2 * TILE
VMEM_LIMIT = 32 * 1024 * 1024


def edge_strip(field_of, fields, rows, cols):
    lane = lax.broadcasted_iota(jnp.int32, (rows, LANES), 1)
    packed = jnp.zeros((rows, LANES), jnp.float32)
    for f in range(fields):
        first, last = field_of(f, 0), field_of(f, cols - LANES)
        ends = jnp.where(lane < LANES // 2, first, last)
        moved = pltpu.roll(ends, 4 * f + 2, 1)
        packed = jnp.where((lane >= 4 * f) & (lane < 4 * f + 4), moved, packed)
    return jnp.transpose(packed)[:STRIP]


def edges_kernel(cells, strip):
    fields, rows, cols = cells.shape
    strip[...] = edge_strip(lambda f, at: cells[f, :, at : at + LANES], fields, rows, cols)


def mismatch_kernel(ending, following, mismatch, strip):
    fields, rows, cols = mismatch.shape
    for f in range(fields):
        mismatch[f] = ending[f] - following[f]
    strip[...] = edge_strip(lambda f, at: mismatch[f, :, at : at + LANES], fields, rows, cols)


def substep(source, tile, coefficients, width):
    pitch, span, near, keep = coefficients
    fields, _, lanes = source.shape
    window = pl.ds(pl.multiple_of((tile - 1) * TILE, TILE), 3 * TILE)
    along_pitch, along_span, around, centre = [], [], [], []
    for g in range(fields):
        rows = source.at[g, window]
        here = rows[TILE : 2 * TILE, :]
        below = rows[TILE + 1 : 2 * TILE + 1, :][:, :width]
        above = rows[TILE - 1 : 2 * TILE - 1, :][:, :width]
        right = pltpu.roll(here, lanes - 1, 1)[:, :width]
        left = pltpu.roll(here, 1, 1)[:, :width]
        along_pitch.append(below - above)
        along_span.append(right - left)
        around.append((below + above) + (right + left))
        centre.append(here[:, :width])
    results = []
    for f in range(fields):
        total = keep[f] * centre[f] + near[f] * around[f]
        for g in range(fields):
            total = total + pitch[f][g] * along_pitch[g]
            total = total + span[f][g] * along_span[g]
        results.append(total)
    return results


def propagate_kernel(
    transposed, sign, scale, position, mat_pitch, mat_span, viscous, cells, extra, strip, upper, lower, result, first, second
):
    fields, rows, cols = cells.shape
    lanes = cols + LANES
    has_left = position[0] > 0
    has_right = position[0] < position[1] - 1
    factor = sign * TIME_STEP * 0.5

    def entry(matrix, f, g):
        return factor * (matrix[g, f] if transposed else matrix[f, g])

    pitch = [[entry(mat_pitch, f, g) for g in range(fields)] for f in range(fields)]
    span = [[entry(mat_span, f, g) for g in range(fields)] for f in range(fields)]
    near = [TIME_STEP * viscous[f] for f in range(fields)]
    keep = [1.0 - 4.0 * TIME_STEP * viscous[f] for f in range(fields)]
    coefficients = (pitch, span, near, keep)

    def within(shape):
        side = lax.broadcasted_iota(jnp.int32, shape, 1) < LANES // 2
        return jnp.where(side, has_right.astype(jnp.int32), has_left.astype(jnp.int32)) > 0

    corner_above = jnp.concatenate([upper[f, :, cols:] for f in range(STRIP // TILE)], axis=0)
    corner_below = jnp.concatenate([lower[f, :, cols:] for f in range(STRIP // TILE)], axis=0)
    along = jnp.concatenate([corner_above, strip[...], corner_below], axis=1)
    along = jnp.concatenate([along, jnp.zeros((LANES - STRIP, along.shape[1]), jnp.float32)], axis=0)
    turned = jnp.transpose(along)[LANES - MARGIN : LANES + rows + MARGIN]
    inside = within(turned.shape)
    for f in range(fields):
        side = pltpu.roll(turned, LANES - (4 * f + 2), 1)
        first[f, :, cols:] = jnp.where(inside, side, 0.0)
        first[f, MARGIN - TILE : MARGIN, :cols] = upper[f, :, :cols]
        first[f, MARGIN + rows : MARGIN + rows + TILE, :cols] = lower[f, :, :cols]
        first[f, MARGIN : MARGIN + rows, :cols] = cells[f]

    inside_tile = within((TILE, LANES))

    def step_one(tile, carry):
        for f, value in enumerate(substep(first, tile, coefficients, lanes)):
            second[f, pl.ds(pl.multiple_of(tile * TILE, TILE), TILE), :cols] = value[:, :cols]
            second[f, pl.ds(pl.multiple_of(tile * TILE, TILE), TILE), cols:] = jnp.where(inside_tile, value[:, cols:], 0.0)
        return carry

    lax.fori_loop(1, (MARGIN + rows) // TILE + 1, step_one, 0)

    def step_two(tile, carry):
        for f, value in enumerate(substep(second, tile, coefficients, cols)):
            at = pl.ds(pl.multiple_of(tile * TILE - MARGIN, TILE), TILE)
            result[f, at, :] = value + scale * extra[f, at, :]
        return carry

    lax.fori_loop(MARGIN // TILE, (MARGIN + rows) // TILE, step_two, 0)


def finish_kernel(adjoint, arrived, gradient):
    gradient[...] = adjoint[...] - arrived[...]


def in_vmem(count):
    return [pl.BlockSpec(memory_space=pltpu.VMEM)] * count


def in_smem(count):
    return [pl.BlockSpec(memory_space=pltpu.SMEM)] * count


PARAMS = pltpu.CompilerParams(vmem_limit_bytes=VMEM_LIMIT)


def edges_of(cells):
    return pl.pallas_call(
        edges_kernel,
        out_shape=jax.ShapeDtypeStruct((STRIP, cells.shape[1]), jnp.float32),
        in_specs=in_vmem(1),
        out_specs=pl.BlockSpec(memory_space=pltpu.VMEM),
        compiler_params=PARAMS,
    )(cells)


def mismatch_of(ending, following):
    fields, rows, cols = ending.shape
    return pl.pallas_call(
        mismatch_kernel,
        out_shape=(
            jax.ShapeDtypeStruct(ending.shape, jnp.float32),
            jax.ShapeDtypeStruct((STRIP, rows), jnp.float32),
        ),
        in_specs=in_vmem(2),
        out_specs=tuple(in_vmem(2)),
        compiler_params=PARAMS,
    )(ending, following)


def exchanged(cells, strip):
    fields, rows, cols = cells.shape
    count = lax.axis_size("span")
    if count == 2:
        sides = lax.ppermute(strip, "span", [(0, 1), (1, 0)])
    else:
        from_left = lax.ppermute(strip, "span", [(i, i + 1) for i in range(count - 1)])
        from_right = lax.ppermute(strip, "span", [(i + 1, i) for i in range(count - 1)])
        kind = lax.broadcasted_iota(jnp.int32, strip.shape, 0) % 4
        sides = jnp.where(kind < 2, from_left, from_right)

    def outer(row, lane):
        ends = sides[:, lane : lane + LANES].reshape(STRIP // TILE, TILE, LANES)
        ends = jnp.pad(ends, ((0, fields - STRIP // TILE), (0, 0), (0, 0)))
        return jnp.concatenate([cells[:, row : row + TILE, :], ends], axis=2)

    ring = lax.axis_size("pitch")
    upper = lax.ppermute(outer(rows - TILE, rows - LANES), "pitch", [(i, (i + 1) % ring) for i in range(ring)])
    lower = lax.ppermute(outer(0, 0), "pitch", [((i + 1) % ring, i) for i in range(ring)])
    return sides, upper, lower


def propagated(position, mat_pitch, mat_span, viscous, cells, extra, halos, transposed, sign, scale):
    fields, rows, cols = cells.shape
    wide = pltpu.VMEM((fields, rows + 2 * MARGIN, cols + LANES), jnp.float32)
    return pl.pallas_call(
        functools.partial(propagate_kernel, transposed, sign, scale),
        out_shape=jax.ShapeDtypeStruct(cells.shape, jnp.float32),
        in_specs=in_smem(4) + in_vmem(5),
        out_specs=pl.BlockSpec(memory_space=pltpu.VMEM),
        scratch_shapes=[wide, wide],
        compiler_params=PARAMS,
    )(position, mat_pitch, mat_span, viscous, cells, extra, *halos)


def passed_along(shard, by):
    count = lax.axis_size("seg")
    return lax.ppermute(shard, "seg", [(i, (i + by) % count) for i in range(count)])


def body(states, forcing, adv_pitch, adv_span, diffusion):
    start = states[0]
    position = jnp.stack([lax.axis_index("span"), lax.axis_size("span")]).astype(jnp.int32)
    following = passed_along(start, -1)
    halos = exchanged(start, edges_of(start))
    ending = propagated(position, adv_pitch, adv_span, diffusion, start, forcing[0], halos, False, -1.0, TIME_STEP)
    arrived = passed_along(ending, 1)
    mismatch, strip = mismatch_of(ending, following)
    halos = exchanged(mismatch, strip)
    adjoint = propagated(position, adv_pitch, adv_span, diffusion, mismatch, start, halos, True, 1.0, 1.0)
    gradient = adjoint - arrived
    return (mismatch[None], gradient[None])


def solution(mesh):
    whole = P("seg", None, "pitch", "span")
    return jax.shard_map(
        body,
        mesh=mesh,
        in_specs=(whole, whole, P(), P(), P()),
        out_specs=(whole, whole),
        check_vma=False,
    )
```

profile of v0, /device:TPU:0, one launch (start us, length us, event | category | flops | bytes accessed | tf_op | source)
XLA Modules:
  0.0 63.2 jit_solution(4955091502889624101)
XLA Ops:
  0.6 0.0 copy-start.6
  0.6 3.9 %collective-permute-start.3 = (f32[5,256,256]{2,1,0:T(8,128)}, f32[5,256,256]{2,1,0:T(8,128)S(1)}, u32[]{:S(2)}, u32[]{:S(2)}) collective-permute-start(f32[5,256,256]{2,1,0:T(8,128)} %bitcast.14), channel_id=1, source_target_pairs={{0,24},{8,0},{16,8},{24,16},{1,25},{9,1},{17,9},{25,17},{2,26},{10... | collective-permute-start | bytes 3932168 | tf_op jit(solution)/shard_map/ppermute | solution.py:198
  4.6 0.0 copy-start
  4.6 1.3 %copy-done = f32[1,5,256,256]{3,2,1,0:T(8,128)S(1)} copy-done((f32[1,5,256,256]{3,2,1,0:T(8,128)S(1)}, f32[1,5,256,256]{3,2,1,0:T(8,128)}, u32[]{:S(2)}) %copy-start) | copy-done | bytes 1310744
  5.9 0.0 copy-start.1
  5.9 0.0 copy-start.4
  5.9 0.0 copy-start.5
  5.9 0.3 shard_map.68
  6.2 0.0 collective-permute-start
  6.3 1.2 %collective-permute-done.strip = f32[24,256]{1,0:T(8,128)S(1)} collective-permute-done((f32[24,256]{1,0:T(8,128)S(1)}, f32[24,256]{1,0:T(8,128)S(1)}, u32[]{:S(2)}, u32[]{:S(2)}) %collective-permute-start) | collective-permute-done | bytes 24608 | tf_op jit(solution)/shard_map/ppermute | solution.py:165
  7.5 1.6 %collective-permute-start.1 = (f32[5,8,384]{2,1,0:T(8,128)S(1)}, f32[5,8,384]{2,1,0:T(8,128)S(1)}, u32[]{:S(2)}, u32[]{:S(2)}) collective-permute-start(f32[5,8,384]{2,1,0:T(8,128)S(1)} %select_maximum_fusion.3), channel_id=1, source_target_pairs={{0,2},{2,4},{4,6},{6,0},{1,3},{3,5},{5,7},{7,1},{8,10},{10,12},{12... | collective-permute-start | bytes 184328 | tf_op jit(solution)/shard_map/ppermute | solution.py:178
  9.1 2.2 %collective-permute-start.2 = (f32[5,8,384]{2,1,0:T(8,128)S(1)}, f32[5,8,384]{2,1,0:T(8,128)S(1)}, u32[]{:S(2)}, u32[]{:S(2)}) collective-permute-start(f32[5,8,384]{2,1,0:T(8,128)S(1)} %select_maximum_fusion.2), channel_id=1, source_target_pairs={{2,0},{4,2},{6,4},{0,6},{3,1},{5,3},{7,5},{1,7},{10,8},{12,10},{14... | collective-permute-start | bytes 184328 | tf_op jit(solution)/shard_map/ppermute | solution.py:179
  11.3 0.1 pad_add_fusion.position
  11.4 2.2 %collective-permute-done.1.upper = f32[5,8,384]{2,1,0:T(8,128)S(1)} collective-permute-done((f32[5,8,384]{2,1,0:T(8,128)S(1)}, f32[5,8,384]{2,1,0:T(8,128)S(1)}, u32[]{:S(2)}, u32[]{:S(2)}) %collective-permute-start.1) | collective-permute-done | bytes 61472 | tf_op jit(solution)/shard_map/ppermute | solution.py:178
  13.6 0.6 collective-permute-done.2.lower
  14.2 0.0 copy-done.6
  14.2 0.0 copy-done.1
  14.2 0.0 copy-done.4
  14.2 0.0 copy-done.5
  14.2 0.0 copy-start.3
  14.2 1.3 %copy-done.3 = f32[1,5,256,256]{3,2,1,0:T(8,128)S(1)} copy-done((f32[1,5,256,256]{3,2,1,0:T(8,128)S(1)}, f32[1,5,256,256]{3,2,1,0:T(8,128)}, u32[]{:S(2)}) %copy-start.3) | copy-done | bytes 1310744
  15.6 10.1 %shard_map.69.ending = f32[5,256,256]{2,1,0:T(8,128)S(1)} custom-call(s32[2]{0:T(128)S(1)} %pad_add_fusion.position, f32[5,5]{1,0:T(8,128)S(1)} %copy-done.4, f32[5,5]{1,0:T(8,128)S(1)} %copy-done.5, f32[5]{0:T(128)S(1)} %copy-done.6, f32[5,256,256]{2,1,0:T(8,128)S(1)} %bitcast.17, f32[5,256,256]{2,1,0:T(8,128)S(1)} %bitcast.20, ...), custom_call_target="tpu_custom_call" | custom-call | tf_op jit(solution)/shard_map/pallas_call | solution.py:186
  25.6 0.1 collective-permute-start.7
  25.7 8.4 %collective-permute-done.3.following = f32[5,256,256]{2,1,0:T(8,128)S(1)} collective-permute-done((f32[5,256,256]{2,1,0:T(8,128)}, f32[5,256,256]{2,1,0:T(8,128)S(1)}, u32[]{:S(2)}, u32[]{:S(2)}) %collective-permute-start.3) | collective-permute-done | bytes 1310752 | tf_op jit(solution)/shard_map/ppermute | solution.py:198
  34.1 1.2 %shard_map.70 = (f32[5,256,256]{2,1,0:T(8,128)}, f32[24,256]{1,0:T(8,128)S(1)}) custom-call(f32[5,256,256]{2,1,0:T(8,128)S(1)} %shard_map.69.ending, f32[5,256,256]{2,1,0:T(8,128)S(1)} %collective-permute-done.3.following), custom_call_target="tpu_custom_call" | custom-call | tf_op jit(solution)/shard_map/pallas_call | solution.py:149
  35.3 0.0 collective-permute-start.4
  35.3 0.8 %fusion = (f32[5,8,256]{2,1,0:T(8,128)S(1)}, f32[5,8,256]{2,1,0:T(8,128)S(1)}) fusion(f32[5,256,256]{2,1,0:T(8,128)} %get-tuple-element.4.cells), kind=kLoop, calls=%fused_computation.11 | loop fusion | bytes 163840 | tf_op jit(solution)/shard_map/slice | solution.py:175
  36.1 0.4 collective-permute-done.4.strip
  36.5 3.7 %collective-permute-start.6 = (f32[5,8,384]{2,1,0:T(8,128)S(1)}, f32[5,8,384]{2,1,0:T(8,128)S(1)}, u32[]{:S(2)}, u32[]{:S(2)}) collective-permute-start(f32[5,8,384]{2,1,0:T(8,128)S(1)} %select_maximum_fusion), channel_id=1, source_target_pairs={{2,0},{4,2},{6,4},{0,6},{3,1},{5,3},{7,5},{1,7},{10,8},{12,10},{14... | collective-permute-start | bytes 184328 | tf_op jit(solution)/shard_map/ppermute | solution.py:179
  40.2 0.0 collective-permute-start.5
  40.2 2.2 %collective-permute-done.6.lower = f32[5,8,384]{2,1,0:T(8,128)S(1)} collective-permute-done((f32[5,8,384]{2,1,0:T(8,128)S(1)}, f32[5,8,384]{2,1,0:T(8,128)S(1)}, u32[]{:S(2)}, u32[]{:S(2)}) %collective-permute-start.6) | collective-permute-done | bytes 61472 | tf_op jit(solution)/shard_map/ppermute | solution.py:179
  42.4 3.8 %collective-permute-done.5.upper = f32[5,8,384]{2,1,0:T(8,128)S(1)} collective-permute-done((f32[5,8,384]{2,1,0:T(8,128)S(1)}, f32[5,8,384]{2,1,0:T(8,128)S(1)}, u32[]{:S(2)}, u32[]{:S(2)}) %collective-permute-start.5) | collective-permute-done | bytes 61472 | tf_op jit(solution)/shard_map/ppermute | solution.py:178
  46.2 0.0 copy-start.2
  46.2 1.3 %copy-done.2 = f32[5,256,256]{2,1,0:T(8,128)S(1)} copy-done((f32[5,256,256]{2,1,0:T(8,128)S(1)}, f32[5,256,256]{2,1,0:T(8,128)}, u32[]{:S(2)}) %copy-start.2) | copy-done | bytes 1310744
  47.5 10.1 %shard_map.71 = f32[5,256,256]{2,1,0:T(8,128)S(1)} custom-call(s32[2]{0:T(128)S(1)} %pad_add_fusion.position, f32[5,5]{1,0:T(8,128)S(1)} %copy-done.4, f32[5,5]{1,0:T(8,128)S(1)} %copy-done.5, f32[5]{0:T(128)S(1)} %copy-done.6, f32[5,256,256]{2,1,0:T(8,128)S(1)} %copy-done.2, f32[5,256,256]{2,1,0:T(8,128)S(1)} %bitcast.18, ...), custom_call_target="tpu_custom_call" | custom-call | tf_op jit(solution)/shard_map/pallas_call | solution.py:186
  57.6 4.3 %collective-permute-done.7 = f32[5,256,256]{2,1,0:T(8,128)S(1)} collective-permute-done((f32[5,256,256]{2,1,0:T(8,128)S(1)}, f32[5,256,256]{2,1,0:T(8,128)S(1)}, u32[]{:S(2)}, u32[]{:S(2)}) %collective-permute-start.7) | collective-permute-done | bytes 1310752 | tf_op jit(solution)/shard_map/ppermute | solution.py:198
  61.9 1.3 %subtract_bitcast_fusion = f32[1,5,256,256]{3,2,1,0:T(8,128)} fusion(f32[5,256,256]{2,1,0:T(8,128)S(1)} %shard_map.71, f32[5,256,256]{2,1,0:T(8,128)S(1)} %collective-permute-done.7), kind=kLoop, calls=%fused_computation | loop fusion | flops 327680 | bytes 3932160 | tf_op jit(solution)/shard_map/broadcast_in_dim | solution.py:212
  (7 shorter events, 0.0 us)
Async XLA Ops:
  0.6 13.6 %copy-start.6 = (f32[5]{0:T(128)S(1)}, f32[5]{0:T(128)}, u32[]{:S(2)}) copy-start(f32[5]{0:T(128)} %viscous.3) | copy-start | bytes 64
  0.6 33.4 %collective-permute-start.3 = (f32[5,256,256]{2,1,0:T(8,128)}, f32[5,256,256]{2,1,0:T(8,128)S(1)}, u32[]{:S(2)}, u32[]{:S(2)}) collective-permute-start(f32[5,256,256]{2,1,0:T(8,128)} %bitcast.14), channel_id=1, source_target_pairs={{0,24},{8,0},{16,8},{24,16},{1,25},{9,1},{17,9},{25,17},{2,26},{10... | collective-permute-start | bytes 3932168 | tf_op jit(solution)/shard_map/ppermute | solution.py:198
  4.6 1.4 %copy-start = (f32[1,5,256,256]{3,2,1,0:T(8,128)S(1)}, f32[1,5,256,256]{3,2,1,0:T(8,128)}, u32[]{:S(2)}) copy-start(f32[1,5,256,256]{3,2,1,0:T(8,128)} %param.5) | copy-start | bytes 3932164
  5.9 8.3 %copy-start.1 = (f32[1,5,256,256]{3,2,1,0:T(8,128)S(1)}, f32[1,5,256,256]{3,2,1,0:T(8,128)}, u32[]{:S(2)}) copy-start(f32[1,5,256,256]{3,2,1,0:T(8,128)} %param.5) | copy-start | bytes 3932164
  5.9 8.3 %copy-start.4 = (f32[5,5]{1,0:T(8,128)S(1)}, f32[5,5]{1,0:T(8,128)}, u32[]{:S(2)}) copy-start(f32[5,5]{1,0:T(8,128)} %mat_pitch.3) | copy-start | bytes 304
  5.9 8.3 %copy-start.5 = (f32[5,5]{1,0:T(8,128)S(1)}, f32[5,5]{1,0:T(8,128)}, u32[]{:S(2)}) copy-start(f32[5,5]{1,0:T(8,128)} %mat_span.3) | copy-start | bytes 304
  6.2 1.2 %collective-permute-start = (f32[24,256]{1,0:T(8,128)S(1)}, f32[24,256]{1,0:T(8,128)S(1)}, u32[]{:S(2)}, u32[]{:S(2)}) collective-permute-start(f32[24,256]{1,0:T(8,128)S(1)} %shard_map.68), channel_id=1, source_target_pairs={{0,1},{1,0},{2,3},{3,2},{4,5},{5,4},{6,7},{7,6},{8,9},{9,8},{10,11... | collective-permute-start | bytes 73736 | tf_op jit(solution)/shard_map/ppermute | solution.py:165
  7.5 6.2 %collective-permute-start.1 = (f32[5,8,384]{2,1,0:T(8,128)S(1)}, f32[5,8,384]{2,1,0:T(8,128)S(1)}, u32[]{:S(2)}, u32[]{:S(2)}) collective-permute-start(f32[5,8,384]{2,1,0:T(8,128)S(1)} %select_maximum_fusion.3), channel_id=1, source_target_pairs={{0,2},{2,4},{4,6},{6,0},{1,3},{3,5},{5,7},{7,1},{8,10},{10,12},{12... | collective-permute-start | bytes 184328 | tf_op jit(solution)/shard_map/ppermute | solution.py:178
  9.1 5.1 %collective-permute-start.2 = (f32[5,8,384]{2,1,0:T(8,128)S(1)}, f32[5,8,384]{2,1,0:T(8,128)S(1)}, u32[]{:S(2)}, u32[]{:S(2)}) collective-permute-start(f32[5,8,384]{2,1,0:T(8,128)S(1)} %select_maximum_fusion.2), channel_id=1, source_target_pairs={{2,0},{4,2},{6,4},{0,6},{3,1},{5,3},{7,5},{1,7},{10,8},{12,10},{14... | collective-permute-start | bytes 184328 | tf_op jit(solution)/shard_map/ppermute | solution.py:179
  14.2 1.3 %copy-start.3 = (f32[1,5,256,256]{3,2,1,0:T(8,128)S(1)}, f32[1,5,256,256]{3,2,1,0:T(8,128)}, u32[]{:S(2)}) copy-start(f32[1,5,256,256]{3,2,1,0:T(8,128)} %param.6) | copy-start | bytes 3932164
  25.6 36.3 %collective-permute-start.7 = (f32[5,256,256]{2,1,0:T(8,128)S(1)}, f32[5,256,256]{2,1,0:T(8,128)S(1)}, u32[]{:S(2)}, u32[]{:S(2)}) collective-permute-start(f32[5,256,256]{2,1,0:T(8,128)S(1)} %shard_map.69.ending), channel_id=1, source_target_pairs={{0,8},{8,16},{16,24},{24,0},{1,9},{9,17},{17,25},{25,1},{2,10},{10... | collective-permute-start | bytes 3932168 | tf_op jit(solution)/shard_map/ppermute | solution.py:198
  35.3 1.2 %collective-permute-start.4 = (f32[24,256]{1,0:T(8,128)S(1)}, f32[24,256]{1,0:T(8,128)S(1)}, u32[]{:S(2)}, u32[]{:S(2)}) collective-permute-start(f32[24,256]{1,0:T(8,128)S(1)} %get-tuple-element.5), channel_id=1, source_target_pairs={{0,1},{1,0},{2,3},{3,2},{4,5},{5,4},{6,7},{7,6},{8,9},{9,8},{10,11... | collective-permute-start | bytes 73736 | tf_op jit(solution)/shard_map/ppermute | solution.py:165
  36.5 5.9 %collective-permute-start.6 = (f32[5,8,384]{2,1,0:T(8,128)S(1)}, f32[5,8,384]{2,1,0:T(8,128)S(1)}, u32[]{:S(2)}, u32[]{:S(2)}) collective-permute-start(f32[5,8,384]{2,1,0:T(8,128)S(1)} %select_maximum_fusion), channel_id=1, source_target_pairs={{2,0},{4,2},{6,4},{0,6},{3,1},{5,3},{7,5},{1,7},{10,8},{12,10},{14... | collective-permute-start | bytes 184328 | tf_op jit(solution)/shard_map/ppermute | solution.py:179
  40.2 6.0 %collective-permute-start.5 = (f32[5,8,384]{2,1,0:T(8,128)S(1)}, f32[5,8,384]{2,1,0:T(8,128)S(1)}, u32[]{:S(2)}, u32[]{:S(2)}) collective-permute-start(f32[5,8,384]{2,1,0:T(8,128)S(1)} %select_maximum_fusion.1), channel_id=1, source_target_pairs={{0,2},{2,4},{4,6},{6,0},{1,3},{3,5},{5,7},{7,1},{8,10},{10,12},{12... | collective-permute-start | bytes 184328 | tf_op jit(solution)/shard_map/ppermute | solution.py:178
  46.2 1.3 %copy-start.2 = (f32[5,256,256]{2,1,0:T(8,128)S(1)}, f32[5,256,256]{2,1,0:T(8,128)}, u32[]{:S(2)}) copy-start(f32[5,256,256]{2,1,0:T(8,128)} %get-tuple-element.4.cells) | copy-start | bytes 3932164
where the time goes:
time: 63.4 us; the launch traced here: 63.2 us
  waiting for transfers between devices  23.1 us (36%)
  Pallas kernels  21.6 us (34%)
  starting transfers between devices  11.6 us (18%)
  local copies, waits for them, and re-layouts  4.81 us (8%)
  other arithmetic  1.35 us (2%)
  between operations  0.72 us (1%)
    pallas_call x2, Pallas kernels, propagated(): pl.pallas_call(functools.partial(propagate_kernel, transposed, sign, scal...  20.1 us
    ppermute x2, waiting for transfers between devices, passed_along(): lax.ppermute(shard, 'seg', [(i, (i + by) % count) for i in range(count)])  12.7 us
    ppermute x2, waiting for transfers between devices, exchanged(): lax.ppermute(outer(rows - TILE, rows - LANES), 'pitch', [(i, (i + 1) % ri...  5.98 us
    ppermute x2, starting transfers between devices, exchanged(): lax.ppermute(outer(0, 0), 'pitch', [((i + 1) % ring, i) for i in range(ri...  5.9 us
    ppermute x2, starting transfers between devices, passed_along(): lax.ppermute(shard, 'seg', [(i, (i + by) % count) for i in range(count)])  4 us
    unnamed x14, local copies, waits for them, and re-layouts  3.99 us
    ppermute x2, waiting for transfers between devices, exchanged(): lax.ppermute(outer(0, 0), 'pitch', [((i + 1) % ring, i) for i in range(ri...  2.82 us
    ppermute x2, starting transfers between devices, exchanged(): lax.ppermute(outer(rows - TILE, rows - LANES), 'pitch', [(i, (i + 1) % ri...  1.63 us
  transfers between devices with their start and end apart: 8, of which 8 were waited for; matrix products, arithmetic and copies ran while one was open for 1% of the time, Pallas kernels for 34%

commit v1 on v0

--- a/solution.py
+++ b/solution.py
@@ -32,10 +32,11 @@
     strip[...] = edge_strip(lambda f, at: cells[f, :, at : at + LANES], fields, rows, cols)
 
 
-def mismatch_kernel(ending, following, mismatch, strip):
+def mismatch_kernel(lead, last, following, mismatch, again, strip):
     fields, rows, cols = mismatch.shape
     for f in range(fields):
-        mismatch[f] = ending[f] - following[f]
+        ending = lead[f] if f < lead.shape[0] else last[f - lead.shape[0]]
+        mismatch[f] = again[f] = ending - following[f]
     strip[...] = edge_strip(lambda f, at: mismatch[f, :, at : at + LANES], fields, rows, cols)
 
 
@@ -66,7 +67,7 @@
 
 
 def propagate_kernel(
-    transposed, sign, scale, position, mat_pitch, mat_span, viscous, cells, extra, strip, upper, lower, result, first, second
+    transposed, sign, scale, position, mat_pitch, mat_span, viscous, cells, extra, strip, upper, lower, lead, last, first, second
 ):
     fields, rows, cols = cells.shape
     lanes = cols + LANES
@@ -113,14 +114,19 @@
     def step_two(tile, carry):
         for f, value in enumerate(substep(second, tile, coefficients, cols)):
             at = pl.ds(pl.multiple_of(tile * TILE - MARGIN, TILE), TILE)
-            result[f, at, :] = value + scale * extra[f, at, :]
+            result, place = (lead, f) if f < lead.shape[0] else (last, f - lead.shape[0])
+            result[place, at, :] = value + scale * extra[f, at, :]
         return carry
 
     lax.fori_loop(MARGIN // TILE, (MARGIN + rows) // TILE, step_two, 0)
 
 
-def finish_kernel(adjoint, arrived, gradient):
-    gradient[...] = adjoint[...] - arrived[...]
+def lead_kernel(adjoint, arrived, gradient):
+    gradient[0] = adjoint[...] - arrived[...]
+
+
+def last_kernel(adjoint, arrived, begun, gradient):
+    gradient[0] = adjoint[...] - arrived[...]
 
 
 def in_vmem(count):
@@ -144,18 +150,39 @@
     )(cells)
 
 
-def mismatch_of(ending, following):
-    fields, rows, cols = ending.shape
+def mismatch_of(lead, last, following):
+    whole = jax.ShapeDtypeStruct(following.shape, jnp.float32)
     return pl.pallas_call(
         mismatch_kernel,
-        out_shape=(
-            jax.ShapeDtypeStruct(ending.shape, jnp.float32),
-            jax.ShapeDtypeStruct((STRIP, rows), jnp.float32),
-        ),
-        in_specs=in_vmem(2),
-        out_specs=tuple(in_vmem(2)),
-        compiler_params=PARAMS,
-    )(ending, following)
+        out_shape=(whole, whole, jax.ShapeDtypeStruct((STRIP, following.shape[1]), jnp.float32)),
+        in_specs=in_vmem(3),
+        out_specs=tuple(in_vmem(3)),
+        compiler_params=PARAMS,
+    )(lead, last, following)
+
+
+def gradient_of(adjoint, arrived):
+    count, rows, cols = adjoint[0].shape
+    rest = adjoint[1].shape[0]
+    whole = jax.ShapeDtypeStruct((1, count + rest, rows, cols), jnp.float32)
+    field = pl.BlockSpec((1, rows, cols), lambda f: (f, 0, 0))
+    begun = pl.pallas_call(
+        lead_kernel,
+        grid=(count,),
+        out_shape=whole,
+        in_specs=[field, field],
+        out_specs=pl.BlockSpec((1, 1, rows, cols), lambda f: (0, f, 0, 0)),
+        compiler_params=PARAMS,
+    )(adjoint[0], arrived[0])
+    return pl.pallas_call(
+        last_kernel,
+        grid=(1,),
+        out_shape=whole,
+        in_specs=in_vmem(2) + [pl.BlockSpec(memory_space=pl.ANY)],
+        out_specs=pl.BlockSpec((1, rest, rows, cols), lambda f: (0, count // rest, 0, 0)),
+        input_output_aliases={2: 0},
+        compiler_params=PARAMS,
+    )(adjoint[1], arrived[1], begun)
 
 
 def exchanged(cells, strip):
@@ -185,9 +212,9 @@
     wide = pltpu.VMEM((fields, rows + 2 * MARGIN, cols + LANES), jnp.float32)
     return pl.pallas_call(
         functools.partial(propagate_kernel, transposed, sign, scale),
-        out_shape=jax.ShapeDtypeStruct(cells.shape, jnp.float32),
+        out_shape=tuple(jax.ShapeDtypeStruct((n, rows, cols), jnp.float32) for n in (fields - 1, 1)),
         in_specs=in_smem(4) + in_vmem(5),
-        out_specs=pl.BlockSpec(memory_space=pltpu.VMEM),
+        out_specs=tuple(in_vmem(2)),
         scratch_shapes=[wide, wide],
         compiler_params=PARAMS,
     )(position, mat_pitch, mat_span, viscous, cells, extra, *halos)
@@ -204,12 +231,11 @@
     following = passed_along(start, -1)
     halos = exchanged(start, edges_of(start))
     ending = propagated(position, adv_pitch, adv_span, diffusion, start, forcing[0], halos, False, -1.0, TIME_STEP)
-    arrived = passed_along(ending, 1)
-    mismatch, strip = mismatch_of(ending, following)
-    halos = exchanged(mismatch, strip)
-    adjoint = propagated(position, adv_pitch, adv_span, diffusion, mismatch, start, halos, True, 1.0, 1.0)
-    gradient = adjoint - arrived
-    return (mismatch[None], gradient[None])
+    arrived = [passed_along(part, 1) for part in ending]
+    mismatch, again, strip = mismatch_of(*ending, following)
+    halos = exchanged(again, strip)
+    adjoint = propagated(position, adv_pitch, adv_span, diffusion, again, start, halos, True, 1.0, 1.0)
+    return (mismatch[None], gradient_of(adjoint, arrived))
 
 
 def solution(mesh):

time: 63.4 us -> 62.8 us (level)
  Pallas kernels: 21.6 us -> 23.9 us
  starting transfers between devices: 11.6 us -> 13.8 us
  local copies, waits for them, and re-layouts: 4.81 us -> 2.7 us
  waiting for transfers between devices: 23.1 us -> 21.4 us
  other arithmetic: 1.35 us -> 0.1 us
    pallas_call x1 -> x3, Pallas kernels: 1.21 us -> 3.53 us  [the longest x1 1.55 us: gradient_of(): pl.pallas_call(lead_kernel, grid=(count,), out_shape=whole, in_specs=[fie...]
    ppermute x2 -> x3, starting transfers between devices: 4 us -> 5.96 us  [passed_along(): lax.ppermute(shard, 'seg', [(i, (i + by) % count) for i in range(count)])]
    ppermute x2, waiting for transfers between devices: 2.82 us -> 1.16 us  [exchanged(): lax.ppermute(outer(0, 0), 'pitch', [((i + 1) % ring, i) for i in range(ri...]
    ppermute x2, starting transfers between devices: 1.63 us -> 3.26 us  [exchanged(): lax.ppermute(outer(rows - TILE, rows - LANES), 'pitch', [(i, (i + 1) % ri...]
    ppermute x2, waiting for transfers between devices: 5.98 us -> 4.49 us  [exchanged(): lax.ppermute(outer(rows - TILE, rows - LANES), 'pitch', [(i, (i + 1) % ri...]
    ppermute x2, starting transfers between devices: 5.9 us -> 4.49 us  [exchanged(): lax.ppermute(outer(0, 0), 'pitch', [((i + 1) % ring, i) for i in range(ri...]
    unnamed x14 -> x12, local copies, waits for them, and re-layouts: 3.99 us -> 2.68 us
    broadcast_in_dim x1 -> x0, other arithmetic: 1.25 us -> none  [body(): return (mismatch[None], gradient[None])]
  transfers between devices with their start and end apart: 8 -> 9, of which waited for: 8 -> 9; matrix products, arithmetic and copies ran while one was open for 1% -> 0% of each run, Pallas kernels for 34% -> 37%
where the time goes in v1:
time: 62.8 us; the launch traced here: 62.6 us
  Pallas kernels  23.9 us (38%)
  waiting for transfers between devices  21.4 us (34%)
  starting transfers between devices  13.8 us (22%)
  local copies, waits for them, and re-layouts  2.7 us (4%)
  between operations  0.72 us (1%)
    pallas_call x2, Pallas kernels, propagated(): pl.pallas_call(functools.partial(propagate_kernel, transposed, sign, scal...  20.1 us
    ppermute x3, waiting for transfers between devices, passed_along(): lax.ppermute(shard, 'seg', [(i, (i + by) % count) for i in range(count)])  13.4 us
    ppermute x3, starting transfers between devices, passed_along(): lax.ppermute(shard, 'seg', [(i, (i + by) % count) for i in range(count)])  5.96 us
    ppermute x2, starting transfers between devices, exchanged(): lax.ppermute(outer(0, 0), 'pitch', [((i + 1) % ring, i) for i in range(ri...  4.49 us
    ppermute x2, waiting for transfers between devices, exchanged(): lax.ppermute(outer(rows - TILE, rows - LANES), 'pitch', [(i, (i + 1) % ri...  4.49 us
    ppermute x2, starting transfers between devices, exchanged(): lax.ppermute(outer(rows - TILE, rows - LANES), 'pitch', [(i, (i + 1) % ri...  3.26 us
    unnamed x12, local copies, waits for them, and re-layouts  2.68 us
    ppermute x2, waiting for transfers between devices, exchanged(): sides = lax.ppermute(strip, 'span', [(0, 1), (1, 0)])  2.35 us
  transfers between devices with their start and end apart: 9, of which 9 were waited for; matrix products, arithmetic and copies ran while one was open for 0% of the time, Pallas kernels for 37%

profile of v1, /device:TPU:0, one launch (start us, length us, event | category | flops | bytes accessed | tf_op | source)
XLA Modules:
  0.0 62.6 jit_solution(13669039805400478472)
XLA Ops:
  0.6 0.0 copy-start.5
  0.6 3.9 %collective-permute-start.3 = (f32[5,256,256]{2,1,0:T(8,128)}, f32[5,256,256]{2,1,0:T(8,128)S(1)}, u32[]{:S(2)}, u32[]{:S(2)}) collective-permute-start(f32[5,256,256]{2,1,0:T(8,128)} %bitcast.12), channel_id=1, source_target_pairs={{0,24},{8,0},{16,8},{24,16},{1,25},{9,1},{17,9},{25,17},{2,26},{10... | collective-permute-start | bytes 3932168 | tf_op jit(solution)/shard_map/ppermute | solution.py:225
  4.6 0.0 copy-start
  4.6 1.3 %copy-done = f32[1,5,256,256]{3,2,1,0:T(8,128)S(1)} copy-done((f32[1,5,256,256]{3,2,1,0:T(8,128)S(1)}, f32[1,5,256,256]{3,2,1,0:T(8,128)}, u32[]{:S(2)}) %copy-start) | copy-done | bytes 1310744
  5.9 0.0 copy-start.1
  5.9 0.0 copy-start.3
  5.9 0.0 copy-start.4
  5.9 0.3 shard_map.68
  6.2 0.0 collective-permute-start
  6.3 1.2 %collective-permute-done.strip = f32[24,256]{1,0:T(8,128)S(1)} collective-permute-done((f32[24,256]{1,0:T(8,128)S(1)}, f32[24,256]{1,0:T(8,128)S(1)}, u32[]{:S(2)}, u32[]{:S(2)}) %collective-permute-start) | collective-permute-done | bytes 24608 | tf_op jit(solution)/shard_map/ppermute | solution.py:192
  7.5 1.6 %collective-permute-start.1 = (f32[5,8,384]{2,1,0:T(8,128)S(1)}, f32[5,8,384]{2,1,0:T(8,128)S(1)}, u32[]{:S(2)}, u32[]{:S(2)}) collective-permute-start(f32[5,8,384]{2,1,0:T(8,128)S(1)} %select_maximum_fusion.3), channel_id=1, source_target_pairs={{0,2},{2,4},{4,6},{6,0},{1,3},{3,5},{5,7},{7,1},{8,10},{10,12},{12... | collective-permute-start | bytes 184328 | tf_op jit(solution)/shard_map/ppermute | solution.py:205
  9.1 2.2 %collective-permute-start.2 = (f32[5,8,384]{2,1,0:T(8,128)S(1)}, f32[5,8,384]{2,1,0:T(8,128)S(1)}, u32[]{:S(2)}, u32[]{:S(2)}) collective-permute-start(f32[5,8,384]{2,1,0:T(8,128)S(1)} %select_maximum_fusion.2), channel_id=1, source_target_pairs={{2,0},{4,2},{6,4},{0,6},{3,1},{5,3},{7,5},{1,7},{10,8},{12,10},{14... | collective-permute-start | bytes 184328 | tf_op jit(solution)/shard_map/ppermute | solution.py:206
  11.3 0.1 pad_add_fusion.position
  11.4 2.2 %collective-permute-done.1.upper = f32[5,8,384]{2,1,0:T(8,128)S(1)} collective-permute-done((f32[5,8,384]{2,1,0:T(8,128)S(1)}, f32[5,8,384]{2,1,0:T(8,128)S(1)}, u32[]{:S(2)}, u32[]{:S(2)}) %collective-permute-start.1) | collective-permute-done | bytes 61472 | tf_op jit(solution)/shard_map/ppermute | solution.py:205
  13.6 0.6 collective-permute-done.2.lower
  14.2 0.0 copy-done.5
  14.2 0.0 copy-done.1
  14.2 0.0 copy-done.3
  14.2 0.0 copy-done.4
  14.2 0.0 copy-start.2
  14.2 1.3 %copy-done.2 = f32[1,5,256,256]{3,2,1,0:T(8,128)S(1)} copy-done((f32[1,5,256,256]{3,2,1,0:T(8,128)S(1)}, f32[1,5,256,256]{3,2,1,0:T(8,128)}, u32[]{:S(2)}) %copy-start.2) | copy-done | bytes 1310744
  15.6 10.1 %shard_map.69 = (f32[4,256,256]{2,1,0:T(8,128)S(1)}, f32[1,256,256]{2,1,0:T(8,128)S(1)}) custom-call(s32[2]{0:T(128)S(1)} %pad_add_fusion.position, f32[5,5]{1,0:T(8,128)S(1)} %copy-done.3, f32[5,5]{1,0:T(8,128)S(1)} %copy-done.4, f32[5]{0:T(128)S(1)} %copy-done.5, f32[5,256,256]{2,1,0:T(8,128)S(1)} %bitcast.15, f32[5,256,256]{2,1,0:T(8,128)S(1)} %bitcast.17, ...), custom_call_target="tpu_custom_call" | custom-call | tf_op jit(solution)/shard_map/pallas_call | solution.py:213
  25.6 0.1 collective-permute-start.8
  25.7 2.0 %collective-permute-start.7 = (f32[1,256,256]{2,1,0:T(8,128)S(1)}, f32[1,256,256]{2,1,0:T(8,128)S(1)}, u32[]{:S(2)}, u32[]{:S(2)}) collective-permute-start(f32[1,256,256]{2,1,0:T(8,128)S(1)} %get-tuple-element.10.last), channel_id=1, source_target_pairs={{0,8},{8,16},{16,24},{24,0},{1,9},{9,17},{17,25},{25,1},{2,10},{10... | collective-permute-start | bytes 786440 | tf_op jit(solution)/shard_map/ppermute | solution.py:225
  27.6 6.4 %collective-permute-done.3.following = f32[5,256,256]{2,1,0:T(8,128)S(1)} collective-permute-done((f32[5,256,256]{2,1,0:T(8,128)}, f32[5,256,256]{2,1,0:T(8,128)S(1)}, u32[]{:S(2)}, u32[]{:S(2)}) %collective-permute-start.3) | collective-permute-done | bytes 1310752 | tf_op jit(solution)/shard_map/ppermute | solution.py:225
  34.1 1.3 %shard_map.70 = (f32[5,256,256]{2,1,0:T(8,128)}, f32[5,256,256]{2,1,0:T(8,128)S(1)}, f32[24,256]{1,0:T(8,128)S(1)}) custom-call(f32[4,256,256]{2,1,0:T(8,128)S(1)} %get-tuple-element.9.lead, f32[1,256,256]{2,1,0:T(8,128)S(1)} %get-tuple-element.10.last, f32[5,256,256]{2,1,0:T(8,128)S(1)} %collective-permute-done.3.following), custom_call_target="tpu_custom_call" | custom-call | tf_op jit(solution)/shard_map/pallas_call | solution.py:155
  35.3 0.0 collective-permute-start.4
  35.3 1.2 %collective-permute-done.4.strip = f32[24,256]{1,0:T(8,128)S(1)} collective-permute-done((f32[24,256]{1,0:T(8,128)S(1)}, f32[24,256]{1,0:T(8,128)S(1)}, u32[]{:S(2)}, u32[]{:S(2)}) %collective-permute-start.4) | collective-permute-done | bytes 24608 | tf_op jit(solution)/shard_map/ppermute | solution.py:192
  36.5 1.6 %collective-permute-start.5 = (f32[5,8,384]{2,1,0:T(8,128)S(1)}, f32[5,8,384]{2,1,0:T(8,128)S(1)}, u32[]{:S(2)}, u32[]{:S(2)}) collective-permute-start(f32[5,8,384]{2,1,0:T(8,128)S(1)} %select_maximum_fusion.1), channel_id=1, source_target_pairs={{0,2},{2,4},{4,6},{6,0},{1,3},{3,5},{5,7},{7,1},{8,10},{10,12},{12... | collective-permute-start | bytes 184328 | tf_op jit(solution)/shard_map/ppermute | solution.py:205
  38.2 2.2 %collective-permute-start.6 = (f32[5,8,384]{2,1,0:T(8,128)S(1)}, f32[5,8,384]{2,1,0:T(8,128)S(1)}, u32[]{:S(2)}, u32[]{:S(2)}) collective-permute-start(f32[5,8,384]{2,1,0:T(8,128)S(1)} %select_maximum_fusion), channel_id=1, source_target_pairs={{2,0},{4,2},{6,4},{0,6},{3,1},{5,3},{7,5},{1,7},{10,8},{12,10},{14... | collective-permute-start | bytes 184328 | tf_op jit(solution)/shard_map/ppermute | solution.py:206
  40.4 2.3 %collective-permute-done.5.upper = f32[5,8,384]{2,1,0:T(8,128)S(1)} collective-permute-done((f32[5,8,384]{2,1,0:T(8,128)S(1)}, f32[5,8,384]{2,1,0:T(8,128)S(1)}, u32[]{:S(2)}, u32[]{:S(2)}) %collective-permute-start.5) | collective-permute-done | bytes 61472 | tf_op jit(solution)/shard_map/ppermute | solution.py:205
  42.7 0.6 collective-permute-done.6.lower
  43.3 10.1 %shard_map.71 = (f32[4,256,256]{2,1,0:T(8,128)S(1)}, f32[1,256,256]{2,1,0:T(8,128)S(1)}) custom-call(s32[2]{0:T(128)S(1)} %pad_add_fusion.position, f32[5,5]{1,0:T(8,128)S(1)} %copy-done.3, f32[5,5]{1,0:T(8,128)S(1)} %copy-done.4, f32[5]{0:T(128)S(1)} %copy-done.5, f32[5,256,256]{2,1,0:T(8,128)S(1)} %get-tuple-element.12.cells, f32[5,256,256]{2,1,0:T(8,128)S(1)} %bitcast.16, ...), custom_call_target="tpu_custom_call" | custom-call | tf_op jit(solution)/shard_map/pallas_call | solution.py:213
  53.4 4.1 %collective-permute-done.8.arrived = f32[4,256,256]{2,1,0:T(8,128)S(1)} collective-permute-done((f32[4,256,256]{2,1,0:T(8,128)S(1)}, f32[4,256,256]{2,1,0:T(8,128)S(1)}, u32[]{:S(2)}, u32[]{:S(2)}) %collective-permute-start.8) | collective-permute-done | bytes 1048608 | tf_op jit(solution)/shard_map/ppermute | solution.py:225
  57.4 1.5 %shard_map.72.begun = f32[1,5,256,256]{3,2,1,0:T(8,128)} custom-call(f32[4,256,256]{2,1,0:T(8,128)S(1)} %get-tuple-element.15.adjoint, f32[4,256,256]{2,1,0:T(8,128)S(1)} %collective-permute-done.8.arrived), custom_call_target="tpu_custom_call" | custom-call | tf_op jit(solution)/shard_map/pallas_call | solution.py:169
  59.0 2.9 %collective-permute-done.7.arrived = f32[1,256,256]{2,1,0:T(8,128)S(1)} collective-permute-done((f32[1,256,256]{2,1,0:T(8,128)S(1)}, f32[1,256,256]{2,1,0:T(8,128)S(1)}, u32[]{:S(2)}, u32[]{:S(2)}) %collective-permute-start.7) | collective-permute-done | bytes 262176 | tf_op jit(solution)/shard_map/ppermute | solution.py:225
  61.9 0.7 %shard_map.73 = f32[1,5,256,256]{3,2,1,0:T(8,128)} custom-call(f32[1,256,256]{2,1,0:T(8,128)S(1)} %get-tuple-element.14.adjoint, f32[1,256,256]{2,1,0:T(8,128)S(1)} %collective-permute-done.7.arrived, f32[1,5,256,256]{3,2,1,0:T(8,128)} %shard_map.72.begun), custom_call_target="tpu_custom_call", output_to_operand_aliasing={{}: (2, {})} | custom-call | tf_op jit(solution)/shard_map/pallas_call | solution.py:177
  (8 shorter events, 0.0 us)
Async XLA Ops:
  0.6 13.6 %copy-start.5 = (f32[5]{0:T(128)S(1)}, f32[5]{0:T(128)}, u32[]{:S(2)}) copy-start(f32[5]{0:T(128)} %viscous.3) | copy-start | bytes 64
  0.6 33.4 %collective-permute-start.3 = (f32[5,256,256]{2,1,0:T(8,128)}, f32[5,256,256]{2,1,0:T(8,128)S(1)}, u32[]{:S(2)}, u32[]{:S(2)}) collective-permute-start(f32[5,256,256]{2,1,0:T(8,128)} %bitcast.12), channel_id=1, source_target_pairs={{0,24},{8,0},{16,8},{24,16},{1,25},{9,1},{17,9},{25,17},{2,26},{10... | collective-permute-start | bytes 3932168 | tf_op jit(solution)/shard_map/ppermute | solution.py:225
  4.6 1.4 %copy-start = (f32[1,5,256,256]{3,2,1,0:T(8,128)S(1)}, f32[1,5,256,256]{3,2,1,0:T(8,128)}, u32[]{:S(2)}) copy-start(f32[1,5,256,256]{3,2,1,0:T(8,128)} %param.5) | copy-start | bytes 3932164
  5.9 8.3 %copy-start.1 = (f32[1,5,256,256]{3,2,1,0:T(8,128)S(1)}, f32[1,5,256,256]{3,2,1,0:T(8,128)}, u32[]{:S(2)}) copy-start(f32[1,5,256,256]{3,2,1,0:T(8,128)} %param.5) | copy-start | bytes 3932164
  5.9 8.3 %copy-start.3 = (f32[5,5]{1,0:T(8,128)S(1)}, f32[5,5]{1,0:T(8,128)}, u32[]{:S(2)}) copy-start(f32[5,5]{1,0:T(8,128)} %mat_pitch.3) | copy-start | bytes 304
  5.9 8.3 %copy-start.4 = (f32[5,5]{1,0:T(8,128)S(1)}, f32[5,5]{1,0:T(8,128)}, u32[]{:S(2)}) copy-start(f32[5,5]{1,0:T(8,128)} %mat_span.3) | copy-start | bytes 304
  6.2 1.2 %collective-permute-start = (f32[24,256]{1,0:T(8,128)S(1)}, f32[24,256]{1,0:T(8,128)S(1)}, u32[]{:S(2)}, u32[]{:S(2)}) collective-permute-start(f32[24,256]{1,0:T(8,128)S(1)} %shard_map.68), channel_id=1, source_target_pairs={{0,1},{1,0},{2,3},{3,2},{4,5},{5,4},{6,7},{7,6},{8,9},{9,8},{10,11... | collective-permute-start | bytes 73736 | tf_op jit(solution)/shard_map/ppermute | solution.py:192
  7.5 6.2 %collective-permute-start.1 = (f32[5,8,384]{2,1,0:T(8,128)S(1)}, f32[5,8,384]{2,1,0:T(8,128)S(1)}, u32[]{:S(2)}, u32[]{:S(2)}) collective-permute-start(f32[5,8,384]{2,1,0:T(8,128)S(1)} %select_maximum_fusion.3), channel_id=1, source_target_pairs={{0,2},{2,4},{4,6},{6,0},{1,3},{3,5},{5,7},{7,1},{8,10},{10,12},{12... | collective-permute-start | bytes 184328 | tf_op jit(solution)/shard_map/ppermute | solution.py:205
  9.1 5.1 %collective-permute-start.2 = (f32[5,8,384]{2,1,0:T(8,128)S(1)}, f32[5,8,384]{2,1,0:T(8,128)S(1)}, u32[]{:S(2)}, u32[]{:S(2)}) collective-permute-start(f32[5,8,384]{2,1,0:T(8,128)S(1)} %select_maximum_fusion.2), channel_id=1, source_target_pairs={{2,0},{4,2},{6,4},{0,6},{3,1},{5,3},{7,5},{1,7},{10,8},{12,10},{14... | collective-permute-start | bytes 184328 | tf_op jit(solution)/shard_map/ppermute | solution.py:206
  14.2 1.3 %copy-start.2 = (f32[1,5,256,256]{3,2,1,0:T(8,128)S(1)}, f32[1,5,256,256]{3,2,1,0:T(8,128)}, u32[]{:S(2)}) copy-start(f32[1,5,256,256]{3,2,1,0:T(8,128)} %param.6) | copy-start | bytes 3932164
  25.6 31.8 %collective-permute-start.8 = (f32[4,256,256]{2,1,0:T(8,128)S(1)}, f32[4,256,256]{2,1,0:T(8,128)S(1)}, u32[]{:S(2)}, u32[]{:S(2)}) collective-permute-start(f32[4,256,256]{2,1,0:T(8,128)S(1)} %get-tuple-element.9.lead), channel_id=1, source_target_pairs={{0,8},{8,16},{16,24},{24,0},{1,9},{9,17},{17,25},{25,1},{2,10},{10... | collective-permute-start | bytes 3145736 | tf_op jit(solution)/shard_map/ppermute | solution.py:225
  25.7 36.2 %collective-permute-start.7 = (f32[1,256,256]{2,1,0:T(8,128)S(1)}, f32[1,256,256]{2,1,0:T(8,128)S(1)}, u32[]{:S(2)}, u32[]{:S(2)}) collective-permute-start(f32[1,256,256]{2,1,0:T(8,128)S(1)} %get-tuple-element.10.last), channel_id=1, source_target_pairs={{0,8},{8,16},{16,24},{24,0},{1,9},{9,17},{17,25},{25,1},{2,10},{10... | collective-permute-start | bytes 786440 | tf_op jit(solution)/shard_map/ppermute | solution.py:225
  35.3 1.2 %collective-permute-start.4 = (f32[24,256]{1,0:T(8,128)S(1)}, f32[24,256]{1,0:T(8,128)S(1)}, u32[]{:S(2)}, u32[]{:S(2)}) collective-permute-start(f32[24,256]{1,0:T(8,128)S(1)} %get-tuple-element.13), channel_id=1, source_target_pairs={{0,1},{1,0},{2,3},{3,2},{4,5},{5,4},{6,7},{7,6},{8,9},{9,8},{10,11... | collective-permute-start | bytes 73736 | tf_op jit(solution)/shard_map/ppermute | solution.py:192
  36.5 6.2 %collective-permute-start.5 = (f32[5,8,384]{2,1,0:T(8,128)S(1)}, f32[5,8,384]{2,1,0:T(8,128)S(1)}, u32[]{:S(2)}, u32[]{:S(2)}) collective-permute-start(f32[5,8,384]{2,1,0:T(8,128)S(1)} %select_maximum_fusion.1), channel_id=1, source_target_pairs={{0,2},{2,4},{4,6},{6,0},{1,3},{3,5},{5,7},{7,1},{8,10},{10,12},{12... | collective-permute-start | bytes 184328 | tf_op jit(solution)/shard_map/ppermute | solution.py:205
  38.2 5.1 %collective-permute-start.6 = (f32[5,8,384]{2,1,0:T(8,128)S(1)}, f32[5,8,384]{2,1,0:T(8,128)S(1)}, u32[]{:S(2)}, u32[]{:S(2)}) collective-permute-start(f32[5,8,384]{2,1,0:T(8,128)S(1)} %select_maximum_fusion), channel_id=1, source_target_pairs={{2,0},{4,2},{6,4},{0,6},{3,1},{5,3},{7,5},{1,7},{10,8},{12,10},{14... | collective-permute-start | bytes 184328 | tf_op jit(solution)/shard_map/ppermute | solution.py:206

commit v2 on v1

--- a/solution.py
+++ b/solution.py
@@ -13,6 +13,7 @@
 LANES = 128
 STRIP = 24
 MARGIN = 2 * TILE
+LAST = 32
 VMEM_LIMIT = 32 * 1024 * 1024
 
 
@@ -34,9 +35,10 @@
 
 def mismatch_kernel(lead, last, following, mismatch, again, strip):
     fields, rows, cols = mismatch.shape
-    for f in range(fields):
-        ending = lead[f] if f < lead.shape[0] else last[f - lead.shape[0]]
-        mismatch[f] = again[f] = ending - following[f]
+    begin = lead.shape[1]
+    for f in range(fields):
+        mismatch[f, :begin] = again[f, :begin] = lead[f] - following[f, :begin]
+        mismatch[f, begin:] = again[f, begin:] = last[f] - following[f, begin:]
     strip[...] = edge_strip(lambda f, at: mismatch[f, :, at : at + LANES], fields, rows, cols)
 
 
@@ -109,24 +111,27 @@
             second[f, pl.ds(pl.multiple_of(tile * TILE, TILE), TILE), cols:] = jnp.where(inside_tile, value[:, cols:], 0.0)
         return carry
 
-    lax.fori_loop(1, (MARGIN + rows) // TILE + 1, step_one, 0)
-
-    def step_two(tile, carry):
+    lax.fori_loop(1, (MARGIN + rows) // TILE + 1, step_one, 0, unroll=2)
+
+    def step_two(result, base, tile, carry):
         for f, value in enumerate(substep(second, tile, coefficients, cols)):
-            at = pl.ds(pl.multiple_of(tile * TILE - MARGIN, TILE), TILE)
-            result, place = (lead, f) if f < lead.shape[0] else (last, f - lead.shape[0])
-            result[place, at, :] = value + scale * extra[f, at, :]
+            at = pl.multiple_of(tile * TILE - MARGIN, TILE)
+            into = pl.multiple_of(at - base, TILE)
+            result[f, pl.ds(into, TILE), :] = value + scale * extra[f, pl.ds(at, TILE), :]
         return carry
 
-    lax.fori_loop(MARGIN // TILE, (MARGIN + rows) // TILE, step_two, 0)
+    begin = lead.shape[1]
+    bounds = [MARGIN // TILE, (MARGIN + begin) // TILE, (MARGIN + rows) // TILE]
+    lax.fori_loop(bounds[0], bounds[1], functools.partial(step_two, lead, 0), 0, unroll=4)
+    lax.fori_loop(bounds[1], bounds[2], functools.partial(step_two, last, begin), 0, unroll=4)
 
 
 def lead_kernel(adjoint, arrived, gradient):
     gradient[0] = adjoint[...] - arrived[...]
 
 
-def last_kernel(adjoint, arrived, begun, gradient):
-    gradient[0] = adjoint[...] - arrived[...]
+def last_kernel(adjoint, early, late, begun, gradient):
+    gradient[0] = adjoint[...] - (early[...] + late[...])
 
 
 def in_vmem(count):
@@ -162,27 +167,26 @@
 
 
 def gradient_of(adjoint, arrived):
-    count, rows, cols = adjoint[0].shape
-    rest = adjoint[1].shape[0]
-    whole = jax.ShapeDtypeStruct((1, count + rest, rows, cols), jnp.float32)
-    field = pl.BlockSpec((1, rows, cols), lambda f: (f, 0, 0))
+    fields, begin, cols = adjoint[0].shape
+    rest = adjoint[1].shape[1]
+    whole = jax.ShapeDtypeStruct((1, fields, begin + rest, cols), jnp.float32)
     begun = pl.pallas_call(
         lead_kernel,
-        grid=(count,),
+        grid=(1,),
         out_shape=whole,
-        in_specs=[field, field],
-        out_specs=pl.BlockSpec((1, 1, rows, cols), lambda f: (0, f, 0, 0)),
+        in_specs=in_vmem(2),
+        out_specs=pl.BlockSpec((1, fields, begin, cols), lambda i: (0, 0, 0, 0)),
         compiler_params=PARAMS,
     )(adjoint[0], arrived[0])
     return pl.pallas_call(
         last_kernel,
         grid=(1,),
         out_shape=whole,
-        in_specs=in_vmem(2) + [pl.BlockSpec(memory_space=pl.ANY)],
-        out_specs=pl.BlockSpec((1, rest, rows, cols), lambda f: (0, count // rest, 0, 0)),
-        input_output_aliases={2: 0},
-        compiler_params=PARAMS,
-    )(adjoint[1], arrived[1], begun)
+        in_specs=in_vmem(3) + [pl.BlockSpec(memory_space=pl.ANY)],
+        out_specs=pl.BlockSpec((1, fields, rest, cols), lambda f: (0, 0, begin // rest, 0)),
+        input_output_aliases={3: 0},
+        compiler_params=PARAMS,
+    )(adjoint[1], *arrived[1], begun)
 
 
 def exchanged(cells, strip):
@@ -212,7 +216,7 @@
     wide = pltpu.VMEM((fields, rows + 2 * MARGIN, cols + LANES), jnp.float32)
     return pl.pallas_call(
         functools.partial(propagate_kernel, transposed, sign, scale),
-        out_shape=tuple(jax.ShapeDtypeStruct((n, rows, cols), jnp.float32) for n in (fields - 1, 1)),
+        out_shape=tuple(jax.ShapeDtypeStruct((fields, n, cols), jnp.float32) for n in (rows - LAST, LAST)),
         in_specs=in_smem(4) + in_vmem(5),
         out_specs=tuple(in_vmem(2)),
         scratch_shapes=[wide, wide],
@@ -223,6 +227,18 @@
 def passed_along(shard, by):
     count = lax.axis_size("seg")
     return lax.ppermute(shard, "seg", [(i, (i + by) % count) for i in range(count)])
+
+
+def passed_in_turn(shard, after, by):
+    count, width = lax.axis_size("seg"), lax.axis_size("span")
+
+    def share(cells, parity):
+        pairs = [(i * width + k, (i + by) % count * width + k) for i in range(count) for k in range(parity, width, 2)]
+        return lax.ppermute(cells, ("seg", "span"), pairs)
+
+    early = share(shard, 0)
+    late = share(lax.optimization_barrier((shard, after))[0], 1)
+    return early, late
 
 
 def body(states, forcing, adv_pitch, adv_span, diffusion):
@@ -231,10 +247,11 @@
     following = passed_along(start, -1)
     halos = exchanged(start, edges_of(start))
     ending = propagated(position, adv_pitch, adv_span, diffusion, start, forcing[0], halos, False, -1.0, TIME_STEP)
-    arrived = [passed_along(part, 1) for part in ending]
+    arrived = [passed_along(ending[0], 1)]
     mismatch, again, strip = mismatch_of(*ending, following)
     halos = exchanged(again, strip)
     adjoint = propagated(position, adv_pitch, adv_span, diffusion, again, start, halos, True, 1.0, 1.0)
+    arrived.append(passed_in_turn(ending[1], adjoint[0], 1))
     return (mismatch[None], gradient_of(adjoint, arrived))
 
 

time: 62.8 us -> 62.2 us (level); the launches traced: 62.6 us -> 61.4 us
  Pallas kernels: 23.9 us -> 20.6 us
  starting transfers between devices: 13.8 us -> 16.5 us
    ppermute x0 -> x2, starting transfers between devices: none -> 4.9 us  [share(): return lax.ppermute(cells, ('seg', 'span'), pairs)]
    pallas_call x2, Pallas kernels: 20.1 us -> 17.2 us  [propagated(): pl.pallas_call(functools.partial(propagate_kernel, transposed, sign, scal...]
    ppermute x3 -> x2, starting transfers between devices: 5.96 us -> 4 us  [passed_along(): lax.ppermute(shard, 'seg', [(i, (i + by) % count) for i in range(count)])]
    ppermute x2, starting transfers between devices: 3.26 us -> 1.63 us  [exchanged(): lax.ppermute(outer(rows - TILE, rows - LANES), 'pitch', [(i, (i + 1) % ri...]
    ppermute x2, starting transfers between devices: 4.49 us -> 5.9 us  [exchanged(): lax.ppermute(outer(0, 0), 'pitch', [((i + 1) % ring, i) for i in range(ri...]
    ppermute x0 -> x2, waiting for transfers between devices: none -> 1.18 us  [share(): return lax.ppermute(cells, ('seg', 'span'), pairs)]
    ppermute x3 -> x2, waiting for transfers between devices: 13.4 us -> 12.7 us  [passed_along(): lax.ppermute(shard, 'seg', [(i, (i + by) % count) for i in range(count)])]
  transfers between devices with their start and end apart: 9 -> 10, of which waited for: 9 -> 8; matrix products, arithmetic and copies ran while one was open for 0% -> 0% of each run, Pallas kernels for 37% -> 32%
where the time goes in v2:
time: 62.2 us; the launch traced here: 61.4 us
  waiting for transfers between devices  20.8 us (33%)
  Pallas kernels  20.6 us (33%)
  starting transfers between devices  16.5 us (27%)
  local copies, waits for them, and re-layouts  2.7 us (4%)
  between operations  0.73 us (1%)
    pallas_call x2, Pallas kernels, propagated(): pl.pallas_call(functools.partial(propagate_kernel, transposed, sign, scal...  17.2 us
    ppermute x2, waiting for transfers between devices, passed_along(): lax.ppermute(shard, 'seg', [(i, (i + by) % count) for i in range(count)])  12.7 us
    ppermute x2, starting transfers between devices, exchanged(): lax.ppermute(outer(0, 0), 'pitch', [((i + 1) % ring, i) for i in range(ri...  5.9 us
    ppermute x2, starting transfers between devices, share(): return lax.ppermute(cells, ('seg', 'span'), pairs)  4.9 us
    ppermute x2, starting transfers between devices, passed_along(): lax.ppermute(shard, 'seg', [(i, (i + by) % count) for i in range(count)])  4 us
    ppermute x2, waiting for transfers between devices, exchanged(): lax.ppermute(outer(rows - TILE, rows - LANES), 'pitch', [(i, (i + 1) % ri...  3.97 us
    unnamed x12, local copies, waits for them, and re-layouts  2.68 us
    ppermute x2, waiting for transfers between devices, exchanged(): sides = lax.ppermute(strip, 'span', [(0, 1), (1, 0)])  2.35 us
  transfers between devices with their start and end apart: 10, of which 8 were waited for; matrix products, arithmetic and copies ran while one was open for 0% of the time, Pallas kernels for 32%

profile of v2, /device:TPU:0, one launch (start us, length us, event | category | flops | bytes accessed | tf_op | source)
XLA Modules:
  0.0 61.4 jit_solution(6358946988308822459)
XLA Ops:
  0.6 0.0 copy-start.5
  0.6 3.9 %collective-permute-start.3 = (f32[5,256,256]{2,1,0:T(8,128)}, f32[5,256,256]{2,1,0:T(8,128)S(1)}, u32[]{:S(2)}, u32[]{:S(2)}) collective-permute-start(f32[5,256,256]{2,1,0:T(8,128)} %bitcast.12), channel_id=1, source_target_pairs={{0,24},{8,0},{16,8},{24,16},{1,25},{9,1},{17,9},{25,17},{2,26},{10... | collective-permute-start | bytes 3932168 | tf_op jit(solution)/shard_map/ppermute | solution.py:229
  4.6 0.0 copy-start
  4.6 1.3 %copy-done = f32[1,5,256,256]{3,2,1,0:T(8,128)S(1)} copy-done((f32[1,5,256,256]{3,2,1,0:T(8,128)S(1)}, f32[1,5,256,256]{3,2,1,0:T(8,128)}, u32[]{:S(2)}) %copy-start) | copy-done | bytes 1310744
  5.9 0.0 copy-start.1
  5.9 0.0 copy-start.3
  5.9 0.0 copy-start.4
  5.9 0.3 shard_map.68
  6.2 0.0 collective-permute-start
  6.3 1.2 %collective-permute-done.strip = f32[24,256]{1,0:T(8,128)S(1)} collective-permute-done((f32[24,256]{1,0:T(8,128)S(1)}, f32[24,256]{1,0:T(8,128)S(1)}, u32[]{:S(2)}, u32[]{:S(2)}) %collective-permute-start) | collective-permute-done | bytes 24608 | tf_op jit(solution)/shard_map/ppermute | solution.py:196
  7.5 1.6 %collective-permute-start.1 = (f32[5,8,384]{2,1,0:T(8,128)S(1)}, f32[5,8,384]{2,1,0:T(8,128)S(1)}, u32[]{:S(2)}, u32[]{:S(2)}) collective-permute-start(f32[5,8,384]{2,1,0:T(8,128)S(1)} %select_maximum_fusion.3), channel_id=1, source_target_pairs={{0,2},{2,4},{4,6},{6,0},{1,3},{3,5},{5,7},{7,1},{8,10},{10,12},{12... | collective-permute-start | bytes 184328 | tf_op jit(solution)/shard_map/ppermute | solution.py:209
  9.1 2.2 %collective-permute-start.2 = (f32[5,8,384]{2,1,0:T(8,128)S(1)}, f32[5,8,384]{2,1,0:T(8,128)S(1)}, u32[]{:S(2)}, u32[]{:S(2)}) collective-permute-start(f32[5,8,384]{2,1,0:T(8,128)S(1)} %select_maximum_fusion.2), channel_id=1, source_target_pairs={{2,0},{4,2},{6,4},{0,6},{3,1},{5,3},{7,5},{1,7},{10,8},{12,10},{14... | collective-permute-start | bytes 184328 | tf_op jit(solution)/shard_map/ppermute | solution.py:210
  11.3 0.1 pad_add_fusion.position
  11.4 2.2 %collective-permute-done.1.upper = f32[5,8,384]{2,1,0:T(8,128)S(1)} collective-permute-done((f32[5,8,384]{2,1,0:T(8,128)S(1)}, f32[5,8,384]{2,1,0:T(8,128)S(1)}, u32[]{:S(2)}, u32[]{:S(2)}) %collective-permute-start.1) | collective-permute-done | bytes 61472 | tf_op jit(solution)/shard_map/ppermute | solution.py:209
  13.6 0.6 collective-permute-done.2.lower
  14.2 0.0 copy-done.5
  14.2 0.0 copy-done.1
  14.2 0.0 copy-done.3
  14.2 0.0 copy-done.4
  14.2 0.0 copy-start.2
  14.2 1.3 %copy-done.2 = f32[1,5,256,256]{3,2,1,0:T(8,128)S(1)} copy-done((f32[1,5,256,256]{3,2,1,0:T(8,128)S(1)}, f32[1,5,256,256]{3,2,1,0:T(8,128)}, u32[]{:S(2)}) %copy-start.2) | copy-done | bytes 1310744
  15.6 8.7 %shard_map.69 = (f32[5,224,256]{2,1,0:T(8,128)S(1)}, f32[5,32,256]{2,1,0:T(8,128)S(1)}) custom-call(s32[2]{0:T(128)S(1)} %pad_add_fusion.position, f32[5,5]{1,0:T(8,128)S(1)} %copy-done.3, f32[5,5]{1,0:T(8,128)S(1)} %copy-done.4, f32[5]{0:T(128)S(1)} %copy-done.5, f32[5,256,256]{2,1,0:T(8,128)S(1)} %bitcast.15, f32[5,256,256]{2,1,0:T(8,128)S(1)} %bitcast.17, ...), custom_call_target="tpu_custom_call" | custom-call | tf_op jit(solution)/shard_map/pallas_call | solution.py:217
  24.2 0.1 collective-permute-start.9
  24.3 9.8 %collective-permute-done.3.following = f32[5,256,256]{2,1,0:T(8,128)S(1)} collective-permute-done((f32[5,256,256]{2,1,0:T(8,128)}, f32[5,256,256]{2,1,0:T(8,128)S(1)}, u32[]{:S(2)}, u32[]{:S(2)}) %collective-permute-start.3) | collective-permute-done | bytes 1310752 | tf_op jit(solution)/shard_map/ppermute | solution.py:229
  34.1 1.3 %shard_map.70 = (f32[5,256,256]{2,1,0:T(8,128)}, f32[5,256,256]{2,1,0:T(8,128)S(1)}, f32[24,256]{1,0:T(8,128)S(1)}) custom-call(f32[5,224,256]{2,1,0:T(8,128)S(1)} %get-tuple-element.10.lead, f32[5,32,256]{2,1,0:T(8,128)S(1)} %get-tuple-element.17.last, f32[5,256,256]{2,1,0:T(8,128)S(1)} %collective-permute-done.3.following), custom_call_target="tpu_custom_call" | custom-call | tf_op jit(solution)/shard_map/pallas_call | solution.py:160
  35.3 0.0 collective-permute-start.4
  35.3 1.2 %collective-permute-done.4.strip = f32[24,256]{1,0:T(8,128)S(1)} collective-permute-done((f32[24,256]{1,0:T(8,128)S(1)}, f32[24,256]{1,0:T(8,128)S(1)}, u32[]{:S(2)}, u32[]{:S(2)}) %collective-permute-start.4) | collective-permute-done | bytes 24608 | tf_op jit(solution)/shard_map/ppermute | solution.py:196
  36.5 3.7 %collective-permute-start.6 = (f32[5,8,384]{2,1,0:T(8,128)S(1)}, f32[5,8,384]{2,1,0:T(8,128)S(1)}, u32[]{:S(2)}, u32[]{:S(2)}) collective-permute-start(f32[5,8,384]{2,1,0:T(8,128)S(1)} %select_maximum_fusion), channel_id=1, source_target_pairs={{2,0},{4,2},{6,4},{0,6},{3,1},{5,3},{7,5},{1,7},{10,8},{12,10},{14... | collective-permute-start | bytes 184328 | tf_op jit(solution)/shard_map/ppermute | solution.py:210
  40.2 0.0 collective-permute-start.5
  40.2 4.2 %collective-permute-start.7 = (f32[5,32,256]{2,1,0:T(8,128)S(1)}, f32[5,32,256]{2,1,0:T(8,128)S(1)}, u32[]{:S(2)}, u32[]{:S(2)}) collective-permute-start(f32[5,32,256]{2,1,0:T(8,128)S(1)} %get-tuple-element.17.last), channel_id=1, source_target_pairs={{0,8},{8,16},{16,24},{24,0},{2,10},{10,18},{18,26},{26,2},{4,12},{... | collective-permute-start | bytes 491528 | tf_op jit(solution)/shard_map/ppermute | solution.py:237
  44.4 0.0 collective-permute-done.6.lower
  44.5 1.8 %collective-permute-done.5.upper = f32[5,8,384]{2,1,0:T(8,128)S(1)} collective-permute-done((f32[5,8,384]{2,1,0:T(8,128)S(1)}, f32[5,8,384]{2,1,0:T(8,128)S(1)}, u32[]{:S(2)}, u32[]{:S(2)}) %collective-permute-start.5) | collective-permute-done | bytes 61472 | tf_op jit(solution)/shard_map/ppermute | solution.py:209
  46.2 8.6 %shard_map.71 = (f32[5,224,256]{2,1,0:T(8,128)S(1)}, f32[5,32,256]{2,1,0:T(8,128)S(1)}) custom-call(s32[2]{0:T(128)S(1)} %pad_add_fusion.position, f32[5,5]{1,0:T(8,128)S(1)} %copy-done.3, f32[5,5]{1,0:T(8,128)S(1)} %copy-done.4, f32[5]{0:T(128)S(1)} %copy-done.5, f32[5,256,256]{2,1,0:T(8,128)S(1)} %get-tuple-element.13.cells, f32[5,256,256]{2,1,0:T(8,128)S(1)} %bitcast.16, ...), custom_call_target="tpu_custom_call" | custom-call | tf_op jit(solution)/shard_map/pallas_call | solution.py:217
  54.8 0.7 %collective-permute-start.8 = (f32[5,32,256]{2,1,0:T(8,128)S(1)}, f32[5,32,256]{2,1,0:T(8,128)S(1)}, u32[]{:S(2)}, u32[]{:S(2)}) collective-permute-start(f32[5,32,256]{2,1,0:T(8,128)S(1)} %get-tuple-element.17.last), channel_id=1, source_target_pairs={{1,9},{9,17},{17,25},{25,1},{3,11},{11,19},{19,27},{27,3},{5,13},{... | collective-permute-start | bytes 491528 | tf_op jit(solution)/shard_map/ppermute | solution.py:237
  55.5 2.9 %collective-permute-done.9.arrived = f32[5,224,256]{2,1,0:T(8,128)S(1)} collective-permute-done((f32[5,224,256]{2,1,0:T(8,128)S(1)}, f32[5,224,256]{2,1,0:T(8,128)S(1)}, u32[]{:S(2)}, u32[]{:S(2)}) %collective-permute-start.9) | collective-permute-done | bytes 1146912 | tf_op jit(solution)/shard_map/ppermute | solution.py:229
  58.4 1.1 %shard_map.72.begun = f32[1,5,256,256]{3,2,1,0:T(8,128)} custom-call(f32[5,224,256]{2,1,0:T(8,128)S(1)} %get-tuple-element.16.adjoint, f32[5,224,256]{2,1,0:T(8,128)S(1)} %collective-permute-done.9.arrived), custom_call_target="tpu_custom_call" | custom-call | tf_op jit(solution)/shard_map/pallas_call | solution.py:173
  59.5 1.2 %collective-permute-done.7.early = f32[5,32,256]{2,1,0:T(8,128)S(1)} collective-permute-done((f32[5,32,256]{2,1,0:T(8,128)S(1)}, f32[5,32,256]{2,1,0:T(8,128)S(1)}, u32[]{:S(2)}, u32[]{:S(2)}) %collective-permute-start.7) | collective-permute-done | bytes 163872 | tf_op jit(solution)/shard_map/ppermute | solution.py:237
  60.7 0.0 collective-permute-done.8.late
  60.7 0.7 %shard_map.73 = f32[1,5,256,256]{3,2,1,0:T(8,128)} custom-call(f32[5,32,256]{2,1,0:T(8,128)S(1)} %get-tuple-element.15.adjoint, f32[5,32,256]{2,1,0:T(8,128)S(1)} %collective-permute-done.7.early, f32[5,32,256]{2,1,0:T(8,128)S(1)} %collective-permute-done.8.late, f32[1,5,256,256]{3,2,1,0:T(8,128)} %shard_map.72.begun), custom_call_target="tpu_custom_call", output_to_operand_aliasing={{}: (3, {})} | custom-call | tf_op jit(solution)/shard_map/pallas_call | solution.py:181
  (8 shorter events, 0.0 us)
Async XLA Ops:
  0.6 13.6 %copy-start.5 = (f32[5]{0:T(128)S(1)}, f32[5]{0:T(128)}, u32[]{:S(2)}) copy-start(f32[5]{0:T(128)} %viscous.3) | copy-start | bytes 64
  0.6 33.4 %collective-permute-start.3 = (f32[5,256,256]{2,1,0:T(8,128)}, f32[5,256,256]{2,1,0:T(8,128)S(1)}, u32[]{:S(2)}, u32[]{:S(2)}) collective-permute-start(f32[5,256,256]{2,1,0:T(8,128)} %bitcast.12), channel_id=1, source_target_pairs={{0,24},{8,0},{16,8},{24,16},{1,25},{9,1},{17,9},{25,17},{2,26},{10... | collective-permute-start | bytes 3932168 | tf_op jit(solution)/shard_map/ppermute | solution.py:229
  4.6 1.4 %copy-start = (f32[1,5,256,256]{3,2,1,0:T(8,128)S(1)}, f32[1,5,256,256]{3,2,1,0:T(8,128)}, u32[]{:S(2)}) copy-start(f32[1,5,256,256]{3,2,1,0:T(8,128)} %param.5) | copy-start | bytes 3932164
  5.9 8.3 %copy-start.1 = (f32[1,5,256,256]{3,2,1,0:T(8,128)S(1)}, f32[1,5,256,256]{3,2,1,0:T(8,128)}, u32[]{:S(2)}) copy-start(f32[1,5,256,256]{3,2,1,0:T(8,128)} %param.5) | copy-start | bytes 3932164
  5.9 8.3 %copy-start.3 = (f32[5,5]{1,0:T(8,128)S(1)}, f32[5,5]{1,0:T(8,128)}, u32[]{:S(2)}) copy-start(f32[5,5]{1,0:T(8,128)} %mat_pitch.3) | copy-start | bytes 304
  5.9 8.3 %copy-start.4 = (f32[5,5]{1,0:T(8,128)S(1)}, f32[5,5]{1,0:T(8,128)}, u32[]{:S(2)}) copy-start(f32[5,5]{1,0:T(8,128)} %mat_span.3) | copy-start | bytes 304
  6.2 1.2 %collective-permute-start = (f32[24,256]{1,0:T(8,128)S(1)}, f32[24,256]{1,0:T(8,128)S(1)}, u32[]{:S(2)}, u32[]{:S(2)}) collective-permute-start(f32[24,256]{1,0:T(8,128)S(1)} %shard_map.68), channel_id=1, source_target_pairs={{0,1},{1,0},{2,3},{3,2},{4,5},{5,4},{6,7},{7,6},{8,9},{9,8},{10,11... | collective-permute-start | bytes 73736 | tf_op jit(solution)/shard_map/ppermute | solution.py:196
  7.5 6.2 %collective-permute-start.1 = (f32[5,8,384]{2,1,0:T(8,128)S(1)}, f32[5,8,384]{2,1,0:T(8,128)S(1)}, u32[]{:S(2)}, u32[]{:S(2)}) collective-permute-start(f32[5,8,384]{2,1,0:T(8,128)S(1)} %select_maximum_fusion.3), channel_id=1, source_target_pairs={{0,2},{2,4},{4,6},{6,0},{1,3},{3,5},{5,7},{7,1},{8,10},{10,12},{12... | collective-permute-start | bytes 184328 | tf_op jit(solution)/shard_map/ppermute | solution.py:209
  9.1 5.1 %collective-permute-start.2 = (f32[5,8,384]{2,1,0:T(8,128)S(1)}, f32[5,8,384]{2,1,0:T(8,128)S(1)}, u32[]{:S(2)}, u32[]{:S(2)}) collective-permute-start(f32[5,8,384]{2,1,0:T(8,128)S(1)} %select_maximum_fusion.2), channel_id=1, source_target_pairs={{2,0},{4,2},{6,4},{0,6},{3,1},{5,3},{7,5},{1,7},{10,8},{12,10},{14... | collective-permute-start | bytes 184328 | tf_op jit(solution)/shard_map/ppermute | solution.py:210
  14.2 1.3 %copy-start.2 = (f32[1,5,256,256]{3,2,1,0:T(8,128)S(1)}, f32[1,5,256,256]{3,2,1,0:T(8,128)}, u32[]{:S(2)}) copy-start(f32[1,5,256,256]{3,2,1,0:T(8,128)} %param.6) | copy-start | bytes 3932164
  24.2 34.2 %collective-permute-start.9 = (f32[5,224,256]{2,1,0:T(8,128)S(1)}, f32[5,224,256]{2,1,0:T(8,128)S(1)}, u32[]{:S(2)}, u32[]{:S(2)}) collective-permute-start(f32[5,224,256]{2,1,0:T(8,128)S(1)} %get-tuple-element.10.lead), channel_id=1, source_target_pairs={{0,8},{8,16},{16,24},{24,0},{1,9},{9,17},{17,25},{25,1},{2,10},{10... | collective-permute-start | bytes 3440648 | tf_op jit(solution)/shard_map/ppermute | solution.py:229
  35.3 1.2 %collective-permute-start.4 = (f32[24,256]{1,0:T(8,128)S(1)}, f32[24,256]{1,0:T(8,128)S(1)}, u32[]{:S(2)}, u32[]{:S(2)}) collective-permute-start(f32[24,256]{1,0:T(8,128)S(1)} %get-tuple-element.14), channel_id=1, source_target_pairs={{0,1},{1,0},{2,3},{3,2},{4,5},{5,4},{6,7},{7,6},{8,9},{9,8},{10,11... | collective-permute-start | bytes 73736 | tf_op jit(solution)/shard_map/ppermute | solution.py:196
  36.5 7.9 %collective-permute-start.6 = (f32[5,8,384]{2,1,0:T(8,128)S(1)}, f32[5,8,384]{2,1,0:T(8,128)S(1)}, u32[]{:S(2)}, u32[]{:S(2)}) collective-permute-start(f32[5,8,384]{2,1,0:T(8,128)S(1)} %select_maximum_fusion), channel_id=1, source_target_pairs={{2,0},{4,2},{6,4},{0,6},{3,1},{5,3},{7,5},{1,7},{10,8},{12,10},{14... | collective-permute-start | bytes 184328 | tf_op jit(solution)/shard_map/ppermute | solution.py:210
  40.2 6.0 %collective-permute-start.5 = (f32[5,8,384]{2,1,0:T(8,128)S(1)}, f32[5,8,384]{2,1,0:T(8,128)S(1)}, u32[]{:S(2)}, u32[]{:S(2)}) collective-permute-start(f32[5,8,384]{2,1,0:T(8,128)S(1)} %select_maximum_fusion.1), channel_id=1, source_target_pairs={{0,2},{2,4},{4,6},{6,0},{1,3},{3,5},{5,7},{7,1},{8,10},{10,12},{12... | collective-permute-start | bytes 184328 | tf_op jit(solution)/shard_map/ppermute | solution.py:209
  40.2 20.5 %collective-permute-start.7 = (f32[5,32,256]{2,1,0:T(8,128)S(1)}, f32[5,32,256]{2,1,0:T(8,128)S(1)}, u32[]{:S(2)}, u32[]{:S(2)}) collective-permute-start(f32[5,32,256]{2,1,0:T(8,128)S(1)} %get-tuple-element.17.last), channel_id=1, source_target_pairs={{0,8},{8,16},{16,24},{24,0},{2,10},{10,18},{18,26},{26,2},{4,12},{... | collective-permute-start | bytes 491528 | tf_op jit(solution)/shard_map/ppermute | solution.py:237
  54.8 5.9 %collective-permute-start.8 = (f32[5,32,256]{2,1,0:T(8,128)S(1)}, f32[5,32,256]{2,1,0:T(8,128)S(1)}, u32[]{:S(2)}, u32[]{:S(2)}) collective-permute-start(f32[5,32,256]{2,1,0:T(8,128)S(1)} %get-tuple-element.17.last), channel_id=1, source_target_pairs={{1,9},{9,17},{17,25},{25,1},{3,11},{11,19},{19,27},{27,3},{5,13},{... | collective-permute-start | bytes 491528 | tf_op jit(solution)/shard_map/ppermute | solution.py:237

commit v3 on v2

--- a/solution.py
+++ b/solution.py
@@ -130,8 +130,8 @@
     gradient[0] = adjoint[...] - arrived[...]
 
 
-def last_kernel(adjoint, early, late, begun, gradient):
-    gradient[0] = adjoint[...] - (early[...] + late[...])
+def last_kernel(adjoint, arrived, begun, gradient):
+    gradient[0] = adjoint[...] - arrived[...]
 
 
 def in_vmem(count):
@@ -182,11 +182,11 @@
         last_kernel,
         grid=(1,),
         out_shape=whole,
-        in_specs=in_vmem(3) + [pl.BlockSpec(memory_space=pl.ANY)],
+        in_specs=in_vmem(2) + [pl.BlockSpec(memory_space=pl.ANY)],
         out_specs=pl.BlockSpec((1, fields, rest, cols), lambda f: (0, 0, begin // rest, 0)),
-        input_output_aliases={3: 0},
-        compiler_params=PARAMS,
-    )(adjoint[1], *arrived[1], begun)
+        input_output_aliases={2: 0},
+        compiler_params=PARAMS,
+    )(adjoint[1], arrived[1], begun)
 
 
 def exchanged(cells, strip):
@@ -229,16 +229,12 @@
     return lax.ppermute(shard, "seg", [(i, (i + by) % count) for i in range(count)])
 
 
-def passed_in_turn(shard, after, by):
-    count, width = lax.axis_size("seg"), lax.axis_size("span")
-
-    def share(cells, parity):
-        pairs = [(i * width + k, (i + by) % count * width + k) for i in range(count) for k in range(parity, width, 2)]
-        return lax.ppermute(cells, ("seg", "span"), pairs)
-
-    early = share(shard, 0)
-    late = share(lax.optimization_barrier((shard, after))[0], 1)
-    return early, late
+def passed_by_swap(shard):
+    count = lax.axis_size("seg")
+    if count % 2:
+        return passed_along(shard, 1)
+    held = lax.ppermute(shard, "seg", [(i, (i + 2) % count if i % 2 else i) for i in range(count)])
+    return lax.ppermute(held, "seg", [(i, i ^ 1) for i in range(count)])
 
 
 def body(states, forcing, adv_pitch, adv_span, diffusion):
@@ -247,11 +243,10 @@
     following = passed_along(start, -1)
     halos = exchanged(start, edges_of(start))
     ending = propagated(position, adv_pitch, adv_span, diffusion, start, forcing[0], halos, False, -1.0, TIME_STEP)
-    arrived = [passed_along(ending[0], 1)]
+    arrived = [passed_along(ending[0], 1), passed_by_swap(ending[1])]
     mismatch, again, strip = mismatch_of(*ending, following)
     halos = exchanged(again, strip)
     adjoint = propagated(position, adv_pitch, adv_span, diffusion, again, start, halos, True, 1.0, 1.0)
-    arrived.append(passed_in_turn(ending[1], adjoint[0], 1))
     return (mismatch[None], gradient_of(adjoint, arrived))
 
 

time: 62.2 us -> 61.8 us (level); the launches traced: 61.4 us -> 61.6 us
  starting transfers between devices: 16.5 us -> 26.3 us
  waiting for transfers between devices: 20.8 us -> 11.3 us
    ppermute x2, waiting for transfers between devices: 12.7 us -> 3.01 us  [passed_along(): lax.ppermute(shard, 'seg', [(i, (i + by) % count) for i in range(count)])]
    ppermute x2, starting transfers between devices: 4.9 us -> 14.5 us  [the longest x1 13.8 us: passed_by_swap(): return lax.ppermute(held, 'seg', [(i, i ^ 1) for i in range(count)])]
    ppermute x2, starting transfers between devices: 1.63 us -> 3.26 us  [exchanged(): lax.ppermute(outer(rows - TILE, rows - LANES), 'pitch', [(i, (i + 1) % ri...]
    ppermute x2, starting transfers between devices: 5.9 us -> 4.49 us  [exchanged(): lax.ppermute(outer(0, 0), 'pitch', [((i + 1) % ring, i) for i in range(ri...]
    ppermute x2, waiting for transfers between devices: 1.18 us -> 0.3 us  [the longest x1 0.3 us: passed_by_swap(): return lax.ppermute(held, 'seg', [(i, i ^ 1) for i in range(count)])]
where the time goes in v3:
time: 61.8 us; the launch traced here: 61.6 us
  starting transfers between devices  26.3 us (43%)
  Pallas kernels  20.5 us (33%)
  waiting for transfers between devices  11.3 us (18%)
  local copies, waits for them, and re-layouts  2.7 us (4%)
  between operations  0.72 us (1%)
    pallas_call x2, Pallas kernels, propagated(): pl.pallas_call(functools.partial(propagate_kernel, transposed, sign, scal...  17.2 us
    ppermute x1, starting transfers between devices, passed_by_swap(): return lax.ppermute(held, 'seg', [(i, i ^ 1) for i in range(count)])  13.8 us
    ppermute x2, starting transfers between devices, exchanged(): lax.ppermute(outer(0, 0), 'pitch', [((i + 1) % ring, i) for i in range(ri...  4.49 us
    ppermute x2, waiting for transfers between devices, exchanged(): lax.ppermute(outer(rows - TILE, rows - LANES), 'pitch', [(i, (i + 1) % ri...  4.49 us
    ppermute x2, starting transfers between devices, passed_along(): lax.ppermute(shard, 'seg', [(i, (i + by) % count) for i in range(count)])  4 us
    ppermute x2, starting transfers between devices, exchanged(): lax.ppermute(outer(rows - TILE, rows - LANES), 'pitch', [(i, (i + 1) % ri...  3.26 us
    ppermute x2, waiting for transfers between devices, passed_along(): lax.ppermute(shard, 'seg', [(i, (i + by) % count) for i in range(count)])  3.01 us
    unnamed x12, local copies, waits for them, and re-layouts  2.68 us
  transfers between devices with their start and end apart: 10, of which 8 were waited for; matrix products, arithmetic and copies ran while one was open for 0% of the time, Pallas kernels for 32%

profile of v3, /device:TPU:0, one launch (start us, length us, event | category | flops | bytes accessed | tf_op | source)
XLA Modules:
  0.0 61.6 jit_solution(6491472393547847776)
XLA Ops:
  0.6 0.0 copy-start.5
  0.6 3.9 %collective-permute-start.3 = (f32[5,256,256]{2,1,0:T(8,128)}, f32[5,256,256]{2,1,0:T(8,128)S(1)}, u32[]{:S(2)}, u32[]{:S(2)}) collective-permute-start(f32[5,256,256]{2,1,0:T(8,128)} %bitcast.12), channel_id=1, source_target_pairs={{0,24},{8,0},{16,8},{24,16},{1,25},{9,1},{17,9},{25,17},{2,26},{10... | collective-permute-start | bytes 3932168 | tf_op jit(solution)/shard_map/ppermute | solution.py:229
  4.6 0.0 copy-start
  4.6 1.3 %copy-done = f32[1,5,256,256]{3,2,1,0:T(8,128)S(1)} copy-done((f32[1,5,256,256]{3,2,1,0:T(8,128)S(1)}, f32[1,5,256,256]{3,2,1,0:T(8,128)}, u32[]{:S(2)}) %copy-start) | copy-done | bytes 1310744
  5.9 0.0 copy-start.1
  5.9 0.0 copy-start.3
  5.9 0.0 copy-start.4
  5.9 0.3 shard_map.68
  6.2 0.0 collective-permute-start
  6.3 1.2 %collective-permute-done.strip = f32[24,256]{1,0:T(8,128)S(1)} collective-permute-done((f32[24,256]{1,0:T(8,128)S(1)}, f32[24,256]{1,0:T(8,128)S(1)}, u32[]{:S(2)}, u32[]{:S(2)}) %collective-permute-start) | collective-permute-done | bytes 24608 | tf_op jit(solution)/shard_map/ppermute | solution.py:196
  7.5 1.6 %collective-permute-start.1 = (f32[5,8,384]{2,1,0:T(8,128)S(1)}, f32[5,8,384]{2,1,0:T(8,128)S(1)}, u32[]{:S(2)}, u32[]{:S(2)}) collective-permute-start(f32[5,8,384]{2,1,0:T(8,128)S(1)} %select_maximum_fusion.3), channel_id=1, source_target_pairs={{0,2},{2,4},{4,6},{6,0},{1,3},{3,5},{5,7},{7,1},{8,10},{10,12},{12... | collective-permute-start | bytes 184328 | tf_op jit(solution)/shard_map/ppermute | solution.py:209
  9.1 2.2 %collective-permute-start.2 = (f32[5,8,384]{2,1,0:T(8,128)S(1)}, f32[5,8,384]{2,1,0:T(8,128)S(1)}, u32[]{:S(2)}, u32[]{:S(2)}) collective-permute-start(f32[5,8,384]{2,1,0:T(8,128)S(1)} %select_maximum_fusion.2), channel_id=1, source_target_pairs={{2,0},{4,2},{6,4},{0,6},{3,1},{5,3},{7,5},{1,7},{10,8},{12,10},{14... | collective-permute-start | bytes 184328 | tf_op jit(solution)/shard_map/ppermute | solution.py:210
  11.3 0.1 pad_add_fusion.position
  11.4 2.2 %collective-permute-done.1.upper = f32[5,8,384]{2,1,0:T(8,128)S(1)} collective-permute-done((f32[5,8,384]{2,1,0:T(8,128)S(1)}, f32[5,8,384]{2,1,0:T(8,128)S(1)}, u32[]{:S(2)}, u32[]{:S(2)}) %collective-permute-start.1) | collective-permute-done | bytes 61472 | tf_op jit(solution)/shard_map/ppermute | solution.py:209
  13.6 0.6 collective-permute-done.2.lower
  14.2 0.0 copy-done.5
  14.2 0.0 copy-done.1
  14.2 0.0 copy-done.3
  14.2 0.0 copy-done.4
  14.2 0.0 copy-start.2
  14.2 1.3 %copy-done.2 = f32[1,5,256,256]{3,2,1,0:T(8,128)S(1)} copy-done((f32[1,5,256,256]{3,2,1,0:T(8,128)S(1)}, f32[1,5,256,256]{3,2,1,0:T(8,128)}, u32[]{:S(2)}) %copy-start.2) | copy-done | bytes 1310744
  15.6 8.7 %shard_map.69 = (f32[5,224,256]{2,1,0:T(8,128)S(1)}, f32[5,32,256]{2,1,0:T(8,128)S(1)}) custom-call(s32[2]{0:T(128)S(1)} %pad_add_fusion.position, f32[5,5]{1,0:T(8,128)S(1)} %copy-done.3, f32[5,5]{1,0:T(8,128)S(1)} %copy-done.4, f32[5]{0:T(128)S(1)} %copy-done.5, f32[5,256,256]{2,1,0:T(8,128)S(1)} %bitcast.15, f32[5,256,256]{2,1,0:T(8,128)S(1)} %bitcast.17, ...), custom_call_target="tpu_custom_call" | custom-call | tf_op jit(solution)/shard_map/pallas_call | solution.py:217
  24.2 0.1 collective-permute-start.9
  24.3 0.7 %collective-permute-start.7 = (f32[5,32,256]{2,1,0:T(8,128)S(1)}, f32[5,32,256]{2,1,0:T(8,128)S(1)}, u32[]{:S(2)}, u32[]{:S(2)}) collective-permute-start(f32[5,32,256]{2,1,0:T(8,128)S(1)} %get-tuple-element.10.last), channel_id=1, source_target_pairs={{0,0},{8,24},{16,16},{24,8},{1,1},{9,25},{17,17},{25,9},{2,2},{10,... | collective-permute-start | bytes 491528 | tf_op jit(solution)/shard_map/ppermute | solution.py:236
  24.9 0.0 collective-permute-done.7
  25.0 13.8 %collective-permute-start.8 = (f32[5,32,256]{2,1,0:T(8,128)S(1)}, f32[5,32,256]{2,1,0:T(8,128)S(1)}, u32[]{:S(2)}, u32[]{:S(2)}) collective-permute-start(f32[5,32,256]{2,1,0:T(8,128)S(1)} %collective-permute-done.7), channel_id=1, source_target_pairs={{0,8},{8,0},{16,24},{24,16},{1,9},{9,1},{17,25},{25,17},{2,10},{10... | collective-permute-start | bytes 491528 | tf_op jit(solution)/shard_map/ppermute | solution.py:237
  38.8 0.0 collective-permute-done.3.following
  38.8 1.3 %shard_map.70 = (f32[5,256,256]{2,1,0:T(8,128)}, f32[5,256,256]{2,1,0:T(8,128)S(1)}, f32[24,256]{1,0:T(8,128)S(1)}) custom-call(f32[5,224,256]{2,1,0:T(8,128)S(1)} %get-tuple-element.9.lead, f32[5,32,256]{2,1,0:T(8,128)S(1)} %get-tuple-element.10.last, f32[5,256,256]{2,1,0:T(8,128)S(1)} %collective-permute-done.3.following), custom_call_target="tpu_custom_call" | custom-call | tf_op jit(solution)/shard_map/pallas_call | solution.py:160
  40.0 0.0 collective-permute-start.4
  40.0 1.2 %collective-permute-done.4.strip = f32[24,256]{1,0:T(8,128)S(1)} collective-permute-done((f32[24,256]{1,0:T(8,128)S(1)}, f32[24,256]{1,0:T(8,128)S(1)}, u32[]{:S(2)}, u32[]{:S(2)}) %collective-permute-start.4) | collective-permute-done | bytes 24608 | tf_op jit(solution)/shard_map/ppermute | solution.py:196
  41.2 1.6 %collective-permute-start.5 = (f32[5,8,384]{2,1,0:T(8,128)S(1)}, f32[5,8,384]{2,1,0:T(8,128)S(1)}, u32[]{:S(2)}, u32[]{:S(2)}) collective-permute-start(f32[5,8,384]{2,1,0:T(8,128)S(1)} %select_maximum_fusion.1), channel_id=1, source_target_pairs={{0,2},{2,4},{4,6},{6,0},{1,3},{3,5},{5,7},{7,1},{8,10},{10,12},{12... | collective-permute-start | bytes 184328 | tf_op jit(solution)/shard_map/ppermute | solution.py:209
  42.9 2.2 %collective-permute-start.6 = (f32[5,8,384]{2,1,0:T(8,128)S(1)}, f32[5,8,384]{2,1,0:T(8,128)S(1)}, u32[]{:S(2)}, u32[]{:S(2)}) collective-permute-start(f32[5,8,384]{2,1,0:T(8,128)S(1)} %select_maximum_fusion), channel_id=1, source_target_pairs={{2,0},{4,2},{6,4},{0,6},{3,1},{5,3},{7,5},{1,7},{10,8},{12,10},{14... | collective-permute-start | bytes 184328 | tf_op jit(solution)/shard_map/ppermute | solution.py:210
  45.1 2.3 %collective-permute-done.5.upper = f32[5,8,384]{2,1,0:T(8,128)S(1)} collective-permute-done((f32[5,8,384]{2,1,0:T(8,128)S(1)}, f32[5,8,384]{2,1,0:T(8,128)S(1)}, u32[]{:S(2)}, u32[]{:S(2)}) %collective-permute-start.5) | collective-permute-done | bytes 61472 | tf_op jit(solution)/shard_map/ppermute | solution.py:209
  47.4 0.6 collective-permute-done.6.lower
  48.0 8.6 %shard_map.71 = (f32[5,224,256]{2,1,0:T(8,128)S(1)}, f32[5,32,256]{2,1,0:T(8,128)S(1)}) custom-call(s32[2]{0:T(128)S(1)} %pad_add_fusion.position, f32[5,5]{1,0:T(8,128)S(1)} %copy-done.3, f32[5,5]{1,0:T(8,128)S(1)} %copy-done.4, f32[5]{0:T(128)S(1)} %copy-done.5, f32[5,256,256]{2,1,0:T(8,128)S(1)} %get-tuple-element.12.cells, f32[5,256,256]{2,1,0:T(8,128)S(1)} %bitcast.16, ...), custom_call_target="tpu_custom_call" | custom-call | tf_op jit(solution)/shard_map/pallas_call | solution.py:217
  56.5 3.0 %collective-permute-done.9.arrived = f32[5,224,256]{2,1,0:T(8,128)S(1)} collective-permute-done((f32[5,224,256]{2,1,0:T(8,128)S(1)}, f32[5,224,256]{2,1,0:T(8,128)S(1)}, u32[]{:S(2)}, u32[]{:S(2)}) %collective-permute-start.9) | collective-permute-done | bytes 1146912 | tf_op jit(solution)/shard_map/ppermute | solution.py:229
  59.5 1.1 %shard_map.72.begun = f32[1,5,256,256]{3,2,1,0:T(8,128)} custom-call(f32[5,224,256]{2,1,0:T(8,128)S(1)} %get-tuple-element.15.adjoint, f32[5,224,256]{2,1,0:T(8,128)S(1)} %collective-permute-done.9.arrived), custom_call_target="tpu_custom_call" | custom-call | tf_op jit(solution)/shard_map/pallas_call | solution.py:173
  60.7 0.3 collective-permute-done.8.arrived
  61.0 0.7 %shard_map.73 = f32[1,5,256,256]{3,2,1,0:T(8,128)} custom-call(f32[5,32,256]{2,1,0:T(8,128)S(1)} %get-tuple-element.14.adjoint, f32[5,32,256]{2,1,0:T(8,128)S(1)} %collective-permute-done.8.arrived, f32[1,5,256,256]{3,2,1,0:T(8,128)} %shard_map.72.begun), custom_call_target="tpu_custom_call", output_to_operand_aliasing={{}: (2, {})} | custom-call | tf_op jit(solution)/shard_map/pallas_call | solution.py:181
  (8 shorter events, 0.0 us)
Async XLA Ops:
  0.6 13.6 %copy-start.5 = (f32[5]{0:T(128)S(1)}, f32[5]{0:T(128)}, u32[]{:S(2)}) copy-start(f32[5]{0:T(128)} %viscous.3) | copy-start | bytes 64
  0.6 38.1 %collective-permute-start.3 = (f32[5,256,256]{2,1,0:T(8,128)}, f32[5,256,256]{2,1,0:T(8,128)S(1)}, u32[]{:S(2)}, u32[]{:S(2)}) collective-permute-start(f32[5,256,256]{2,1,0:T(8,128)} %bitcast.12), channel_id=1, source_target_pairs={{0,24},{8,0},{16,8},{24,16},{1,25},{9,1},{17,9},{25,17},{2,26},{10... | collective-permute-start | bytes 3932168 | tf_op jit(solution)/shard_map/ppermute | solution.py:229
  4.6 1.4 %copy-start = (f32[1,5,256,256]{3,2,1,0:T(8,128)S(1)}, f32[1,5,256,256]{3,2,1,0:T(8,128)}, u32[]{:S(2)}) copy-start(f32[1,5,256,256]{3,2,1,0:T(8,128)} %param.5) | copy-start | bytes 3932164
  5.9 8.3 %copy-start.1 = (f32[1,5,256,256]{3,2,1,0:T(8,128)S(1)}, f32[1,5,256,256]{3,2,1,0:T(8,128)}, u32[]{:S(2)}) copy-start(f32[1,5,256,256]{3,2,1,0:T(8,128)} %param.5) | copy-start | bytes 3932164
  5.9 8.3 %copy-start.3 = (f32[5,5]{1,0:T(8,128)S(1)}, f32[5,5]{1,0:T(8,128)}, u32[]{:S(2)}) copy-start(f32[5,5]{1,0:T(8,128)} %mat_pitch.3) | copy-start | bytes 304
  5.9 8.3 %copy-start.4 = (f32[5,5]{1,0:T(8,128)S(1)}, f32[5,5]{1,0:T(8,128)}, u32[]{:S(2)}) copy-start(f32[5,5]{1,0:T(8,128)} %mat_span.3) | copy-start | bytes 304
  6.2 1.2 %collective-permute-start = (f32[24,256]{1,0:T(8,128)S(1)}, f32[24,256]{1,0:T(8,128)S(1)}, u32[]{:S(2)}, u32[]{:S(2)}) collective-permute-start(f32[24,256]{1,0:T(8,128)S(1)} %shard_map.68), channel_id=1, source_target_pairs={{0,1},{1,0},{2,3},{3,2},{4,5},{5,4},{6,7},{7,6},{8,9},{9,8},{10,11... | collective-permute-start | bytes 73736 | tf_op jit(solution)/shard_map/ppermute | solution.py:196
  7.5 6.2 %collective-permute-start.1 = (f32[5,8,384]{2,1,0:T(8,128)S(1)}, f32[5,8,384]{2,1,0:T(8,128)S(1)}, u32[]{:S(2)}, u32[]{:S(2)}) collective-permute-start(f32[5,8,384]{2,1,0:T(8,128)S(1)} %select_maximum_fusion.3), channel_id=1, source_target_pairs={{0,2},{2,4},{4,6},{6,0},{1,3},{3,5},{5,7},{7,1},{8,10},{10,12},{12... | collective-permute-start | bytes 184328 | tf_op jit(solution)/shard_map/ppermute | solution.py:209
  9.1 5.1 %collective-permute-start.2 = (f32[5,8,384]{2,1,0:T(8,128)S(1)}, f32[5,8,384]{2,1,0:T(8,128)S(1)}, u32[]{:S(2)}, u32[]{:S(2)}) collective-permute-start(f32[5,8,384]{2,1,0:T(8,128)S(1)} %select_maximum_fusion.2), channel_id=1, source_target_pairs={{2,0},{4,2},{6,4},{0,6},{3,1},{5,3},{7,5},{1,7},{10,8},{12,10},{14... | collective-permute-start | bytes 184328 | tf_op jit(solution)/shard_map/ppermute | solution.py:210
  14.2 1.3 %copy-start.2 = (f32[1,5,256,256]{3,2,1,0:T(8,128)S(1)}, f32[1,5,256,256]{3,2,1,0:T(8,128)}, u32[]{:S(2)}) copy-start(f32[1,5,256,256]{3,2,1,0:T(8,128)} %param.6) | copy-start | bytes 3932164
  24.2 35.3 %collective-permute-start.9 = (f32[5,224,256]{2,1,0:T(8,128)S(1)}, f32[5,224,256]{2,1,0:T(8,128)S(1)}, u32[]{:S(2)}, u32[]{:S(2)}) collective-permute-start(f32[5,224,256]{2,1,0:T(8,128)S(1)} %get-tuple-element.9.lead), channel_id=1, source_target_pairs={{0,8},{8,16},{16,24},{24,0},{1,9},{9,17},{17,25},{25,1},{2,10},{10... | collective-permute-start | bytes 3440648 | tf_op jit(solution)/shard_map/ppermute | solution.py:229
  24.3 0.7 %collective-permute-start.7 = (f32[5,32,256]{2,1,0:T(8,128)S(1)}, f32[5,32,256]{2,1,0:T(8,128)S(1)}, u32[]{:S(2)}, u32[]{:S(2)}) collective-permute-start(f32[5,32,256]{2,1,0:T(8,128)S(1)} %get-tuple-element.10.last), channel_id=1, source_target_pairs={{0,0},{8,24},{16,16},{24,8},{1,1},{9,25},{17,17},{25,9},{2,2},{10,... | collective-permute-start | bytes 491528 | tf_op jit(solution)/shard_map/ppermute | solution.py:236
  25.0 36.0 %collective-permute-start.8 = (f32[5,32,256]{2,1,0:T(8,128)S(1)}, f32[5,32,256]{2,1,0:T(8,128)S(1)}, u32[]{:S(2)}, u32[]{:S(2)}) collective-permute-start(f32[5,32,256]{2,1,0:T(8,128)S(1)} %collective-permute-done.7), channel_id=1, source_target_pairs={{0,8},{8,0},{16,24},{24,16},{1,9},{9,1},{17,25},{25,17},{2,10},{10... | collective-permute-start | bytes 491528 | tf_op jit(solution)/shard_map/ppermute | solution.py:237
  40.0 1.2 %collective-permute-start.4 = (f32[24,256]{1,0:T(8,128)S(1)}, f32[24,256]{1,0:T(8,128)S(1)}, u32[]{:S(2)}, u32[]{:S(2)}) collective-permute-start(f32[24,256]{1,0:T(8,128)S(1)} %get-tuple-element.13), channel_id=1, source_target_pairs={{0,1},{1,0},{2,3},{3,2},{4,5},{5,4},{6,7},{7,6},{8,9},{9,8},{10,11... | collective-permute-start | bytes 73736 | tf_op jit(solution)/shard_map/ppermute | solution.py:196
  41.2 6.2 %collective-permute-start.5 = (f32[5,8,384]{2,1,0:T(8,128)S(1)}, f32[5,8,384]{2,1,0:T(8,128)S(1)}, u32[]{:S(2)}, u32[]{:S(2)}) collective-permute-start(f32[5,8,384]{2,1,0:T(8,128)S(1)} %select_maximum_fusion.1), channel_id=1, source_target_pairs={{0,2},{2,4},{4,6},{6,0},{1,3},{3,5},{5,7},{7,1},{8,10},{10,12},{12... | collective-permute-start | bytes 184328 | tf_op jit(solution)/shard_map/ppermute | solution.py:209
  42.9 5.1 %collective-permute-start.6 = (f32[5,8,384]{2,1,0:T(8,128)S(1)}, f32[5,8,384]{2,1,0:T(8,128)S(1)}, u32[]{:S(2)}, u32[]{:S(2)}) collective-permute-start(f32[5,8,384]{2,1,0:T(8,128)S(1)} %select_maximum_fusion), channel_id=1, source_target_pairs={{2,0},{4,2},{6,4},{0,6},{3,1},{5,3},{7,5},{1,7},{10,8},{12,10},{14... | collective-permute-start | bytes 184328 | tf_op jit(solution)/shard_map/ppermute | solution.py:210

commit v4 on v2

--- a/solution.py
+++ b/solution.py
@@ -229,15 +229,16 @@
     return lax.ppermute(shard, "seg", [(i, (i + by) % count) for i in range(count)])
 
 
-def passed_in_turn(shard, after, by):
+def passed_by_swap(shard, after):
     count, width = lax.axis_size("seg"), lax.axis_size("span")
-
-    def share(cells, parity):
-        pairs = [(i * width + k, (i + by) % count * width + k) for i in range(count) for k in range(parity, width, 2)]
+    held = lax.ppermute(shard, "seg", [(i, (i + 2) % count if i % 2 else i) for i in range(count)])
+
+    def swapped(cells, parity):
+        pairs = [(i * width + k, (i ^ 1) * width + k) for i in range(count) for k in range(parity, width, 2)]
         return lax.ppermute(cells, ("seg", "span"), pairs)
 
-    early = share(shard, 0)
-    late = share(lax.optimization_barrier((shard, after))[0], 1)
+    early = swapped(held, 0)
+    late = swapped(lax.optimization_barrier((held, after))[0], 1)
     return early, late
 
 
@@ -251,7 +252,7 @@
     mismatch, again, strip = mismatch_of(*ending, following)
     halos = exchanged(again, strip)
     adjoint = propagated(position, adv_pitch, adv_span, diffusion, again, start, halos, True, 1.0, 1.0)
-    arrived.append(passed_in_turn(ending[1], adjoint[0], 1))
+    arrived.append(passed_by_swap(ending[1], adjoint[0]))
     return (mismatch[None], gradient_of(adjoint, arrived))
 
 

time: 62.2 us -> 61.5 us (0.989)
  waiting for transfers between devices: 20.8 us -> 19.9 us
  starting transfers between devices: 16.5 us -> 17.2 us
    ppermute x2, waiting for transfers between devices: 12.7 us -> 12.1 us  [passed_along(): lax.ppermute(shard, 'seg', [(i, (i + by) % count) for i in range(count)])]
    ppermute x2 -> x3, starting transfers between devices: 4.9 us -> 5.57 us  [the longest x2 4.9 us: swapped(): return lax.ppermute(cells, ('seg', 'span'), pairs)]
  transfers between devices with their start and end apart: 10 -> 11, of which waited for: 8 -> 8; matrix products, arithmetic and copies ran while one was open for 0% -> 0% of each run, Pallas kernels for 32% -> 32%
where the time goes in v4:
time: 61.5 us; the launch traced here: 61.2 us
  Pallas kernels  20.6 us (33%)
  waiting for transfers between devices  19.9 us (32%)
  starting transfers between devices  17.2 us (28%)
  local copies, waits for them, and re-layouts  2.7 us (4%)
  between operations  0.75 us (1%)
    pallas_call x2, Pallas kernels, propagated(): pl.pallas_call(functools.partial(propagate_kernel, transposed, sign, scal...  17.2 us
    ppermute x2, waiting for transfers between devices, passed_along(): lax.ppermute(shard, 'seg', [(i, (i + by) % count) for i in range(count)])  12.1 us
    ppermute x2, starting transfers between devices, exchanged(): lax.ppermute(outer(0, 0), 'pitch', [((i + 1) % ring, i) for i in range(ri...  5.9 us
    ppermute x2, starting transfers between devices, swapped(): return lax.ppermute(cells, ('seg', 'span'), pairs)  4.9 us
    ppermute x2, starting transfers between devices, passed_along(): lax.ppermute(shard, 'seg', [(i, (i + by) % count) for i in range(count)])  4 us
    ppermute x2, waiting for transfers between devices, exchanged(): lax.ppermute(outer(rows - TILE, rows - LANES), 'pitch', [(i, (i + 1) % ri...  3.96 us
    unnamed x12, local copies, waits for them, and re-layouts  2.68 us
    ppermute x2, waiting for transfers between devices, exchanged(): sides = lax.ppermute(strip, 'span', [(0, 1), (1, 0)])  2.35 us
  transfers between devices with their start and end apart: 11, of which 8 were waited for; matrix products, arithmetic and copies ran while one was open for 0% of the time, Pallas kernels for 32%

profile of v4, /device:TPU:0, one launch (start us, length us, event | category | flops | bytes accessed | tf_op | source)
XLA Modules:
  0.0 61.2 jit_solution(11993426190062698486)
XLA Ops:
  0.6 0.0 copy-start.5
  0.6 3.9 %collective-permute-start.3 = (f32[5,256,256]{2,1,0:T(8,128)}, f32[5,256,256]{2,1,0:T(8,128)S(1)}, u32[]{:S(2)}, u32[]{:S(2)}) collective-permute-start(f32[5,256,256]{2,1,0:T(8,128)} %bitcast.12), channel_id=1, source_target_pairs={{0,24},{8,0},{16,8},{24,16},{1,25},{9,1},{17,9},{25,17},{2,26},{10... | collective-permute-start | bytes 3932168 | tf_op jit(solution)/shard_map/ppermute | solution.py:229
  4.6 0.0 copy-start
  4.6 1.3 %copy-done = f32[1,5,256,256]{3,2,1,0:T(8,128)S(1)} copy-done((f32[1,5,256,256]{3,2,1,0:T(8,128)S(1)}, f32[1,5,256,256]{3,2,1,0:T(8,128)}, u32[]{:S(2)}) %copy-start) | copy-done | bytes 1310744
  5.9 0.0 copy-start.1
  5.9 0.0 copy-start.3
  5.9 0.0 copy-start.4
  5.9 0.3 shard_map.68
  6.2 0.0 collective-permute-start
  6.3 1.2 %collective-permute-done.strip = f32[24,256]{1,0:T(8,128)S(1)} collective-permute-done((f32[24,256]{1,0:T(8,128)S(1)}, f32[24,256]{1,0:T(8,128)S(1)}, u32[]{:S(2)}, u32[]{:S(2)}) %collective-permute-start) | collective-permute-done | bytes 24608 | tf_op jit(solution)/shard_map/ppermute | solution.py:196
  7.5 1.6 %collective-permute-start.1 = (f32[5,8,384]{2,1,0:T(8,128)S(1)}, f32[5,8,384]{2,1,0:T(8,128)S(1)}, u32[]{:S(2)}, u32[]{:S(2)}) collective-permute-start(f32[5,8,384]{2,1,0:T(8,128)S(1)} %select_maximum_fusion.3), channel_id=1, source_target_pairs={{0,2},{2,4},{4,6},{6,0},{1,3},{3,5},{5,7},{7,1},{8,10},{10,12},{12... | collective-permute-start | bytes 184328 | tf_op jit(solution)/shard_map/ppermute | solution.py:209
  9.1 2.2 %collective-permute-start.2 = (f32[5,8,384]{2,1,0:T(8,128)S(1)}, f32[5,8,384]{2,1,0:T(8,128)S(1)}, u32[]{:S(2)}, u32[]{:S(2)}) collective-permute-start(f32[5,8,384]{2,1,0:T(8,128)S(1)} %select_maximum_fusion.2), channel_id=1, source_target_pairs={{2,0},{4,2},{6,4},{0,6},{3,1},{5,3},{7,5},{1,7},{10,8},{12,10},{14... | collective-permute-start | bytes 184328 | tf_op jit(solution)/shard_map/ppermute | solution.py:210
  11.3 0.1 pad_add_fusion.position
  11.4 2.2 %collective-permute-done.1.upper = f32[5,8,384]{2,1,0:T(8,128)S(1)} collective-permute-done((f32[5,8,384]{2,1,0:T(8,128)S(1)}, f32[5,8,384]{2,1,0:T(8,128)S(1)}, u32[]{:S(2)}, u32[]{:S(2)}) %collective-permute-start.1) | collective-permute-done | bytes 61472 | tf_op jit(solution)/shard_map/ppermute | solution.py:209
  13.6 0.6 collective-permute-done.2.lower
  14.2 0.0 copy-done.5
  14.2 0.0 copy-done.1
  14.2 0.0 copy-done.3
  14.2 0.0 copy-done.4
  14.2 0.0 copy-start.2
  14.2 1.3 %copy-done.2 = f32[1,5,256,256]{3,2,1,0:T(8,128)S(1)} copy-done((f32[1,5,256,256]{3,2,1,0:T(8,128)S(1)}, f32[1,5,256,256]{3,2,1,0:T(8,128)}, u32[]{:S(2)}) %copy-start.2) | copy-done | bytes 1310744
  15.6 8.7 %shard_map.69 = (f32[5,224,256]{2,1,0:T(8,128)S(1)}, f32[5,32,256]{2,1,0:T(8,128)S(1)}) custom-call(s32[2]{0:T(128)S(1)} %pad_add_fusion.position, f32[5,5]{1,0:T(8,128)S(1)} %copy-done.3, f32[5,5]{1,0:T(8,128)S(1)} %copy-done.4, f32[5]{0:T(128)S(1)} %copy-done.5, f32[5,256,256]{2,1,0:T(8,128)S(1)} %bitcast.15, f32[5,256,256]{2,1,0:T(8,128)S(1)} %bitcast.17, ...), custom_call_target="tpu_custom_call" | custom-call | tf_op jit(solution)/shard_map/pallas_call | solution.py:217
  24.2 0.1 collective-permute-start.10
  24.3 0.7 %collective-permute-start.7 = (f32[5,32,256]{2,1,0:T(8,128)S(1)}, f32[5,32,256]{2,1,0:T(8,128)S(1)}, u32[]{:S(2)}, u32[]{:S(2)}) collective-permute-start(f32[5,32,256]{2,1,0:T(8,128)S(1)} %get-tuple-element.11.last), channel_id=1, source_target_pairs={{0,0},{8,24},{16,16},{24,8},{1,1},{9,25},{17,17},{25,9},{2,2},{10,... | collective-permute-start | bytes 491528 | tf_op jit(solution)/shard_map/ppermute | solution.py:234
  24.9 9.2 %collective-permute-done.3.following = f32[5,256,256]{2,1,0:T(8,128)S(1)} collective-permute-done((f32[5,256,256]{2,1,0:T(8,128)}, f32[5,256,256]{2,1,0:T(8,128)S(1)}, u32[]{:S(2)}, u32[]{:S(2)}) %collective-permute-start.3) | collective-permute-done | bytes 1310752 | tf_op jit(solution)/shard_map/ppermute | solution.py:229
  34.1 1.3 %shard_map.70 = (f32[5,256,256]{2,1,0:T(8,128)}, f32[5,256,256]{2,1,0:T(8,128)S(1)}, f32[24,256]{1,0:T(8,128)S(1)}) custom-call(f32[5,224,256]{2,1,0:T(8,128)S(1)} %get-tuple-element.10.lead, f32[5,32,256]{2,1,0:T(8,128)S(1)} %get-tuple-element.11.last, f32[5,256,256]{2,1,0:T(8,128)S(1)} %collective-permute-done.3.following), custom_call_target="tpu_custom_call" | custom-call | tf_op jit(solution)/shard_map/pallas_call | solution.py:160
  35.4 0.0 collective-permute-start.4
  35.4 1.2 %collective-permute-done.4.strip = f32[24,256]{1,0:T(8,128)S(1)} collective-permute-done((f32[24,256]{1,0:T(8,128)S(1)}, f32[24,256]{1,0:T(8,128)S(1)}, u32[]{:S(2)}, u32[]{:S(2)}) %collective-permute-start.4) | collective-permute-done | bytes 24608 | tf_op jit(solution)/shard_map/ppermute | solution.py:196
  36.6 3.7 %collective-permute-start.6 = (f32[5,8,384]{2,1,0:T(8,128)S(1)}, f32[5,8,384]{2,1,0:T(8,128)S(1)}, u32[]{:S(2)}, u32[]{:S(2)}) collective-permute-start(f32[5,8,384]{2,1,0:T(8,128)S(1)} %select_maximum_fusion), channel_id=1, source_target_pairs={{2,0},{4,2},{6,4},{0,6},{3,1},{5,3},{7,5},{1,7},{10,8},{12,10},{14... | collective-permute-start | bytes 184328 | tf_op jit(solution)/shard_map/ppermute | solution.py:210
  40.2 0.0 collective-permute-start.5
  40.3 0.0 collective-permute-done.7
  40.3 4.2 %collective-permute-start.8 = (f32[5,32,256]{2,1,0:T(8,128)S(1)}, f32[5,32,256]{2,1,0:T(8,128)S(1)}, u32[]{:S(2)}, u32[]{:S(2)}) collective-permute-start(f32[5,32,256]{2,1,0:T(8,128)S(1)} %collective-permute-done.7), channel_id=1, source_target_pairs={{0,8},{8,0},{16,24},{24,16},{2,10},{10,2},{18,26},{26,18},{4,12},{... | collective-permute-start | bytes 491528 | tf_op jit(solution)/shard_map/ppermute | solution.py:238
  44.5 0.0 collective-permute-done.6.lower
  44.5 1.8 %collective-permute-done.5.upper = f32[5,8,384]{2,1,0:T(8,128)S(1)} collective-permute-done((f32[5,8,384]{2,1,0:T(8,128)S(1)}, f32[5,8,384]{2,1,0:T(8,128)S(1)}, u32[]{:S(2)}, u32[]{:S(2)}) %collective-permute-start.5) | collective-permute-done | bytes 61472 | tf_op jit(solution)/shard_map/ppermute | solution.py:209
  46.3 8.6 %shard_map.71 = (f32[5,224,256]{2,1,0:T(8,128)S(1)}, f32[5,32,256]{2,1,0:T(8,128)S(1)}) custom-call(s32[2]{0:T(128)S(1)} %pad_add_fusion.position, f32[5,5]{1,0:T(8,128)S(1)} %copy-done.3, f32[5,5]{1,0:T(8,128)S(1)} %copy-done.4, f32[5]{0:T(128)S(1)} %copy-done.5, f32[5,256,256]{2,1,0:T(8,128)S(1)} %get-tuple-element.13.cells, f32[5,256,256]{2,1,0:T(8,128)S(1)} %bitcast.16, ...), custom_call_target="tpu_custom_call" | custom-call | tf_op jit(solution)/shard_map/pallas_call | solution.py:217
  54.8 0.7 %collective-permute-start.9 = (f32[5,32,256]{2,1,0:T(8,128)S(1)}, f32[5,32,256]{2,1,0:T(8,128)S(1)}, u32[]{:S(2)}, u32[]{:S(2)}) collective-permute-start(f32[5,32,256]{2,1,0:T(8,128)S(1)} %collective-permute-done.7), channel_id=1, source_target_pairs={{1,9},{9,1},{17,25},{25,17},{3,11},{11,3},{19,27},{27,19},{5,13},{... | collective-permute-start | bytes 491528 | tf_op jit(solution)/shard_map/ppermute | solution.py:238
  55.5 2.9 %collective-permute-done.10.arrived = f32[5,224,256]{2,1,0:T(8,128)S(1)} collective-permute-done((f32[5,224,256]{2,1,0:T(8,128)S(1)}, f32[5,224,256]{2,1,0:T(8,128)S(1)}, u32[]{:S(2)}, u32[]{:S(2)}) %collective-permute-start.10) | collective-permute-done | bytes 1146912 | tf_op jit(solution)/shard_map/ppermute | solution.py:229
  58.4 1.1 %shard_map.72.begun = f32[1,5,256,256]{3,2,1,0:T(8,128)} custom-call(f32[5,224,256]{2,1,0:T(8,128)S(1)} %get-tuple-element.16.adjoint, f32[5,224,256]{2,1,0:T(8,128)S(1)} %collective-permute-done.10.arrived), custom_call_target="tpu_custom_call" | custom-call | tf_op jit(solution)/shard_map/pallas_call | solution.py:173
  59.5 0.9 %collective-permute-done.8.early = f32[5,32,256]{2,1,0:T(8,128)S(1)} collective-permute-done((f32[5,32,256]{2,1,0:T(8,128)S(1)}, f32[5,32,256]{2,1,0:T(8,128)S(1)}, u32[]{:S(2)}, u32[]{:S(2)}) %collective-permute-start.8) | collective-permute-done | bytes 163872 | tf_op jit(solution)/shard_map/ppermute | solution.py:238
  60.5 0.0 collective-permute-done.9.late
  60.5 0.7 %shard_map.73 = f32[1,5,256,256]{3,2,1,0:T(8,128)} custom-call(f32[5,32,256]{2,1,0:T(8,128)S(1)} %get-tuple-element.15.adjoint, f32[5,32,256]{2,1,0:T(8,128)S(1)} %collective-permute-done.8.early, f32[5,32,256]{2,1,0:T(8,128)S(1)} %collective-permute-done.9.late, f32[1,5,256,256]{3,2,1,0:T(8,128)} %shard_map.72.begun), custom_call_target="tpu_custom_call", output_to_operand_aliasing={{}: (3, {})} | custom-call | tf_op jit(solution)/shard_map/pallas_call | solution.py:181
  (8 shorter events, 0.0 us)
Async XLA Ops:
  0.6 13.6 %copy-start.5 = (f32[5]{0:T(128)S(1)}, f32[5]{0:T(128)}, u32[]{:S(2)}) copy-start(f32[5]{0:T(128)} %viscous.3) | copy-start | bytes 64
  0.6 33.5 %collective-permute-start.3 = (f32[5,256,256]{2,1,0:T(8,128)}, f32[5,256,256]{2,1,0:T(8,128)S(1)}, u32[]{:S(2)}, u32[]{:S(2)}) collective-permute-start(f32[5,256,256]{2,1,0:T(8,128)} %bitcast.12), channel_id=1, source_target_pairs={{0,24},{8,0},{16,8},{24,16},{1,25},{9,1},{17,9},{25,17},{2,26},{10... | collective-permute-start | bytes 3932168 | tf_op jit(solution)/shard_map/ppermute | solution.py:229
  4.6 1.4 %copy-start = (f32[1,5,256,256]{3,2,1,0:T(8,128)S(1)}, f32[1,5,256,256]{3,2,1,0:T(8,128)}, u32[]{:S(2)}) copy-start(f32[1,5,256,256]{3,2,1,0:T(8,128)} %param.5) | copy-start | bytes 3932164
  5.9 8.3 %copy-start.1 = (f32[1,5,256,256]{3,2,1,0:T(8,128)S(1)}, f32[1,5,256,256]{3,2,1,0:T(8,128)}, u32[]{:S(2)}) copy-start(f32[1,5,256,256]{3,2,1,0:T(8,128)} %param.5) | copy-start | bytes 3932164
  5.9 8.3 %copy-start.3 = (f32[5,5]{1,0:T(8,128)S(1)}, f32[5,5]{1,0:T(8,128)}, u32[]{:S(2)}) copy-start(f32[5,5]{1,0:T(8,128)} %mat_pitch.3) | copy-start | bytes 304
  5.9 8.3 %copy-start.4 = (f32[5,5]{1,0:T(8,128)S(1)}, f32[5,5]{1,0:T(8,128)}, u32[]{:S(2)}) copy-start(f32[5,5]{1,0:T(8,128)} %mat_span.3) | copy-start | bytes 304
  6.2 1.2 %collective-permute-start = (f32[24,256]{1,0:T(8,128)S(1)}, f32[24,256]{1,0:T(8,128)S(1)}, u32[]{:S(2)}, u32[]{:S(2)}) collective-permute-start(f32[24,256]{1,0:T(8,128)S(1)} %shard_map.68), channel_id=1, source_target_pairs={{0,1},{1,0},{2,3},{3,2},{4,5},{5,4},{6,7},{7,6},{8,9},{9,8},{10,11... | collective-permute-start | bytes 73736 | tf_op jit(solution)/shard_map/ppermute | solution.py:196
  7.5 6.2 %collective-permute-start.1 = (f32[5,8,384]{2,1,0:T(8,128)S(1)}, f32[5,8,384]{2,1,0:T(8,128)S(1)}, u32[]{:S(2)}, u32[]{:S(2)}) collective-permute-start(f32[5,8,384]{2,1,0:T(8,128)S(1)} %select_maximum_fusion.3), channel_id=1, source_target_pairs={{0,2},{2,4},{4,6},{6,0},{1,3},{3,5},{5,7},{7,1},{8,10},{10,12},{12... | collective-permute-start | bytes 184328 | tf_op jit(solution)/shard_map/ppermute | solution.py:209
  9.1 5.1 %collective-permute-start.2 = (f32[5,8,384]{2,1,0:T(8,128)S(1)}, f32[5,8,384]{2,1,0:T(8,128)S(1)}, u32[]{:S(2)}, u32[]{:S(2)}) collective-permute-start(f32[5,8,384]{2,1,0:T(8,128)S(1)} %select_maximum_fusion.2), channel_id=1, source_target_pairs={{2,0},{4,2},{6,4},{0,6},{3,1},{5,3},{7,5},{1,7},{10,8},{12,10},{14... | collective-permute-start | bytes 184328 | tf_op jit(solution)/shard_map/ppermute | solution.py:210
  14.2 1.3 %copy-start.2 = (f32[1,5,256,256]{3,2,1,0:T(8,128)S(1)}, f32[1,5,256,256]{3,2,1,0:T(8,128)}, u32[]{:S(2)}) copy-start(f32[1,5,256,256]{3,2,1,0:T(8,128)} %param.6) | copy-start | bytes 3932164
  24.2 34.2 %collective-permute-start.10 = (f32[5,224,256]{2,1,0:T(8,128)S(1)}, f32[5,224,256]{2,1,0:T(8,128)S(1)}, u32[]{:S(2)}, u32[]{:S(2)}) collective-permute-start(f32[5,224,256]{2,1,0:T(8,128)S(1)} %get-tuple-element.10.lead), channel_id=1, source_target_pairs={{0,8},{8,16},{16,24},{24,0},{1,9},{9,17},{17,25},{25,1},{2,10},{10... | collective-permute-start | bytes 3440648 | tf_op jit(solution)/shard_map/ppermute | solution.py:229
  24.3 16.0 %collective-permute-start.7 = (f32[5,32,256]{2,1,0:T(8,128)S(1)}, f32[5,32,256]{2,1,0:T(8,128)S(1)}, u32[]{:S(2)}, u32[]{:S(2)}) collective-permute-start(f32[5,32,256]{2,1,0:T(8,128)S(1)} %get-tuple-element.11.last), channel_id=1, source_target_pairs={{0,0},{8,24},{16,16},{24,8},{1,1},{9,25},{17,17},{25,9},{2,2},{10,... | collective-permute-start | bytes 491528 | tf_op jit(solution)/shard_map/ppermute | solution.py:234
  35.4 1.2 %collective-permute-start.4 = (f32[24,256]{1,0:T(8,128)S(1)}, f32[24,256]{1,0:T(8,128)S(1)}, u32[]{:S(2)}, u32[]{:S(2)}) collective-permute-start(f32[24,256]{1,0:T(8,128)S(1)} %get-tuple-element.14), channel_id=1, source_target_pairs={{0,1},{1,0},{2,3},{3,2},{4,5},{5,4},{6,7},{7,6},{8,9},{9,8},{10,11... | collective-permute-start | bytes 73736 | tf_op jit(solution)/shard_map/ppermute | solution.py:196
  36.6 7.9 %collective-permute-start.6 = (f32[5,8,384]{2,1,0:T(8,128)S(1)}, f32[5,8,384]{2,1,0:T(8,128)S(1)}, u32[]{:S(2)}, u32[]{:S(2)}) collective-permute-start(f32[5,8,384]{2,1,0:T(8,128)S(1)} %select_maximum_fusion), channel_id=1, source_target_pairs={{2,0},{4,2},{6,4},{0,6},{3,1},{5,3},{7,5},{1,7},{10,8},{12,10},{14... | collective-permute-start | bytes 184328 | tf_op jit(solution)/shard_map/ppermute | solution.py:210
  40.2 6.0 %collective-permute-start.5 = (f32[5,8,384]{2,1,0:T(8,128)S(1)}, f32[5,8,384]{2,1,0:T(8,128)S(1)}, u32[]{:S(2)}, u32[]{:S(2)}) collective-permute-start(f32[5,8,384]{2,1,0:T(8,128)S(1)} %select_maximum_fusion.1), channel_id=1, source_target_pairs={{0,2},{2,4},{4,6},{6,0},{1,3},{3,5},{5,7},{7,1},{8,10},{10,12},{12... | collective-permute-start | bytes 184328 | tf_op jit(solution)/shard_map/ppermute | solution.py:209
  40.3 20.2 %collective-permute-start.8 = (f32[5,32,256]{2,1,0:T(8,128)S(1)}, f32[5,32,256]{2,1,0:T(8,128)S(1)}, u32[]{:S(2)}, u32[]{:S(2)}) collective-permute-start(f32[5,32,256]{2,1,0:T(8,128)S(1)} %collective-permute-done.7), channel_id=1, source_target_pairs={{0,8},{8,0},{16,24},{24,16},{2,10},{10,2},{18,26},{26,18},{4,12},{... | collective-permute-start | bytes 491528 | tf_op jit(solution)/shard_map/ppermute | solution.py:238
  54.8 5.6 %collective-permute-start.9 = (f32[5,32,256]{2,1,0:T(8,128)S(1)}, f32[5,32,256]{2,1,0:T(8,128)S(1)}, u32[]{:S(2)}, u32[]{:S(2)}) collective-permute-start(f32[5,32,256]{2,1,0:T(8,128)S(1)} %collective-permute-done.7), channel_id=1, source_target_pairs={{1,9},{9,1},{17,25},{25,17},{3,11},{11,3},{19,27},{27,19},{5,13},{... | collective-permute-start | bytes 491528 | tf_op jit(solution)/shard_map/ppermute | solution.py:238

commit v5 on v4

--- a/solution.py
+++ b/solution.py
@@ -111,7 +111,7 @@
             second[f, pl.ds(pl.multiple_of(tile * TILE, TILE), TILE), cols:] = jnp.where(inside_tile, value[:, cols:], 0.0)
         return carry
 
-    lax.fori_loop(1, (MARGIN + rows) // TILE + 1, step_one, 0, unroll=2)
+    lax.fori_loop(1, (MARGIN + rows) // TILE + 1, step_one, 0, unroll=17)
 
     def step_two(result, base, tile, carry):
         for f, value in enumerate(substep(second, tile, coefficients, cols)):
@@ -122,7 +122,7 @@
 
     begin = lead.shape[1]
     bounds = [MARGIN // TILE, (MARGIN + begin) // TILE, (MARGIN + rows) // TILE]
-    lax.fori_loop(bounds[0], bounds[1], functools.partial(step_two, lead, 0), 0, unroll=4)
+    lax.fori_loop(bounds[0], bounds[1], functools.partial(step_two, lead, 0), 0, unroll=7)
     lax.fori_loop(bounds[1], bounds[2], functools.partial(step_two, last, begin), 0, unroll=4)
 
 

time: 61.5 us -> 61.7 us (level)
  waiting for transfers between devices: 19.9 us -> 20.8 us
  Pallas kernels: 20.6 us -> 19.9 us
    ppermute x2, waiting for transfers between devices: 12.1 us -> 12.7 us  [passed_along(): lax.ppermute(shard, 'seg', [(i, (i + by) % count) for i in range(count)])]
    pallas_call x2, Pallas kernels: 17.2 us -> 16.6 us  [propagated(): pl.pallas_call(functools.partial(propagate_kernel, transposed, sign, scal...]
  transfers between devices with their start and end apart: 11 -> 11, of which waited for: 8 -> 8; matrix products, arithmetic and copies ran while one was open for 0% -> 0% of each run, Pallas kernels for 32% -> 31%
where the time goes in v5:
time: 61.7 us; the launch traced here: 61.4 us
  waiting for transfers between devices  20.8 us (34%)
  Pallas kernels  19.9 us (32%)
  starting transfers between devices  17.2 us (28%)
  local copies, waits for them, and re-layouts  2.7 us (4%)
  between operations  0.75 us (1%)
    pallas_call x2, Pallas kernels, propagated(): pl.pallas_call(functools.partial(propagate_kernel, transposed, sign, scal...  16.6 us
    ppermute x2, waiting for transfers between devices, passed_along(): lax.ppermute(shard, 'seg', [(i, (i + by) % count) for i in range(count)])  12.7 us
    ppermute x2, starting transfers between devices, exchanged(): lax.ppermute(outer(0, 0), 'pitch', [((i + 1) % ring, i) for i in range(ri...  5.9 us
    ppermute x2, starting transfers between devices, swapped(): return lax.ppermute(cells, ('seg', 'span'), pairs)  4.9 us
    ppermute x2, starting transfers between devices, passed_along(): lax.ppermute(shard, 'seg', [(i, (i + by) % count) for i in range(count)])  4 us
    ppermute x2, waiting for transfers between devices, exchanged(): lax.ppermute(outer(rows - TILE, rows - LANES), 'pitch', [(i, (i + 1) % ri...  3.96 us
    unnamed x12, local copies, waits for them, and re-layouts  2.68 us
    ppermute x2, waiting for transfers between devices, exchanged(): sides = lax.ppermute(strip, 'span', [(0, 1), (1, 0)])  2.35 us
  transfers between devices with their start and end apart: 11, of which 8 were waited for; matrix products, arithmetic and copies ran while one was open for 0% of the time, Pallas kernels for 31%

profile of v5, /device:TPU:0, one launch (start us, length us, event | category | flops | bytes accessed | tf_op | source)
XLA Modules:
  0.0 61.4 jit_solution(1242558804343535177)
XLA Ops:
  0.6 0.0 copy-start.5
  0.6 3.9 %collective-permute-start.3 = (f32[5,256,256]{2,1,0:T(8,128)}, f32[5,256,256]{2,1,0:T(8,128)S(1)}, u32[]{:S(2)}, u32[]{:S(2)}) collective-permute-start(f32[5,256,256]{2,1,0:T(8,128)} %bitcast.12), channel_id=1, source_target_pairs={{0,24},{8,0},{16,8},{24,16},{1,25},{9,1},{17,9},{25,17},{2,26},{10... | collective-permute-start | bytes 3932168 | tf_op jit(solution)/shard_map/ppermute | solution.py:229
  4.6 0.0 copy-start
  4.6 1.3 %copy-done = f32[1,5,256,256]{3,2,1,0:T(8,128)S(1)} copy-done((f32[1,5,256,256]{3,2,1,0:T(8,128)S(1)}, f32[1,5,256,256]{3,2,1,0:T(8,128)}, u32[]{:S(2)}) %copy-start) | copy-done | bytes 1310744
  5.9 0.0 copy-start.1
  5.9 0.0 copy-start.3
  5.9 0.0 copy-start.4
  5.9 0.3 shard_map.68
  6.2 0.0 collective-permute-start
  6.3 1.2 %collective-permute-done.strip = f32[24,256]{1,0:T(8,128)S(1)} collective-permute-done((f32[24,256]{1,0:T(8,128)S(1)}, f32[24,256]{1,0:T(8,128)S(1)}, u32[]{:S(2)}, u32[]{:S(2)}) %collective-permute-start) | collective-permute-done | bytes 24608 | tf_op jit(solution)/shard_map/ppermute | solution.py:196
  7.5 1.6 %collective-permute-start.1 = (f32[5,8,384]{2,1,0:T(8,128)S(1)}, f32[5,8,384]{2,1,0:T(8,128)S(1)}, u32[]{:S(2)}, u32[]{:S(2)}) collective-permute-start(f32[5,8,384]{2,1,0:T(8,128)S(1)} %select_maximum_fusion.3), channel_id=1, source_target_pairs={{0,2},{2,4},{4,6},{6,0},{1,3},{3,5},{5,7},{7,1},{8,10},{10,12},{12... | collective-permute-start | bytes 184328 | tf_op jit(solution)/shard_map/ppermute | solution.py:209
  9.1 2.2 %collective-permute-start.2 = (f32[5,8,384]{2,1,0:T(8,128)S(1)}, f32[5,8,384]{2,1,0:T(8,128)S(1)}, u32[]{:S(2)}, u32[]{:S(2)}) collective-permute-start(f32[5,8,384]{2,1,0:T(8,128)S(1)} %select_maximum_fusion.2), channel_id=1, source_target_pairs={{2,0},{4,2},{6,4},{0,6},{3,1},{5,3},{7,5},{1,7},{10,8},{12,10},{14... | collective-permute-start | bytes 184328 | tf_op jit(solution)/shard_map/ppermute | solution.py:210
  11.3 0.1 pad_add_fusion.position
  11.4 2.2 %collective-permute-done.1.upper = f32[5,8,384]{2,1,0:T(8,128)S(1)} collective-permute-done((f32[5,8,384]{2,1,0:T(8,128)S(1)}, f32[5,8,384]{2,1,0:T(8,128)S(1)}, u32[]{:S(2)}, u32[]{:S(2)}) %collective-permute-start.1) | collective-permute-done | bytes 61472 | tf_op jit(solution)/shard_map/ppermute | solution.py:209
  13.6 0.6 collective-permute-done.2.lower
  14.2 0.0 copy-done.5
  14.2 0.0 copy-done.1
  14.2 0.0 copy-done.3
  14.2 0.0 copy-done.4
  14.2 0.0 copy-start.2
  14.2 1.3 %copy-done.2 = f32[1,5,256,256]{3,2,1,0:T(8,128)S(1)} copy-done((f32[1,5,256,256]{3,2,1,0:T(8,128)S(1)}, f32[1,5,256,256]{3,2,1,0:T(8,128)}, u32[]{:S(2)}) %copy-start.2) | copy-done | bytes 1310744
  15.6 8.3 %shard_map.69 = (f32[5,224,256]{2,1,0:T(8,128)S(1)}, f32[5,32,256]{2,1,0:T(8,128)S(1)}) custom-call(s32[2]{0:T(128)S(1)} %pad_add_fusion.position, f32[5,5]{1,0:T(8,128)S(1)} %copy-done.3, f32[5,5]{1,0:T(8,128)S(1)} %copy-done.4, f32[5]{0:T(128)S(1)} %copy-done.5, f32[5,256,256]{2,1,0:T(8,128)S(1)} %bitcast.15, f32[5,256,256]{2,1,0:T(8,128)S(1)} %bitcast.17, ...), custom_call_target="tpu_custom_call" | custom-call | tf_op jit(solution)/shard_map/pallas_call | solution.py:217
  23.9 0.1 collective-permute-start.10
  23.9 0.7 %collective-permute-start.7 = (f32[5,32,256]{2,1,0:T(8,128)S(1)}, f32[5,32,256]{2,1,0:T(8,128)S(1)}, u32[]{:S(2)}, u32[]{:S(2)}) collective-permute-start(f32[5,32,256]{2,1,0:T(8,128)S(1)} %get-tuple-element.11.last), channel_id=1, source_target_pairs={{0,0},{8,24},{16,16},{24,8},{1,1},{9,25},{17,17},{25,9},{2,2},{10,... | collective-permute-start | bytes 491528 | tf_op jit(solution)/shard_map/ppermute | solution.py:234
  24.6 9.5 %collective-permute-done.3.following = f32[5,256,256]{2,1,0:T(8,128)S(1)} collective-permute-done((f32[5,256,256]{2,1,0:T(8,128)}, f32[5,256,256]{2,1,0:T(8,128)S(1)}, u32[]{:S(2)}, u32[]{:S(2)}) %collective-permute-start.3) | collective-permute-done | bytes 1310752 | tf_op jit(solution)/shard_map/ppermute | solution.py:229
  34.1 1.3 %shard_map.70 = (f32[5,256,256]{2,1,0:T(8,128)}, f32[5,256,256]{2,1,0:T(8,128)S(1)}, f32[24,256]{1,0:T(8,128)S(1)}) custom-call(f32[5,224,256]{2,1,0:T(8,128)S(1)} %get-tuple-element.10.lead, f32[5,32,256]{2,1,0:T(8,128)S(1)} %get-tuple-element.11.last, f32[5,256,256]{2,1,0:T(8,128)S(1)} %collective-permute-done.3.following), custom_call_target="tpu_custom_call" | custom-call | tf_op jit(solution)/shard_map/pallas_call | solution.py:160
  35.4 0.0 collective-permute-start.4
  35.4 1.2 %collective-permute-done.4.strip = f32[24,256]{1,0:T(8,128)S(1)} collective-permute-done((f32[24,256]{1,0:T(8,128)S(1)}, f32[24,256]{1,0:T(8,128)S(1)}, u32[]{:S(2)}, u32[]{:S(2)}) %collective-permute-start.4) | collective-permute-done | bytes 24608 | tf_op jit(solution)/shard_map/ppermute | solution.py:196
  36.6 3.7 %collective-permute-start.6 = (f32[5,8,384]{2,1,0:T(8,128)S(1)}, f32[5,8,384]{2,1,0:T(8,128)S(1)}, u32[]{:S(2)}, u32[]{:S(2)}) collective-permute-start(f32[5,8,384]{2,1,0:T(8,128)S(1)} %select_maximum_fusion), channel_id=1, source_target_pairs={{2,0},{4,2},{6,4},{0,6},{3,1},{5,3},{7,5},{1,7},{10,8},{12,10},{14... | collective-permute-start | bytes 184328 | tf_op jit(solution)/shard_map/ppermute | solution.py:210
  40.2 0.0 collective-permute-start.5
  40.3 0.0 collective-permute-done.7
  40.3 4.2 %collective-permute-start.8 = (f32[5,32,256]{2,1,0:T(8,128)S(1)}, f32[5,32,256]{2,1,0:T(8,128)S(1)}, u32[]{:S(2)}, u32[]{:S(2)}) collective-permute-start(f32[5,32,256]{2,1,0:T(8,128)S(1)} %collective-permute-done.7), channel_id=1, source_target_pairs={{0,8},{8,0},{16,24},{24,16},{2,10},{10,2},{18,26},{26,18},{4,12},{... | collective-permute-start | bytes 491528 | tf_op jit(solution)/shard_map/ppermute | solution.py:238
  44.5 0.0 collective-permute-done.6.lower
  44.5 1.8 %collective-permute-done.5.upper = f32[5,8,384]{2,1,0:T(8,128)S(1)} collective-permute-done((f32[5,8,384]{2,1,0:T(8,128)S(1)}, f32[5,8,384]{2,1,0:T(8,128)S(1)}, u32[]{:S(2)}, u32[]{:S(2)}) %collective-permute-start.5) | collective-permute-done | bytes 61472 | tf_op jit(solution)/shard_map/ppermute | solution.py:209
  46.3 8.3 %shard_map.71 = (f32[5,224,256]{2,1,0:T(8,128)S(1)}, f32[5,32,256]{2,1,0:T(8,128)S(1)}) custom-call(s32[2]{0:T(128)S(1)} %pad_add_fusion.position, f32[5,5]{1,0:T(8,128)S(1)} %copy-done.3, f32[5,5]{1,0:T(8,128)S(1)} %copy-done.4, f32[5]{0:T(128)S(1)} %copy-done.5, f32[5,256,256]{2,1,0:T(8,128)S(1)} %get-tuple-element.13.cells, f32[5,256,256]{2,1,0:T(8,128)S(1)} %bitcast.16, ...), custom_call_target="tpu_custom_call" | custom-call | tf_op jit(solution)/shard_map/pallas_call | solution.py:217
  54.5 0.7 %collective-permute-start.9 = (f32[5,32,256]{2,1,0:T(8,128)S(1)}, f32[5,32,256]{2,1,0:T(8,128)S(1)}, u32[]{:S(2)}, u32[]{:S(2)}) collective-permute-start(f32[5,32,256]{2,1,0:T(8,128)S(1)} %collective-permute-done.7), channel_id=1, source_target_pairs={{1,9},{9,1},{17,25},{25,17},{3,11},{11,3},{19,27},{27,19},{5,13},{... | collective-permute-start | bytes 491528 | tf_op jit(solution)/shard_map/ppermute | solution.py:238
  55.2 3.2 %collective-permute-done.10.arrived = f32[5,224,256]{2,1,0:T(8,128)S(1)} collective-permute-done((f32[5,224,256]{2,1,0:T(8,128)S(1)}, f32[5,224,256]{2,1,0:T(8,128)S(1)}, u32[]{:S(2)}, u32[]{:S(2)}) %collective-permute-start.10) | collective-permute-done | bytes 1146912 | tf_op jit(solution)/shard_map/ppermute | solution.py:229
  58.4 1.1 %shard_map.72.begun = f32[1,5,256,256]{3,2,1,0:T(8,128)} custom-call(f32[5,224,256]{2,1,0:T(8,128)S(1)} %get-tuple-element.16.adjoint, f32[5,224,256]{2,1,0:T(8,128)S(1)} %collective-permute-done.10.arrived), custom_call_target="tpu_custom_call" | custom-call | tf_op jit(solution)/shard_map/pallas_call | solution.py:173
  59.5 1.2 %collective-permute-done.8.early = f32[5,32,256]{2,1,0:T(8,128)S(1)} collective-permute-done((f32[5,32,256]{2,1,0:T(8,128)S(1)}, f32[5,32,256]{2,1,0:T(8,128)S(1)}, u32[]{:S(2)}, u32[]{:S(2)}) %collective-permute-start.8) | collective-permute-done | bytes 163872 | tf_op jit(solution)/shard_map/ppermute | solution.py:238
  60.7 0.0 collective-permute-done.9.late
  60.7 0.7 %shard_map.73 = f32[1,5,256,256]{3,2,1,0:T(8,128)} custom-call(f32[5,32,256]{2,1,0:T(8,128)S(1)} %get-tuple-element.15.adjoint, f32[5,32,256]{2,1,0:T(8,128)S(1)} %collective-permute-done.8.early, f32[5,32,256]{2,1,0:T(8,128)S(1)} %collective-permute-done.9.late, f32[1,5,256,256]{3,2,1,0:T(8,128)} %shard_map.72.begun), custom_call_target="tpu_custom_call", output_to_operand_aliasing={{}: (3, {})} | custom-call | tf_op jit(solution)/shard_map/pallas_call | solution.py:181
  (8 shorter events, 0.0 us)
Async XLA Ops:
  0.6 13.6 %copy-start.5 = (f32[5]{0:T(128)S(1)}, f32[5]{0:T(128)}, u32[]{:S(2)}) copy-start(f32[5]{0:T(128)} %viscous.3) | copy-start | bytes 64
  0.6 33.5 %collective-permute-start.3 = (f32[5,256,256]{2,1,0:T(8,128)}, f32[5,256,256]{2,1,0:T(8,128)S(1)}, u32[]{:S(2)}, u32[]{:S(2)}) collective-permute-start(f32[5,256,256]{2,1,0:T(8,128)} %bitcast.12), channel_id=1, source_target_pairs={{0,24},{8,0},{16,8},{24,16},{1,25},{9,1},{17,9},{25,17},{2,26},{10... | collective-permute-start | bytes 3932168 | tf_op jit(solution)/shard_map/ppermute | solution.py:229
  4.6 1.4 %copy-start = (f32[1,5,256,256]{3,2,1,0:T(8,128)S(1)}, f32[1,5,256,256]{3,2,1,0:T(8,128)}, u32[]{:S(2)}) copy-start(f32[1,5,256,256]{3,2,1,0:T(8,128)} %param.5) | copy-start | bytes 3932164
  5.9 8.3 %copy-start.1 = (f32[1,5,256,256]{3,2,1,0:T(8,128)S(1)}, f32[1,5,256,256]{3,2,1,0:T(8,128)}, u32[]{:S(2)}) copy-start(f32[1,5,256,256]{3,2,1,0:T(8,128)} %param.5) | copy-start | bytes 3932164
  5.9 8.3 %copy-start.3 = (f32[5,5]{1,0:T(8,128)S(1)}, f32[5,5]{1,0:T(8,128)}, u32[]{:S(2)}) copy-start(f32[5,5]{1,0:T(8,128)} %mat_pitch.3) | copy-start | bytes 304
  5.9 8.3 %copy-start.4 = (f32[5,5]{1,0:T(8,128)S(1)}, f32[5,5]{1,0:T(8,128)}, u32[]{:S(2)}) copy-start(f32[5,5]{1,0:T(8,128)} %mat_span.3) | copy-start | bytes 304
  6.2 1.2 %collective-permute-start = (f32[24,256]{1,0:T(8,128)S(1)}, f32[24,256]{1,0:T(8,128)S(1)}, u32[]{:S(2)}, u32[]{:S(2)}) collective-permute-start(f32[24,256]{1,0:T(8,128)S(1)} %shard_map.68), channel_id=1, source_target_pairs={{0,1},{1,0},{2,3},{3,2},{4,5},{5,4},{6,7},{7,6},{8,9},{9,8},{10,11... | collective-permute-start | bytes 73736 | tf_op jit(solution)/shard_map/ppermute | solution.py:196
  7.5 6.2 %collective-permute-start.1 = (f32[5,8,384]{2,1,0:T(8,128)S(1)}, f32[5,8,384]{2,1,0:T(8,128)S(1)}, u32[]{:S(2)}, u32[]{:S(2)}) collective-permute-start(f32[5,8,384]{2,1,0:T(8,128)S(1)} %select_maximum_fusion.3), channel_id=1, source_target_pairs={{0,2},{2,4},{4,6},{6,0},{1,3},{3,5},{5,7},{7,1},{8,10},{10,12},{12... | collective-permute-start | bytes 184328 | tf_op jit(solution)/shard_map/ppermute | solution.py:209
  9.1 5.1 %collective-permute-start.2 = (f32[5,8,384]{2,1,0:T(8,128)S(1)}, f32[5,8,384]{2,1,0:T(8,128)S(1)}, u32[]{:S(2)}, u32[]{:S(2)}) collective-permute-start(f32[5,8,384]{2,1,0:T(8,128)S(1)} %select_maximum_fusion.2), channel_id=1, source_target_pairs={{2,0},{4,2},{6,4},{0,6},{3,1},{5,3},{7,5},{1,7},{10,8},{12,10},{14... | collective-permute-start | bytes 184328 | tf_op jit(solution)/shard_map/ppermute | solution.py:210
  14.2 1.3 %copy-start.2 = (f32[1,5,256,256]{3,2,1,0:T(8,128)S(1)}, f32[1,5,256,256]{3,2,1,0:T(8,128)}, u32[]{:S(2)}) copy-start(f32[1,5,256,256]{3,2,1,0:T(8,128)} %param.6) | copy-start | bytes 3932164
  23.9 34.5 %collective-permute-start.10 = (f32[5,224,256]{2,1,0:T(8,128)S(1)}, f32[5,224,256]{2,1,0:T(8,128)S(1)}, u32[]{:S(2)}, u32[]{:S(2)}) collective-permute-start(f32[5,224,256]{2,1,0:T(8,128)S(1)} %get-tuple-element.10.lead), channel_id=1, source_target_pairs={{0,8},{8,16},{16,24},{24,0},{1,9},{9,17},{17,25},{25,1},{2,10},{10... | collective-permute-start | bytes 3440648 | tf_op jit(solution)/shard_map/ppermute | solution.py:229
  23.9 16.3 %collective-permute-start.7 = (f32[5,32,256]{2,1,0:T(8,128)S(1)}, f32[5,32,256]{2,1,0:T(8,128)S(1)}, u32[]{:S(2)}, u32[]{:S(2)}) collective-permute-start(f32[5,32,256]{2,1,0:T(8,128)S(1)} %get-tuple-element.11.last), channel_id=1, source_target_pairs={{0,0},{8,24},{16,16},{24,8},{1,1},{9,25},{17,17},{25,9},{2,2},{10,... | collective-permute-start | bytes 491528 | tf_op jit(solution)/shard_map/ppermute | solution.py:234
  35.4 1.2 %collective-permute-start.4 = (f32[24,256]{1,0:T(8,128)S(1)}, f32[24,256]{1,0:T(8,128)S(1)}, u32[]{:S(2)}, u32[]{:S(2)}) collective-permute-start(f32[24,256]{1,0:T(8,128)S(1)} %get-tuple-element.14), channel_id=1, source_target_pairs={{0,1},{1,0},{2,3},{3,2},{4,5},{5,4},{6,7},{7,6},{8,9},{9,8},{10,11... | collective-permute-start | bytes 73736 | tf_op jit(solution)/shard_map/ppermute | solution.py:196
  36.6 7.9 %collective-permute-start.6 = (f32[5,8,384]{2,1,0:T(8,128)S(1)}, f32[5,8,384]{2,1,0:T(8,128)S(1)}, u32[]{:S(2)}, u32[]{:S(2)}) collective-permute-start(f32[5,8,384]{2,1,0:T(8,128)S(1)} %select_maximum_fusion), channel_id=1, source_target_pairs={{2,0},{4,2},{6,4},{0,6},{3,1},{5,3},{7,5},{1,7},{10,8},{12,10},{14... | collective-permute-start | bytes 184328 | tf_op jit(solution)/shard_map/ppermute | solution.py:210
  40.2 6.0 %collective-permute-start.5 = (f32[5,8,384]{2,1,0:T(8,128)S(1)}, f32[5,8,384]{2,1,0:T(8,128)S(1)}, u32[]{:S(2)}, u32[]{:S(2)}) collective-permute-start(f32[5,8,384]{2,1,0:T(8,128)S(1)} %select_maximum_fusion.1), channel_id=1, source_target_pairs={{0,2},{2,4},{4,6},{6,0},{1,3},{3,5},{5,7},{7,1},{8,10},{10,12},{12... | collective-permute-start | bytes 184328 | tf_op jit(solution)/shard_map/ppermute | solution.py:209
  40.3 20.5 %collective-permute-start.8 = (f32[5,32,256]{2,1,0:T(8,128)S(1)}, f32[5,32,256]{2,1,0:T(8,128)S(1)}, u32[]{:S(2)}, u32[]{:S(2)}) collective-permute-start(f32[5,32,256]{2,1,0:T(8,128)S(1)} %collective-permute-done.7), channel_id=1, source_target_pairs={{0,8},{8,0},{16,24},{24,16},{2,10},{10,2},{18,26},{26,18},{4,12},{... | collective-permute-start | bytes 491528 | tf_op jit(solution)/shard_map/ppermute | solution.py:238
  54.5 6.2 %collective-permute-start.9 = (f32[5,32,256]{2,1,0:T(8,128)S(1)}, f32[5,32,256]{2,1,0:T(8,128)S(1)}, u32[]{:S(2)}, u32[]{:S(2)}) collective-permute-start(f32[5,32,256]{2,1,0:T(8,128)S(1)} %collective-permute-done.7), channel_id=1, source_target_pairs={{1,9},{9,1},{17,25},{25,17},{3,11},{11,3},{19,27},{27,19},{5,13},{... | collective-permute-start | bytes 491528 | tf_op jit(solution)/shard_map/ppermute | solution.py:238

commit v6 on v5

--- a/solution.py
+++ b/solution.py
@@ -13,7 +13,7 @@
 LANES = 128
 STRIP = 24
 MARGIN = 2 * TILE
-LAST = 32
+LAST = 40
 VMEM_LIMIT = 32 * 1024 * 1024
 
 
@@ -122,16 +122,20 @@
 
     begin = lead.shape[1]
     bounds = [MARGIN // TILE, (MARGIN + begin) // TILE, (MARGIN + rows) // TILE]
-    lax.fori_loop(bounds[0], bounds[1], functools.partial(step_two, lead, 0), 0, unroll=7)
-    lax.fori_loop(bounds[1], bounds[2], functools.partial(step_two, last, begin), 0, unroll=4)
+    lax.fori_loop(bounds[0], bounds[1], functools.partial(step_two, lead, 0), 0, unroll=9)
+    lax.fori_loop(bounds[1], bounds[2], functools.partial(step_two, last, begin), 0, unroll=last.shape[1] // TILE)
 
 
 def lead_kernel(adjoint, arrived, gradient):
     gradient[0] = adjoint[...] - arrived[...]
 
 
-def last_kernel(adjoint, early, late, begun, gradient):
-    gradient[0] = adjoint[...] - (early[...] + late[...])
+def last_kernel(adjoint, early, late, begun, gradient, staged, done):
+    staged[...] = adjoint[...] - (early[...] + late[...])
+    rows = staged.shape[1]
+    copy = pltpu.make_async_copy(staged, gradient.at[0, :, pl.ds(gradient.shape[2] - rows, rows)], done)
+    copy.start()
+    copy.wait()
 
 
 def in_vmem(count):
@@ -180,10 +184,10 @@
     )(adjoint[0], arrived[0])
     return pl.pallas_call(
         last_kernel,
-        grid=(1,),
         out_shape=whole,
         in_specs=in_vmem(3) + [pl.BlockSpec(memory_space=pl.ANY)],
-        out_specs=pl.BlockSpec((1, fields, rest, cols), lambda f: (0, 0, begin // rest, 0)),
+        out_specs=pl.BlockSpec(memory_space=pl.ANY),
+        scratch_shapes=[pltpu.VMEM((fields, rest, cols), jnp.float32), pltpu.SemaphoreType.DMA],
         input_output_aliases={3: 0},
         compiler_params=PARAMS,
     )(adjoint[1], *arrived[1], begun)

time: 61.7 us -> 61.6 us (level); the launches traced: 61.4 us -> 60.6 us
  waiting for transfers between devices: 20.8 us -> 20 us
    ppermute x2, waiting for transfers between devices: 12.7 us -> 11.8 us  [passed_along(): lax.ppermute(shard, 'seg', [(i, (i + by) % count) for i in range(count)])]
  transfers between devices with their start and end apart: 11 -> 11, of which waited for: 8 -> 8; matrix products, arithmetic and copies ran while one was open for 0% -> 0% of each run, Pallas kernels for 31% -> 32%
where the time goes in v6:
time: 61.6 us; the launch traced here: 60.6 us
  waiting for transfers between devices  20 us (32%)
  Pallas kernels  19.9 us (32%)
  starting transfers between devices  17.2 us (28%)
  local copies, waits for them, and re-layouts  2.7 us (4%)
  between operations  0.75 us (1%)
    pallas_call x2, Pallas kernels, propagated(): pl.pallas_call(functools.partial(propagate_kernel, transposed, sign, scal...  16.6 us
    ppermute x2, waiting for transfers between devices, passed_along(): lax.ppermute(shard, 'seg', [(i, (i + by) % count) for i in range(count)])  11.8 us
    ppermute x2, starting transfers between devices, exchanged(): lax.ppermute(outer(0, 0), 'pitch', [((i + 1) % ring, i) for i in range(ri...  5.9 us
    ppermute x2, starting transfers between devices, swapped(): return lax.ppermute(cells, ('seg', 'span'), pairs)  4.9 us
    ppermute x2, starting transfers between devices, passed_along(): lax.ppermute(shard, 'seg', [(i, (i + by) % count) for i in range(count)])  4 us
    ppermute x2, waiting for transfers between devices, exchanged(): lax.ppermute(outer(rows - TILE, rows - LANES), 'pitch', [(i, (i + 1) % ri...  3.96 us
    unnamed x12, local copies, waits for them, and re-layouts  2.68 us
    ppermute x2, waiting for transfers between devices, exchanged(): sides = lax.ppermute(strip, 'span', [(0, 1), (1, 0)])  2.35 us
  transfers between devices with their start and end apart: 11, of which 8 were waited for; matrix products, arithmetic and copies ran while one was open for 0% of the time, Pallas kernels for 32%

profile of v6, /device:TPU:0, one launch (start us, length us, event | category | flops | bytes accessed | tf_op | source)
XLA Modules:
  0.0 60.6 jit_solution(11301219094023973977)
XLA Ops:
  0.6 0.0 copy-start.5
  0.6 3.9 %collective-permute-start.3 = (f32[5,256,256]{2,1,0:T(8,128)}, f32[5,256,256]{2,1,0:T(8,128)S(1)}, u32[]{:S(2)}, u32[]{:S(2)}) collective-permute-start(f32[5,256,256]{2,1,0:T(8,128)} %bitcast.12), channel_id=1, source_target_pairs={{0,24},{8,0},{16,8},{24,16},{1,25},{9,1},{17,9},{25,17},{2,26},{10... | collective-permute-start | bytes 3932168 | tf_op jit(solution)/shard_map/ppermute | solution.py:233
  4.6 0.0 copy-start
  4.6 1.3 %copy-done = f32[1,5,256,256]{3,2,1,0:T(8,128)S(1)} copy-done((f32[1,5,256,256]{3,2,1,0:T(8,128)S(1)}, f32[1,5,256,256]{3,2,1,0:T(8,128)}, u32[]{:S(2)}) %copy-start) | copy-done | bytes 1310744
  5.9 0.0 copy-start.1
  5.9 0.0 copy-start.3
  5.9 0.0 copy-start.4
  5.9 0.3 shard_map.68
  6.2 0.0 collective-permute-start
  6.3 1.2 %collective-permute-done.strip = f32[24,256]{1,0:T(8,128)S(1)} collective-permute-done((f32[24,256]{1,0:T(8,128)S(1)}, f32[24,256]{1,0:T(8,128)S(1)}, u32[]{:S(2)}, u32[]{:S(2)}) %collective-permute-start) | collective-permute-done | bytes 24608 | tf_op jit(solution)/shard_map/ppermute | solution.py:200
  7.5 1.6 %collective-permute-start.1 = (f32[5,8,384]{2,1,0:T(8,128)S(1)}, f32[5,8,384]{2,1,0:T(8,128)S(1)}, u32[]{:S(2)}, u32[]{:S(2)}) collective-permute-start(f32[5,8,384]{2,1,0:T(8,128)S(1)} %select_maximum_fusion.3), channel_id=1, source_target_pairs={{0,2},{2,4},{4,6},{6,0},{1,3},{3,5},{5,7},{7,1},{8,10},{10,12},{12... | collective-permute-start | bytes 184328 | tf_op jit(solution)/shard_map/ppermute | solution.py:213
  9.1 2.2 %collective-permute-start.2 = (f32[5,8,384]{2,1,0:T(8,128)S(1)}, f32[5,8,384]{2,1,0:T(8,128)S(1)}, u32[]{:S(2)}, u32[]{:S(2)}) collective-permute-start(f32[5,8,384]{2,1,0:T(8,128)S(1)} %select_maximum_fusion.2), channel_id=1, source_target_pairs={{2,0},{4,2},{6,4},{0,6},{3,1},{5,3},{7,5},{1,7},{10,8},{12,10},{14... | collective-permute-start | bytes 184328 | tf_op jit(solution)/shard_map/ppermute | solution.py:214
  11.3 0.1 pad_add_fusion.position
  11.4 2.2 %collective-permute-done.1.upper = f32[5,8,384]{2,1,0:T(8,128)S(1)} collective-permute-done((f32[5,8,384]{2,1,0:T(8,128)S(1)}, f32[5,8,384]{2,1,0:T(8,128)S(1)}, u32[]{:S(2)}, u32[]{:S(2)}) %collective-permute-start.1) | collective-permute-done | bytes 61472 | tf_op jit(solution)/shard_map/ppermute | solution.py:213
  13.6 0.6 collective-permute-done.2.lower
  14.2 0.0 copy-done.5
  14.2 0.0 copy-done.1
  14.2 0.0 copy-done.3
  14.2 0.0 copy-done.4
  14.2 0.0 copy-start.2
  14.2 1.3 %copy-done.2 = f32[1,5,256,256]{3,2,1,0:T(8,128)S(1)} copy-done((f32[1,5,256,256]{3,2,1,0:T(8,128)S(1)}, f32[1,5,256,256]{3,2,1,0:T(8,128)}, u32[]{:S(2)}) %copy-start.2) | copy-done | bytes 1310744
  15.6 8.3 %shard_map.69 = (f32[5,216,256]{2,1,0:T(8,128)S(1)}, f32[5,40,256]{2,1,0:T(8,128)S(1)}) custom-call(s32[2]{0:T(128)S(1)} %pad_add_fusion.position, f32[5,5]{1,0:T(8,128)S(1)} %copy-done.3, f32[5,5]{1,0:T(8,128)S(1)} %copy-done.4, f32[5]{0:T(128)S(1)} %copy-done.5, f32[5,256,256]{2,1,0:T(8,128)S(1)} %bitcast.15, f32[5,256,256]{2,1,0:T(8,128)S(1)} %bitcast.17, ...), custom_call_target="tpu_custom_call" | custom-call | tf_op jit(solution)/shard_map/pallas_call | solution.py:221
  23.9 0.1 collective-permute-start.10
  23.9 0.7 %collective-permute-start.7 = (f32[5,40,256]{2,1,0:T(8,128)S(1)}, f32[5,40,256]{2,1,0:T(8,128)S(1)}, u32[]{:S(2)}, u32[]{:S(2)}) collective-permute-start(f32[5,40,256]{2,1,0:T(8,128)S(1)} %get-tuple-element.11.last), channel_id=1, source_target_pairs={{0,0},{8,24},{16,16},{24,8},{1,1},{9,25},{17,17},{25,9},{2,2},{10,... | collective-permute-start | bytes 614408 | tf_op jit(solution)/shard_map/ppermute | solution.py:238
  24.6 9.5 %collective-permute-done.3.following = f32[5,256,256]{2,1,0:T(8,128)S(1)} collective-permute-done((f32[5,256,256]{2,1,0:T(8,128)}, f32[5,256,256]{2,1,0:T(8,128)S(1)}, u32[]{:S(2)}, u32[]{:S(2)}) %collective-permute-start.3) | collective-permute-done | bytes 1310752 | tf_op jit(solution)/shard_map/ppermute | solution.py:233
  34.1 1.3 %shard_map.70 = (f32[5,256,256]{2,1,0:T(8,128)}, f32[5,256,256]{2,1,0:T(8,128)S(1)}, f32[24,256]{1,0:T(8,128)S(1)}) custom-call(f32[5,216,256]{2,1,0:T(8,128)S(1)} %get-tuple-element.10.lead, f32[5,40,256]{2,1,0:T(8,128)S(1)} %get-tuple-element.11.last, f32[5,256,256]{2,1,0:T(8,128)S(1)} %collective-permute-done.3.following), custom_call_target="tpu_custom_call" | custom-call | tf_op jit(solution)/shard_map/pallas_call | solution.py:164
  35.4 0.0 collective-permute-start.4
  35.4 1.2 %collective-permute-done.4.strip = f32[24,256]{1,0:T(8,128)S(1)} collective-permute-done((f32[24,256]{1,0:T(8,128)S(1)}, f32[24,256]{1,0:T(8,128)S(1)}, u32[]{:S(2)}, u32[]{:S(2)}) %collective-permute-start.4) | collective-permute-done | bytes 24608 | tf_op jit(solution)/shard_map/ppermute | solution.py:200
  36.6 3.7 %collective-permute-start.6 = (f32[5,8,384]{2,1,0:T(8,128)S(1)}, f32[5,8,384]{2,1,0:T(8,128)S(1)}, u32[]{:S(2)}, u32[]{:S(2)}) collective-permute-start(f32[5,8,384]{2,1,0:T(8,128)S(1)} %select_maximum_fusion), channel_id=1, source_target_pairs={{2,0},{4,2},{6,4},{0,6},{3,1},{5,3},{7,5},{1,7},{10,8},{12,10},{14... | collective-permute-start | bytes 184328 | tf_op jit(solution)/shard_map/ppermute | solution.py:214
  40.3 0.0 collective-permute-start.5
  40.3 0.0 collective-permute-done.7
  40.3 4.2 %collective-permute-start.8 = (f32[5,40,256]{2,1,0:T(8,128)S(1)}, f32[5,40,256]{2,1,0:T(8,128)S(1)}, u32[]{:S(2)}, u32[]{:S(2)}) collective-permute-start(f32[5,40,256]{2,1,0:T(8,128)S(1)} %collective-permute-done.7), channel_id=1, source_target_pairs={{0,8},{8,0},{16,24},{24,16},{2,10},{10,2},{18,26},{26,18},{4,12},{... | collective-permute-start | bytes 614408 | tf_op jit(solution)/shard_map/ppermute | solution.py:242
  44.5 0.0 collective-permute-done.6.lower
  44.5 1.8 %collective-permute-done.5.upper = f32[5,8,384]{2,1,0:T(8,128)S(1)} collective-permute-done((f32[5,8,384]{2,1,0:T(8,128)S(1)}, f32[5,8,384]{2,1,0:T(8,128)S(1)}, u32[]{:S(2)}, u32[]{:S(2)}) %collective-permute-start.5) | collective-permute-done | bytes 61472 | tf_op jit(solution)/shard_map/ppermute | solution.py:213
  46.3 8.2 %shard_map.71 = (f32[5,216,256]{2,1,0:T(8,128)S(1)}, f32[5,40,256]{2,1,0:T(8,128)S(1)}) custom-call(s32[2]{0:T(128)S(1)} %pad_add_fusion.position, f32[5,5]{1,0:T(8,128)S(1)} %copy-done.3, f32[5,5]{1,0:T(8,128)S(1)} %copy-done.4, f32[5]{0:T(128)S(1)} %copy-done.5, f32[5,256,256]{2,1,0:T(8,128)S(1)} %get-tuple-element.13.cells, f32[5,256,256]{2,1,0:T(8,128)S(1)} %bitcast.16, ...), custom_call_target="tpu_custom_call" | custom-call | tf_op jit(solution)/shard_map/pallas_call | solution.py:221
  54.5 0.7 %collective-permute-start.9 = (f32[5,40,256]{2,1,0:T(8,128)S(1)}, f32[5,40,256]{2,1,0:T(8,128)S(1)}, u32[]{:S(2)}, u32[]{:S(2)}) collective-permute-start(f32[5,40,256]{2,1,0:T(8,128)S(1)} %collective-permute-done.7), channel_id=1, source_target_pairs={{1,9},{9,1},{17,25},{25,17},{3,11},{11,3},{19,27},{27,19},{5,13},{... | collective-permute-start | bytes 614408 | tf_op jit(solution)/shard_map/ppermute | solution.py:242
  55.2 2.3 %collective-permute-done.10.arrived = f32[5,216,256]{2,1,0:T(8,128)S(1)} collective-permute-done((f32[5,216,256]{2,1,0:T(8,128)S(1)}, f32[5,216,256]{2,1,0:T(8,128)S(1)}, u32[]{:S(2)}, u32[]{:S(2)}) %collective-permute-start.10) | collective-permute-done | bytes 1105952 | tf_op jit(solution)/shard_map/ppermute | solution.py:233
  57.5 1.1 %shard_map.72.begun = f32[1,5,256,256]{3,2,1,0:T(8,128)} custom-call(f32[5,216,256]{2,1,0:T(8,128)S(1)} %get-tuple-element.16.adjoint, f32[5,216,256]{2,1,0:T(8,128)S(1)} %collective-permute-done.10.arrived), custom_call_target="tpu_custom_call" | custom-call | tf_op jit(solution)/shard_map/pallas_call | solution.py:177
  58.6 1.3 %collective-permute-done.8.early = f32[5,40,256]{2,1,0:T(8,128)S(1)} collective-permute-done((f32[5,40,256]{2,1,0:T(8,128)S(1)}, f32[5,40,256]{2,1,0:T(8,128)S(1)}, u32[]{:S(2)}, u32[]{:S(2)}) %collective-permute-start.8) | collective-permute-done | bytes 204832 | tf_op jit(solution)/shard_map/ppermute | solution.py:242
  59.9 0.0 collective-permute-done.9.late
  59.9 0.7 %shard_map.73 = f32[1,5,256,256]{3,2,1,0:T(8,128)} custom-call(f32[5,40,256]{2,1,0:T(8,128)S(1)} %get-tuple-element.15.adjoint, f32[5,40,256]{2,1,0:T(8,128)S(1)} %collective-permute-done.8.early, f32[5,40,256]{2,1,0:T(8,128)S(1)} %collective-permute-done.9.late, f32[1,5,256,256]{3,2,1,0:T(8,128)} %shard_map.72.begun), custom_call_target="tpu_custom_call", output_to_operand_aliasing={{}: (3, {})} | custom-call | tf_op jit(solution)/shard_map/pallas_call | solution.py:185
  (8 shorter events, 0.0 us)
Async XLA Ops:
  0.6 13.6 %copy-start.5 = (f32[5]{0:T(128)S(1)}, f32[5]{0:T(128)}, u32[]{:S(2)}) copy-start(f32[5]{0:T(128)} %viscous.3) | copy-start | bytes 64
  0.6 33.5 %collective-permute-start.3 = (f32[5,256,256]{2,1,0:T(8,128)}, f32[5,256,256]{2,1,0:T(8,128)S(1)}, u32[]{:S(2)}, u32[]{:S(2)}) collective-permute-start(f32[5,256,256]{2,1,0:T(8,128)} %bitcast.12), channel_id=1, source_target_pairs={{0,24},{8,0},{16,8},{24,16},{1,25},{9,1},{17,9},{25,17},{2,26},{10... | collective-permute-start | bytes 3932168 | tf_op jit(solution)/shard_map/ppermute | solution.py:233
  4.6 1.4 %copy-start = (f32[1,5,256,256]{3,2,1,0:T(8,128)S(1)}, f32[1,5,256,256]{3,2,1,0:T(8,128)}, u32[]{:S(2)}) copy-start(f32[1,5,256,256]{3,2,1,0:T(8,128)} %param.5) | copy-start | bytes 3932164
  5.9 8.3 %copy-start.1 = (f32[1,5,256,256]{3,2,1,0:T(8,128)S(1)}, f32[1,5,256,256]{3,2,1,0:T(8,128)}, u32[]{:S(2)}) copy-start(f32[1,5,256,256]{3,2,1,0:T(8,128)} %param.5) | copy-start | bytes 3932164
  5.9 8.3 %copy-start.3 = (f32[5,5]{1,0:T(8,128)S(1)}, f32[5,5]{1,0:T(8,128)}, u32[]{:S(2)}) copy-start(f32[5,5]{1,0:T(8,128)} %mat_pitch.3) | copy-start | bytes 304
  5.9 8.3 %copy-start.4 = (f32[5,5]{1,0:T(8,128)S(1)}, f32[5,5]{1,0:T(8,128)}, u32[]{:S(2)}) copy-start(f32[5,5]{1,0:T(8,128)} %mat_span.3) | copy-start | bytes 304
  6.2 1.2 %collective-permute-start = (f32[24,256]{1,0:T(8,128)S(1)}, f32[24,256]{1,0:T(8,128)S(1)}, u32[]{:S(2)}, u32[]{:S(2)}) collective-permute-start(f32[24,256]{1,0:T(8,128)S(1)} %shard_map.68), channel_id=1, source_target_pairs={{0,1},{1,0},{2,3},{3,2},{4,5},{5,4},{6,7},{7,6},{8,9},{9,8},{10,11... | collective-permute-start | bytes 73736 | tf_op jit(solution)/shard_map/ppermute | solution.py:200
  7.5 6.2 %collective-permute-start.1 = (f32[5,8,384]{2,1,0:T(8,128)S(1)}, f32[5,8,384]{2,1,0:T(8,128)S(1)}, u32[]{:S(2)}, u32[]{:S(2)}) collective-permute-start(f32[5,8,384]{2,1,0:T(8,128)S(1)} %select_maximum_fusion.3), channel_id=1, source_target_pairs={{0,2},{2,4},{4,6},{6,0},{1,3},{3,5},{5,7},{7,1},{8,10},{10,12},{12... | collective-permute-start | bytes 184328 | tf_op jit(solution)/shard_map/ppermute | solution.py:213
  9.1 5.1 %collective-permute-start.2 = (f32[5,8,384]{2,1,0:T(8,128)S(1)}, f32[5,8,384]{2,1,0:T(8,128)S(1)}, u32[]{:S(2)}, u32[]{:S(2)}) collective-permute-start(f32[5,8,384]{2,1,0:T(8,128)S(1)} %select_maximum_fusion.2), channel_id=1, source_target_pairs={{2,0},{4,2},{6,4},{0,6},{3,1},{5,3},{7,5},{1,7},{10,8},{12,10},{14... | collective-permute-start | bytes 184328 | tf_op jit(solution)/shard_map/ppermute | solution.py:214
  14.2 1.3 %copy-start.2 = (f32[1,5,256,256]{3,2,1,0:T(8,128)S(1)}, f32[1,5,256,256]{3,2,1,0:T(8,128)}, u32[]{:S(2)}) copy-start(f32[1,5,256,256]{3,2,1,0:T(8,128)} %param.6) | copy-start | bytes 3932164
  23.9 33.7 %collective-permute-start.10 = (f32[5,216,256]{2,1,0:T(8,128)S(1)}, f32[5,216,256]{2,1,0:T(8,128)S(1)}, u32[]{:S(2)}, u32[]{:S(2)}) collective-permute-start(f32[5,216,256]{2,1,0:T(8,128)S(1)} %get-tuple-element.10.lead), channel_id=1, source_target_pairs={{0,8},{8,16},{16,24},{24,0},{1,9},{9,17},{17,25},{25,1},{2,10},{10... | collective-permute-start | bytes 3317768 | tf_op jit(solution)/shard_map/ppermute | solution.py:233
  23.9 16.3 %collective-permute-start.7 = (f32[5,40,256]{2,1,0:T(8,128)S(1)}, f32[5,40,256]{2,1,0:T(8,128)S(1)}, u32[]{:S(2)}, u32[]{:S(2)}) collective-permute-start(f32[5,40,256]{2,1,0:T(8,128)S(1)} %get-tuple-element.11.last), channel_id=1, source_target_pairs={{0,0},{8,24},{16,16},{24,8},{1,1},{9,25},{17,17},{25,9},{2,2},{10,... | collective-permute-start | bytes 614408 | tf_op jit(solution)/shard_map/ppermute | solution.py:238
  35.4 1.2 %collective-permute-start.4 = (f32[24,256]{1,0:T(8,128)S(1)}, f32[24,256]{1,0:T(8,128)S(1)}, u32[]{:S(2)}, u32[]{:S(2)}) collective-permute-start(f32[24,256]{1,0:T(8,128)S(1)} %get-tuple-element.14), channel_id=1, source_target_pairs={{0,1},{1,0},{2,3},{3,2},{4,5},{5,4},{6,7},{7,6},{8,9},{9,8},{10,11... | collective-permute-start | bytes 73736 | tf_op jit(solution)/shard_map/ppermute | solution.py:200
  36.6 7.9 %collective-permute-start.6 = (f32[5,8,384]{2,1,0:T(8,128)S(1)}, f32[5,8,384]{2,1,0:T(8,128)S(1)}, u32[]{:S(2)}, u32[]{:S(2)}) collective-permute-start(f32[5,8,384]{2,1,0:T(8,128)S(1)} %select_maximum_fusion), channel_id=1, source_target_pairs={{2,0},{4,2},{6,4},{0,6},{3,1},{5,3},{7,5},{1,7},{10,8},{12,10},{14... | collective-permute-start | bytes 184328 | tf_op jit(solution)/shard_map/ppermute | solution.py:214
  40.3 6.0 %collective-permute-start.5 = (f32[5,8,384]{2,1,0:T(8,128)S(1)}, f32[5,8,384]{2,1,0:T(8,128)S(1)}, u32[]{:S(2)}, u32[]{:S(2)}) collective-permute-start(f32[5,8,384]{2,1,0:T(8,128)S(1)} %select_maximum_fusion.1), channel_id=1, source_target_pairs={{0,2},{2,4},{4,6},{6,0},{1,3},{3,5},{5,7},{7,1},{8,10},{10,12},{12... | collective-permute-start | bytes 184328 | tf_op jit(solution)/shard_map/ppermute | solution.py:213
  40.3 19.6 %collective-permute-start.8 = (f32[5,40,256]{2,1,0:T(8,128)S(1)}, f32[5,40,256]{2,1,0:T(8,128)S(1)}, u32[]{:S(2)}, u32[]{:S(2)}) collective-permute-start(f32[5,40,256]{2,1,0:T(8,128)S(1)} %collective-permute-done.7), channel_id=1, source_target_pairs={{0,8},{8,0},{16,24},{24,16},{2,10},{10,2},{18,26},{26,18},{4,12},{... | collective-permute-start | bytes 614408 | tf_op jit(solution)/shard_map/ppermute | solution.py:242
  54.5 5.4 %collective-permute-start.9 = (f32[5,40,256]{2,1,0:T(8,128)S(1)}, f32[5,40,256]{2,1,0:T(8,128)S(1)}, u32[]{:S(2)}, u32[]{:S(2)}) collective-permute-start(f32[5,40,256]{2,1,0:T(8,128)S(1)} %collective-permute-done.7), channel_id=1, source_target_pairs={{1,9},{9,1},{17,25},{25,17},{3,11},{11,3},{19,27},{27,19},{5,13},{... | collective-permute-start | bytes 614408 | tf_op jit(solution)/shard_map/ppermute | solution.py:242

commit v7 on v6

--- a/solution.py
+++ b/solution.py
@@ -111,7 +111,7 @@
             second[f, pl.ds(pl.multiple_of(tile * TILE, TILE), TILE), cols:] = jnp.where(inside_tile, value[:, cols:], 0.0)
         return carry
 
-    lax.fori_loop(1, (MARGIN + rows) // TILE + 1, step_one, 0, unroll=17)
+    lax.fori_loop(1, (MARGIN + rows) // TILE + 1, step_one, 0, unroll=2)
 
     def step_two(result, base, tile, carry):
         for f, value in enumerate(substep(second, tile, coefficients, cols)):

time: 61.6 us -> 61.6 us (level)
  the two profiles are of different devices: /device:TPU:0 before, /device:TPU:1 now
where the time goes in v7:
time: 61.6 us; the launch traced here: 61.4 us
  Pallas kernels  20.5 us (33%)
  starting transfers between devices  18.9 us (31%)
  waiting for transfers between devices  18.4 us (30%)
  local copies, waits for them, and re-layouts  2.69 us (4%)
  between operations  0.74 us (1%)
    pallas_call x2, Pallas kernels, propagated(): pl.pallas_call(functools.partial(propagate_kernel, transposed, sign, scal...  17.1 us
    ppermute x2, waiting for transfers between devices, passed_along(): lax.ppermute(shard, 'seg', [(i, (i + by) % count) for i in range(count)])  8.54 us
    ppermute x2, starting transfers between devices, exchanged(): lax.ppermute(outer(0, 0), 'pitch', [((i + 1) % ring, i) for i in range(ri...  5.48 us
    ppermute x2, waiting for transfers between devices, exchanged(): lax.ppermute(outer(rows - TILE, rows - LANES), 'pitch', [(i, (i + 1) % ri...  5.14 us
    ppermute x2, starting transfers between devices, swapped(): return lax.ppermute(cells, ('seg', 'span'), pairs)  4.62 us
    ppermute x2, starting transfers between devices, exchanged(): sides = lax.ppermute(strip, 'span', [(0, 1), (1, 0)])  3.68 us
    ppermute x2, starting transfers between devices, passed_along(): lax.ppermute(shard, 'seg', [(i, (i + by) % count) for i in range(count)])  3.11 us
    unnamed x12, local copies, waits for them, and re-layouts  2.68 us
  transfers between devices with their start and end apart: 11, of which 7 were waited for; matrix products, arithmetic and copies ran while one was open for 0% of the time, Pallas kernels for 32%

profile of v7, /device:TPU:1, one launch (start us, length us, event | category | flops | bytes accessed | tf_op | source)
XLA Modules:
  0.0 61.4 jit_solution(16568011098145441162)
XLA Ops:
  0.6 0.0 copy-start.5
  0.6 3.0 %collective-permute-start.3 = (f32[5,256,256]{2,1,0:T(8,128)}, f32[5,256,256]{2,1,0:T(8,128)S(1)}, u32[]{:S(2)}, u32[]{:S(2)}) collective-permute-start(f32[5,256,256]{2,1,0:T(8,128)} %bitcast.12), channel_id=1, source_target_pairs={{0,24},{8,0},{16,8},{24,16},{1,25},{9,1},{17,9},{25,17},{2,26},{10... | collective-permute-start | bytes 3932168 | tf_op jit(solution)/shard_map/ppermute | solution.py:233
  3.7 0.0 copy-start
  3.7 1.3 %copy-done = f32[1,5,256,256]{3,2,1,0:T(8,128)S(1)} copy-done((f32[1,5,256,256]{3,2,1,0:T(8,128)S(1)}, f32[1,5,256,256]{3,2,1,0:T(8,128)}, u32[]{:S(2)}) %copy-start) | copy-done | bytes 1310744
  5.0 0.0 copy-start.1
  5.0 0.0 copy-start.3
  5.0 0.0 copy-start.4
  5.0 0.3 shard_map.68
  5.3 1.0 %collective-permute-start = (f32[24,256]{1,0:T(8,128)S(1)}, f32[24,256]{1,0:T(8,128)S(1)}, u32[]{:S(2)}, u32[]{:S(2)}) collective-permute-start(f32[24,256]{1,0:T(8,128)S(1)} %shard_map.68), channel_id=1, source_target_pairs={{0,1},{1,0},{2,3},{3,2},{4,5},{5,4},{6,7},{7,6},{8,9},{9,8},{10,11... | collective-permute-start | bytes 73736 | tf_op jit(solution)/shard_map/ppermute | solution.py:200
  6.3 0.8 %collective-permute-done.strip = f32[24,256]{1,0:T(8,128)S(1)} collective-permute-done((f32[24,256]{1,0:T(8,128)S(1)}, f32[24,256]{1,0:T(8,128)S(1)}, u32[]{:S(2)}, u32[]{:S(2)}) %collective-permute-start) | collective-permute-done | bytes 24608 | tf_op jit(solution)/shard_map/ppermute | solution.py:200
  7.2 1.3 %collective-permute-start.1 = (f32[5,8,384]{2,1,0:T(8,128)S(1)}, f32[5,8,384]{2,1,0:T(8,128)S(1)}, u32[]{:S(2)}, u32[]{:S(2)}) collective-permute-start(f32[5,8,384]{2,1,0:T(8,128)S(1)} %select_maximum_fusion.3), channel_id=1, source_target_pairs={{0,2},{2,4},{4,6},{6,0},{1,3},{3,5},{5,7},{7,1},{8,10},{10,12},{12... | collective-permute-start | bytes 184328 | tf_op jit(solution)/shard_map/ppermute | solution.py:213
  8.5 2.1 %collective-permute-start.2 = (f32[5,8,384]{2,1,0:T(8,128)S(1)}, f32[5,8,384]{2,1,0:T(8,128)S(1)}, u32[]{:S(2)}, u32[]{:S(2)}) collective-permute-start(f32[5,8,384]{2,1,0:T(8,128)S(1)} %select_maximum_fusion.2), channel_id=1, source_target_pairs={{2,0},{4,2},{6,4},{0,6},{3,1},{5,3},{7,5},{1,7},{10,8},{12,10},{14... | collective-permute-start | bytes 184328 | tf_op jit(solution)/shard_map/ppermute | solution.py:214
  10.6 0.1 pad_add_fusion.position
  10.7 1.6 %collective-permute-done.1.upper = f32[5,8,384]{2,1,0:T(8,128)S(1)} collective-permute-done((f32[5,8,384]{2,1,0:T(8,128)S(1)}, f32[5,8,384]{2,1,0:T(8,128)S(1)}, u32[]{:S(2)}, u32[]{:S(2)}) %collective-permute-start.1) | collective-permute-done | bytes 61472 | tf_op jit(solution)/shard_map/ppermute | solution.py:213
  12.3 0.0 collective-permute-done.2.lower
  12.3 0.0 copy-done.5
  12.3 0.0 copy-done.1
  12.3 0.0 copy-done.3
  12.3 0.0 copy-done.4
  12.3 0.0 copy-start.2
  12.3 1.3 %copy-done.2 = f32[1,5,256,256]{3,2,1,0:T(8,128)S(1)} copy-done((f32[1,5,256,256]{3,2,1,0:T(8,128)S(1)}, f32[1,5,256,256]{3,2,1,0:T(8,128)}, u32[]{:S(2)}) %copy-start.2) | copy-done | bytes 1310744
  13.6 8.6 %shard_map.69 = (f32[5,216,256]{2,1,0:T(8,128)S(1)}, f32[5,40,256]{2,1,0:T(8,128)S(1)}) custom-call(s32[2]{0:T(128)S(1)} %pad_add_fusion.position, f32[5,5]{1,0:T(8,128)S(1)} %copy-done.3, f32[5,5]{1,0:T(8,128)S(1)} %copy-done.4, f32[5]{0:T(128)S(1)} %copy-done.5, f32[5,256,256]{2,1,0:T(8,128)S(1)} %bitcast.15, f32[5,256,256]{2,1,0:T(8,128)S(1)} %bitcast.17, ...), custom_call_target="tpu_custom_call" | custom-call | tf_op jit(solution)/shard_map/pallas_call | solution.py:221
  22.2 0.1 collective-permute-start.10
  22.3 0.7 %collective-permute-start.7 = (f32[5,40,256]{2,1,0:T(8,128)S(1)}, f32[5,40,256]{2,1,0:T(8,128)S(1)}, u32[]{:S(2)}, u32[]{:S(2)}) collective-permute-start(f32[5,40,256]{2,1,0:T(8,128)S(1)} %get-tuple-element.11.last), channel_id=1, source_target_pairs={{0,0},{8,24},{16,16},{24,8},{1,1},{9,25},{17,17},{25,9},{2,2},{10,... | collective-permute-start | bytes 614408 | tf_op jit(solution)/shard_map/ppermute | solution.py:238
  23.0 8.5 %collective-permute-done.3.following = f32[5,256,256]{2,1,0:T(8,128)S(1)} collective-permute-done((f32[5,256,256]{2,1,0:T(8,128)}, f32[5,256,256]{2,1,0:T(8,128)S(1)}, u32[]{:S(2)}, u32[]{:S(2)}) %collective-permute-start.3) | collective-permute-done | bytes 1310752 | tf_op jit(solution)/shard_map/ppermute | solution.py:233
  31.5 1.3 %shard_map.70 = (f32[5,256,256]{2,1,0:T(8,128)}, f32[5,256,256]{2,1,0:T(8,128)S(1)}, f32[24,256]{1,0:T(8,128)S(1)}) custom-call(f32[5,216,256]{2,1,0:T(8,128)S(1)} %get-tuple-element.10.lead, f32[5,40,256]{2,1,0:T(8,128)S(1)} %get-tuple-element.11.last, f32[5,256,256]{2,1,0:T(8,128)S(1)} %collective-permute-done.3.following), custom_call_target="tpu_custom_call" | custom-call | tf_op jit(solution)/shard_map/pallas_call | solution.py:164
  32.7 2.7 %collective-permute-start.4 = (f32[24,256]{1,0:T(8,128)S(1)}, f32[24,256]{1,0:T(8,128)S(1)}, u32[]{:S(2)}, u32[]{:S(2)}) collective-permute-start(f32[24,256]{1,0:T(8,128)S(1)} %get-tuple-element.14), channel_id=1, source_target_pairs={{0,1},{1,0},{2,3},{3,2},{4,5},{5,4},{6,7},{7,6},{8,9},{9,8},{10,11... | collective-permute-start | bytes 73736 | tf_op jit(solution)/shard_map/ppermute | solution.py:200
  35.4 0.8 %collective-permute-done.4.strip = f32[24,256]{1,0:T(8,128)S(1)} collective-permute-done((f32[24,256]{1,0:T(8,128)S(1)}, f32[24,256]{1,0:T(8,128)S(1)}, u32[]{:S(2)}, u32[]{:S(2)}) %collective-permute-start.4) | collective-permute-done | bytes 24608 | tf_op jit(solution)/shard_map/ppermute | solution.py:200
  36.3 3.4 %collective-permute-start.6 = (f32[5,8,384]{2,1,0:T(8,128)S(1)}, f32[5,8,384]{2,1,0:T(8,128)S(1)}, u32[]{:S(2)}, u32[]{:S(2)}) collective-permute-start(f32[5,8,384]{2,1,0:T(8,128)S(1)} %select_maximum_fusion), channel_id=1, source_target_pairs={{2,0},{4,2},{6,4},{0,6},{3,1},{5,3},{7,5},{1,7},{10,8},{12,10},{14... | collective-permute-start | bytes 184328 | tf_op jit(solution)/shard_map/ppermute | solution.py:214
  39.7 0.0 collective-permute-start.5
  39.7 0.0 collective-permute-done.7
  39.7 0.7 %collective-permute-start.8 = (f32[5,40,256]{2,1,0:T(8,128)S(1)}, f32[5,40,256]{2,1,0:T(8,128)S(1)}, u32[]{:S(2)}, u32[]{:S(2)}) collective-permute-start(f32[5,40,256]{2,1,0:T(8,128)S(1)} %collective-permute-done.7), channel_id=1, source_target_pairs={{0,8},{8,0},{16,24},{24,16},{2,10},{10,2},{18,26},{26,18},{4,12},{... | collective-permute-start | bytes 614408 | tf_op jit(solution)/shard_map/ppermute | solution.py:242
  40.4 0.6 collective-permute-done.6.lower
  41.0 3.6 %collective-permute-done.5.upper = f32[5,8,384]{2,1,0:T(8,128)S(1)} collective-permute-done((f32[5,8,384]{2,1,0:T(8,128)S(1)}, f32[5,8,384]{2,1,0:T(8,128)S(1)}, u32[]{:S(2)}, u32[]{:S(2)}) %collective-permute-start.5) | collective-permute-done | bytes 61472 | tf_op jit(solution)/shard_map/ppermute | solution.py:213
  44.6 8.5 %shard_map.71 = (f32[5,216,256]{2,1,0:T(8,128)S(1)}, f32[5,40,256]{2,1,0:T(8,128)S(1)}) custom-call(s32[2]{0:T(128)S(1)} %pad_add_fusion.position, f32[5,5]{1,0:T(8,128)S(1)} %copy-done.3, f32[5,5]{1,0:T(8,128)S(1)} %copy-done.4, f32[5]{0:T(128)S(1)} %copy-done.5, f32[5,256,256]{2,1,0:T(8,128)S(1)} %get-tuple-element.13.cells, f32[5,256,256]{2,1,0:T(8,128)S(1)} %bitcast.16, ...), custom_call_target="tpu_custom_call" | custom-call | tf_op jit(solution)/shard_map/pallas_call | solution.py:221
  53.1 3.9 %collective-permute-start.9 = (f32[5,40,256]{2,1,0:T(8,128)S(1)}, f32[5,40,256]{2,1,0:T(8,128)S(1)}, u32[]{:S(2)}, u32[]{:S(2)}) collective-permute-start(f32[5,40,256]{2,1,0:T(8,128)S(1)} %collective-permute-done.7), channel_id=1, source_target_pairs={{1,9},{9,1},{17,25},{25,17},{3,11},{11,3},{19,27},{27,19},{5,13},{... | collective-permute-start | bytes 614408 | tf_op jit(solution)/shard_map/ppermute | solution.py:242
  57.0 0.0 collective-permute-done.10.arrived
  57.1 1.1 %shard_map.72.begun = f32[1,5,256,256]{3,2,1,0:T(8,128)} custom-call(f32[5,216,256]{2,1,0:T(8,128)S(1)} %get-tuple-element.16.adjoint, f32[5,216,256]{2,1,0:T(8,128)S(1)} %collective-permute-done.10.arrived), custom_call_target="tpu_custom_call" | custom-call | tf_op jit(solution)/shard_map/pallas_call | solution.py:177
  58.2 0.0 collective-permute-done.8.early
  58.2 2.5 %collective-permute-done.9.late = f32[5,40,256]{2,1,0:T(8,128)S(1)} collective-permute-done((f32[5,40,256]{2,1,0:T(8,128)S(1)}, f32[5,40,256]{2,1,0:T(8,128)S(1)}, u32[]{:S(2)}, u32[]{:S(2)}) %collective-permute-start.9) | collective-permute-done | bytes 204832 | tf_op jit(solution)/shard_map/ppermute | solution.py:242
  60.6 0.7 %shard_map.73 = f32[1,5,256,256]{3,2,1,0:T(8,128)} custom-call(f32[5,40,256]{2,1,0:T(8,128)S(1)} %get-tuple-element.15.adjoint, f32[5,40,256]{2,1,0:T(8,128)S(1)} %collective-permute-done.8.early, f32[5,40,256]{2,1,0:T(8,128)S(1)} %collective-permute-done.9.late, f32[1,5,256,256]{3,2,1,0:T(8,128)} %shard_map.72.begun), custom_call_target="tpu_custom_call", output_to_operand_aliasing={{}: (3, {})} | custom-call | tf_op jit(solution)/shard_map/pallas_call | solution.py:185
  (8 shorter events, 0.0 us)
Async XLA Ops:
  0.6 11.6 %copy-start.5 = (f32[5]{0:T(128)S(1)}, f32[5]{0:T(128)}, u32[]{:S(2)}) copy-start(f32[5]{0:T(128)} %viscous.3) | copy-start | bytes 64
  0.6 30.9 %collective-permute-start.3 = (f32[5,256,256]{2,1,0:T(8,128)}, f32[5,256,256]{2,1,0:T(8,128)S(1)}, u32[]{:S(2)}, u32[]{:S(2)}) collective-permute-start(f32[5,256,256]{2,1,0:T(8,128)} %bitcast.12), channel_id=1, source_target_pairs={{0,24},{8,0},{16,8},{24,16},{1,25},{9,1},{17,9},{25,17},{2,26},{10... | collective-permute-start | bytes 3932168 | tf_op jit(solution)/shard_map/ppermute | solution.py:233
  3.7 1.4 %copy-start = (f32[1,5,256,256]{3,2,1,0:T(8,128)S(1)}, f32[1,5,256,256]{3,2,1,0:T(8,128)}, u32[]{:S(2)}) copy-start(f32[1,5,256,256]{3,2,1,0:T(8,128)} %param.5) | copy-start | bytes 3932164
  5.0 7.2 %copy-start.1 = (f32[1,5,256,256]{3,2,1,0:T(8,128)S(1)}, f32[1,5,256,256]{3,2,1,0:T(8,128)}, u32[]{:S(2)}) copy-start(f32[1,5,256,256]{3,2,1,0:T(8,128)} %param.5) | copy-start | bytes 3932164
  5.0 7.2 %copy-start.3 = (f32[5,5]{1,0:T(8,128)S(1)}, f32[5,5]{1,0:T(8,128)}, u32[]{:S(2)}) copy-start(f32[5,5]{1,0:T(8,128)} %mat_pitch.3) | copy-start | bytes 304
  5.0 7.2 %copy-start.4 = (f32[5,5]{1,0:T(8,128)S(1)}, f32[5,5]{1,0:T(8,128)}, u32[]{:S(2)}) copy-start(f32[5,5]{1,0:T(8,128)} %mat_span.3) | copy-start | bytes 304
  5.3 1.8 %collective-permute-start = (f32[24,256]{1,0:T(8,128)S(1)}, f32[24,256]{1,0:T(8,128)S(1)}, u32[]{:S(2)}, u32[]{:S(2)}) collective-permute-start(f32[24,256]{1,0:T(8,128)S(1)} %shard_map.68), channel_id=1, source_target_pairs={{0,1},{1,0},{2,3},{3,2},{4,5},{5,4},{6,7},{7,6},{8,9},{9,8},{10,11... | collective-permute-start | bytes 73736 | tf_op jit(solution)/shard_map/ppermute | solution.py:200
  7.2 5.1 %collective-permute-start.1 = (f32[5,8,384]{2,1,0:T(8,128)S(1)}, f32[5,8,384]{2,1,0:T(8,128)S(1)}, u32[]{:S(2)}, u32[]{:S(2)}) collective-permute-start(f32[5,8,384]{2,1,0:T(8,128)S(1)} %select_maximum_fusion.3), channel_id=1, source_target_pairs={{0,2},{2,4},{4,6},{6,0},{1,3},{3,5},{5,7},{7,1},{8,10},{10,12},{12... | collective-permute-start | bytes 184328 | tf_op jit(solution)/shard_map/ppermute | solution.py:213
  8.5 3.7 %collective-permute-start.2 = (f32[5,8,384]{2,1,0:T(8,128)S(1)}, f32[5,8,384]{2,1,0:T(8,128)S(1)}, u32[]{:S(2)}, u32[]{:S(2)}) collective-permute-start(f32[5,8,384]{2,1,0:T(8,128)S(1)} %select_maximum_fusion.2), channel_id=1, source_target_pairs={{2,0},{4,2},{6,4},{0,6},{3,1},{5,3},{7,5},{1,7},{10,8},{12,10},{14... | collective-permute-start | bytes 184328 | tf_op jit(solution)/shard_map/ppermute | solution.py:214
  12.3 1.3 %copy-start.2 = (f32[1,5,256,256]{3,2,1,0:T(8,128)S(1)}, f32[1,5,256,256]{3,2,1,0:T(8,128)}, u32[]{:S(2)}) copy-start(f32[1,5,256,256]{3,2,1,0:T(8,128)} %param.6) | copy-start | bytes 3932164
  22.2 34.8 %collective-permute-start.10 = (f32[5,216,256]{2,1,0:T(8,128)S(1)}, f32[5,216,256]{2,1,0:T(8,128)S(1)}, u32[]{:S(2)}, u32[]{:S(2)}) collective-permute-start(f32[5,216,256]{2,1,0:T(8,128)S(1)} %get-tuple-element.10.lead), channel_id=1, source_target_pairs={{0,8},{8,16},{16,24},{24,0},{1,9},{9,17},{17,25},{25,1},{2,10},{10... | collective-permute-start | bytes 3317768 | tf_op jit(solution)/shard_map/ppermute | solution.py:233
  22.3 17.4 %collective-permute-start.7 = (f32[5,40,256]{2,1,0:T(8,128)S(1)}, f32[5,40,256]{2,1,0:T(8,128)S(1)}, u32[]{:S(2)}, u32[]{:S(2)}) collective-permute-start(f32[5,40,256]{2,1,0:T(8,128)S(1)} %get-tuple-element.11.last), channel_id=1, source_target_pairs={{0,0},{8,24},{16,16},{24,8},{1,1},{9,25},{17,17},{25,9},{2,2},{10,... | collective-permute-start | bytes 614408 | tf_op jit(solution)/shard_map/ppermute | solution.py:238
  32.7 3.5 %collective-permute-start.4 = (f32[24,256]{1,0:T(8,128)S(1)}, f32[24,256]{1,0:T(8,128)S(1)}, u32[]{:S(2)}, u32[]{:S(2)}) collective-permute-start(f32[24,256]{1,0:T(8,128)S(1)} %get-tuple-element.14), channel_id=1, source_target_pairs={{0,1},{1,0},{2,3},{3,2},{4,5},{5,4},{6,7},{7,6},{8,9},{9,8},{10,11... | collective-permute-start | bytes 73736 | tf_op jit(solution)/shard_map/ppermute | solution.py:200
  36.3 4.7 %collective-permute-start.6 = (f32[5,8,384]{2,1,0:T(8,128)S(1)}, f32[5,8,384]{2,1,0:T(8,128)S(1)}, u32[]{:S(2)}, u32[]{:S(2)}) collective-permute-start(f32[5,8,384]{2,1,0:T(8,128)S(1)} %select_maximum_fusion), channel_id=1, source_target_pairs={{2,0},{4,2},{6,4},{0,6},{3,1},{5,3},{7,5},{1,7},{10,8},{12,10},{14... | collective-permute-start | bytes 184328 | tf_op jit(solution)/shard_map/ppermute | solution.py:214
  39.7 4.9 %collective-permute-start.5 = (f32[5,8,384]{2,1,0:T(8,128)S(1)}, f32[5,8,384]{2,1,0:T(8,128)S(1)}, u32[]{:S(2)}, u32[]{:S(2)}) collective-permute-start(f32[5,8,384]{2,1,0:T(8,128)S(1)} %select_maximum_fusion.1), channel_id=1, source_target_pairs={{0,2},{2,4},{4,6},{6,0},{1,3},{3,5},{5,7},{7,1},{8,10},{10,12},{12... | collective-permute-start | bytes 184328 | tf_op jit(solution)/shard_map/ppermute | solution.py:213
  39.7 18.5 %collective-permute-start.8 = (f32[5,40,256]{2,1,0:T(8,128)S(1)}, f32[5,40,256]{2,1,0:T(8,128)S(1)}, u32[]{:S(2)}, u32[]{:S(2)}) collective-permute-start(f32[5,40,256]{2,1,0:T(8,128)S(1)} %collective-permute-done.7), channel_id=1, source_target_pairs={{0,8},{8,0},{16,24},{24,16},{2,10},{10,2},{18,26},{26,18},{4,12},{... | collective-permute-start | bytes 614408 | tf_op jit(solution)/shard_map/ppermute | solution.py:242
  53.1 7.5 %collective-permute-start.9 = (f32[5,40,256]{2,1,0:T(8,128)S(1)}, f32[5,40,256]{2,1,0:T(8,128)S(1)}, u32[]{:S(2)}, u32[]{:S(2)}) collective-permute-start(f32[5,40,256]{2,1,0:T(8,128)S(1)} %collective-permute-done.7), channel_id=1, source_target_pairs={{1,9},{9,1},{17,25},{25,17},{3,11},{11,3},{19,27},{27,19},{5,13},{... | collective-permute-start | bytes 614408 | tf_op jit(solution)/shard_map/ppermute | solution.py:242

commit v8 on v6

--- a/solution.py
+++ b/solution.py
@@ -13,7 +13,7 @@
 LANES = 128
 STRIP = 24
 MARGIN = 2 * TILE
-LAST = 40
+LAST = 48
 VMEM_LIMIT = 32 * 1024 * 1024
 
 
@@ -122,7 +122,7 @@
 
     begin = lead.shape[1]
     bounds = [MARGIN // TILE, (MARGIN + begin) // TILE, (MARGIN + rows) // TILE]
-    lax.fori_loop(bounds[0], bounds[1], functools.partial(step_two, lead, 0), 0, unroll=9)
+    lax.fori_loop(bounds[0], bounds[1], functools.partial(step_two, lead, 0), 0, unroll=2)
     lax.fori_loop(bounds[1], bounds[2], functools.partial(step_two, last, begin), 0, unroll=last.shape[1] // TILE)
 
 

time: 61.6 us -> 61.6 us (level)
  the two profiles are of different devices: /device:TPU:0 before, /device:TPU:1 now
where the time goes in v8:
time: 61.6 us; the launch traced here: 61.4 us
  Pallas kernels  20.3 us (33%)
  starting transfers between devices  18.9 us (31%)
  waiting for transfers between devices  18.6 us (30%)
  local copies, waits for them, and re-layouts  2.69 us (4%)
  between operations  0.74 us (1%)
    pallas_call x2, Pallas kernels, propagated(): pl.pallas_call(functools.partial(propagate_kernel, transposed, sign, scal...  16.9 us
    ppermute x2, waiting for transfers between devices, passed_along(): lax.ppermute(shard, 'seg', [(i, (i + by) % count) for i in range(count)])  8.62 us
    ppermute x2, starting transfers between devices, exchanged(): lax.ppermute(outer(0, 0), 'pitch', [((i + 1) % ring, i) for i in range(ri...  5.48 us
    ppermute x2, waiting for transfers between devices, exchanged(): lax.ppermute(outer(rows - TILE, rows - LANES), 'pitch', [(i, (i + 1) % ri...  5.14 us
    ppermute x2, starting transfers between devices, swapped(): return lax.ppermute(cells, ('seg', 'span'), pairs)  4.62 us
    ppermute x2, starting transfers between devices, exchanged(): sides = lax.ppermute(strip, 'span', [(0, 1), (1, 0)])  3.68 us
    ppermute x2, starting transfers between devices, passed_along(): lax.ppermute(shard, 'seg', [(i, (i + by) % count) for i in range(count)])  3.11 us
    unnamed x12, local copies, waits for them, and re-layouts  2.68 us
  transfers between devices with their start and end apart: 11, of which 7 were waited for; matrix products, arithmetic and copies ran while one was open for 0% of the time, Pallas kernels for 32%

profile of v8, /device:TPU:1, one launch (start us, length us, event | category | flops | bytes accessed | tf_op | source)
XLA Modules:
  0.0 61.4 jit_solution(10037928417593303704)
XLA Ops:
  0.6 0.0 copy-start.5
  0.6 3.0 %collective-permute-start.3 = (f32[5,256,256]{2,1,0:T(8,128)}, f32[5,256,256]{2,1,0:T(8,128)S(1)}, u32[]{:S(2)}, u32[]{:S(2)}) collective-permute-start(f32[5,256,256]{2,1,0:T(8,128)} %bitcast.12), channel_id=1, source_target_pairs={{0,24},{8,0},{16,8},{24,16},{1,25},{9,1},{17,9},{25,17},{2,26},{10... | collective-permute-start | bytes 3932168 | tf_op jit(solution)/shard_map/ppermute | solution.py:233
  3.7 0.0 copy-start
  3.7 1.3 %copy-done = f32[1,5,256,256]{3,2,1,0:T(8,128)S(1)} copy-done((f32[1,5,256,256]{3,2,1,0:T(8,128)S(1)}, f32[1,5,256,256]{3,2,1,0:T(8,128)}, u32[]{:S(2)}) %copy-start) | copy-done | bytes 1310744
  5.0 0.0 copy-start.1
  5.0 0.0 copy-start.3
  5.0 0.0 copy-start.4
  5.0 0.3 shard_map.68
  5.3 1.0 %collective-permute-start = (f32[24,256]{1,0:T(8,128)S(1)}, f32[24,256]{1,0:T(8,128)S(1)}, u32[]{:S(2)}, u32[]{:S(2)}) collective-permute-start(f32[24,256]{1,0:T(8,128)S(1)} %shard_map.68), channel_id=1, source_target_pairs={{0,1},{1,0},{2,3},{3,2},{4,5},{5,4},{6,7},{7,6},{8,9},{9,8},{10,11... | collective-permute-start | bytes 73736 | tf_op jit(solution)/shard_map/ppermute | solution.py:200
  6.3 0.8 %collective-permute-done.strip = f32[24,256]{1,0:T(8,128)S(1)} collective-permute-done((f32[24,256]{1,0:T(8,128)S(1)}, f32[24,256]{1,0:T(8,128)S(1)}, u32[]{:S(2)}, u32[]{:S(2)}) %collective-permute-start) | collective-permute-done | bytes 24608 | tf_op jit(solution)/shard_map/ppermute | solution.py:200
  7.2 1.3 %collective-permute-start.1 = (f32[5,8,384]{2,1,0:T(8,128)S(1)}, f32[5,8,384]{2,1,0:T(8,128)S(1)}, u32[]{:S(2)}, u32[]{:S(2)}) collective-permute-start(f32[5,8,384]{2,1,0:T(8,128)S(1)} %select_maximum_fusion.3), channel_id=1, source_target_pairs={{0,2},{2,4},{4,6},{6,0},{1,3},{3,5},{5,7},{7,1},{8,10},{10,12},{12... | collective-permute-start | bytes 184328 | tf_op jit(solution)/shard_map/ppermute | solution.py:213
  8.5 2.1 %collective-permute-start.2 = (f32[5,8,384]{2,1,0:T(8,128)S(1)}, f32[5,8,384]{2,1,0:T(8,128)S(1)}, u32[]{:S(2)}, u32[]{:S(2)}) collective-permute-start(f32[5,8,384]{2,1,0:T(8,128)S(1)} %select_maximum_fusion.2), channel_id=1, source_target_pairs={{2,0},{4,2},{6,4},{0,6},{3,1},{5,3},{7,5},{1,7},{10,8},{12,10},{14... | collective-permute-start | bytes 184328 | tf_op jit(solution)/shard_map/ppermute | solution.py:214
  10.6 0.1 pad_add_fusion.position
  10.7 1.6 %collective-permute-done.1.upper = f32[5,8,384]{2,1,0:T(8,128)S(1)} collective-permute-done((f32[5,8,384]{2,1,0:T(8,128)S(1)}, f32[5,8,384]{2,1,0:T(8,128)S(1)}, u32[]{:S(2)}, u32[]{:S(2)}) %collective-permute-start.1) | collective-permute-done | bytes 61472 | tf_op jit(solution)/shard_map/ppermute | solution.py:213
  12.3 0.0 collective-permute-done.2.lower
  12.3 0.0 copy-done.5
  12.3 0.0 copy-done.1
  12.3 0.0 copy-done.3
  12.3 0.0 copy-done.4
  12.3 0.0 copy-start.2
  12.3 1.3 %copy-done.2 = f32[1,5,256,256]{3,2,1,0:T(8,128)S(1)} copy-done((f32[1,5,256,256]{3,2,1,0:T(8,128)S(1)}, f32[1,5,256,256]{3,2,1,0:T(8,128)}, u32[]{:S(2)}) %copy-start.2) | copy-done | bytes 1310744
  13.6 8.5 %shard_map.69 = (f32[5,208,256]{2,1,0:T(8,128)S(1)}, f32[5,48,256]{2,1,0:T(8,128)S(1)}) custom-call(s32[2]{0:T(128)S(1)} %pad_add_fusion.position, f32[5,5]{1,0:T(8,128)S(1)} %copy-done.3, f32[5,5]{1,0:T(8,128)S(1)} %copy-done.4, f32[5]{0:T(128)S(1)} %copy-done.5, f32[5,256,256]{2,1,0:T(8,128)S(1)} %bitcast.15, f32[5,256,256]{2,1,0:T(8,128)S(1)} %bitcast.17, ...), custom_call_target="tpu_custom_call" | custom-call | tf_op jit(solution)/shard_map/pallas_call | solution.py:221
  22.1 0.1 collective-permute-start.10
  22.2 0.7 %collective-permute-start.7 = (f32[5,48,256]{2,1,0:T(8,128)S(1)}, f32[5,48,256]{2,1,0:T(8,128)S(1)}, u32[]{:S(2)}, u32[]{:S(2)}) collective-permute-start(f32[5,48,256]{2,1,0:T(8,128)S(1)} %get-tuple-element.11.last), channel_id=1, source_target_pairs={{0,0},{8,24},{16,16},{24,8},{1,1},{9,25},{17,17},{25,9},{2,2},{10,... | collective-permute-start | bytes 737288 | tf_op jit(solution)/shard_map/ppermute | solution.py:238
  22.9 8.6 %collective-permute-done.3.following = f32[5,256,256]{2,1,0:T(8,128)S(1)} collective-permute-done((f32[5,256,256]{2,1,0:T(8,128)}, f32[5,256,256]{2,1,0:T(8,128)S(1)}, u32[]{:S(2)}, u32[]{:S(2)}) %collective-permute-start.3) | collective-permute-done | bytes 1310752 | tf_op jit(solution)/shard_map/ppermute | solution.py:233
  31.5 1.3 %shard_map.70 = (f32[5,256,256]{2,1,0:T(8,128)}, f32[5,256,256]{2,1,0:T(8,128)S(1)}, f32[24,256]{1,0:T(8,128)S(1)}) custom-call(f32[5,208,256]{2,1,0:T(8,128)S(1)} %get-tuple-element.10.lead, f32[5,48,256]{2,1,0:T(8,128)S(1)} %get-tuple-element.11.last, f32[5,256,256]{2,1,0:T(8,128)S(1)} %collective-permute-done.3.following), custom_call_target="tpu_custom_call" | custom-call | tf_op jit(solution)/shard_map/pallas_call | solution.py:164
  32.7 2.7 %collective-permute-start.4 = (f32[24,256]{1,0:T(8,128)S(1)}, f32[24,256]{1,0:T(8,128)S(1)}, u32[]{:S(2)}, u32[]{:S(2)}) collective-permute-start(f32[24,256]{1,0:T(8,128)S(1)} %get-tuple-element.14), channel_id=1, source_target_pairs={{0,1},{1,0},{2,3},{3,2},{4,5},{5,4},{6,7},{7,6},{8,9},{9,8},{10,11... | collective-permute-start | bytes 73736 | tf_op jit(solution)/shard_map/ppermute | solution.py:200
  35.4 0.8 %collective-permute-done.4.strip = f32[24,256]{1,0:T(8,128)S(1)} collective-permute-done((f32[24,256]{1,0:T(8,128)S(1)}, f32[24,256]{1,0:T(8,128)S(1)}, u32[]{:S(2)}, u32[]{:S(2)}) %collective-permute-start.4) | collective-permute-done | bytes 24608 | tf_op jit(solution)/shard_map/ppermute | solution.py:200
  36.3 3.4 %collective-permute-start.6 = (f32[5,8,384]{2,1,0:T(8,128)S(1)}, f32[5,8,384]{2,1,0:T(8,128)S(1)}, u32[]{:S(2)}, u32[]{:S(2)}) collective-permute-start(f32[5,8,384]{2,1,0:T(8,128)S(1)} %select_maximum_fusion), channel_id=1, source_target_pairs={{2,0},{4,2},{6,4},{0,6},{3,1},{5,3},{7,5},{1,7},{10,8},{12,10},{14... | collective-permute-start | bytes 184328 | tf_op jit(solution)/shard_map/ppermute | solution.py:214
  39.7 0.0 collective-permute-start.5
  39.7 0.0 collective-permute-done.7
  39.7 0.7 %collective-permute-start.8 = (f32[5,48,256]{2,1,0:T(8,128)S(1)}, f32[5,48,256]{2,1,0:T(8,128)S(1)}, u32[]{:S(2)}, u32[]{:S(2)}) collective-permute-start(f32[5,48,256]{2,1,0:T(8,128)S(1)} %collective-permute-done.7), channel_id=1, source_target_pairs={{0,8},{8,0},{16,24},{24,16},{2,10},{10,2},{18,26},{26,18},{4,12},{... | collective-permute-start | bytes 737288 | tf_op jit(solution)/shard_map/ppermute | solution.py:242
  40.4 0.6 collective-permute-done.6.lower
  41.0 3.6 %collective-permute-done.5.upper = f32[5,8,384]{2,1,0:T(8,128)S(1)} collective-permute-done((f32[5,8,384]{2,1,0:T(8,128)S(1)}, f32[5,8,384]{2,1,0:T(8,128)S(1)}, u32[]{:S(2)}, u32[]{:S(2)}) %collective-permute-start.5) | collective-permute-done | bytes 61472 | tf_op jit(solution)/shard_map/ppermute | solution.py:213
  44.6 8.4 %shard_map.71 = (f32[5,208,256]{2,1,0:T(8,128)S(1)}, f32[5,48,256]{2,1,0:T(8,128)S(1)}) custom-call(s32[2]{0:T(128)S(1)} %pad_add_fusion.position, f32[5,5]{1,0:T(8,128)S(1)} %copy-done.3, f32[5,5]{1,0:T(8,128)S(1)} %copy-done.4, f32[5]{0:T(128)S(1)} %copy-done.5, f32[5,256,256]{2,1,0:T(8,128)S(1)} %get-tuple-element.13.cells, f32[5,256,256]{2,1,0:T(8,128)S(1)} %bitcast.16, ...), custom_call_target="tpu_custom_call" | custom-call | tf_op jit(solution)/shard_map/pallas_call | solution.py:221
  53.0 3.9 %collective-permute-start.9 = (f32[5,48,256]{2,1,0:T(8,128)S(1)}, f32[5,48,256]{2,1,0:T(8,128)S(1)}, u32[]{:S(2)}, u32[]{:S(2)}) collective-permute-start(f32[5,48,256]{2,1,0:T(8,128)S(1)} %collective-permute-done.7), channel_id=1, source_target_pairs={{1,9},{9,1},{17,25},{25,17},{3,11},{11,3},{19,27},{27,19},{5,13},{... | collective-permute-start | bytes 737288 | tf_op jit(solution)/shard_map/ppermute | solution.py:242
  56.9 0.0 collective-permute-done.10.arrived
  56.9 1.1 %shard_map.72.begun = f32[1,5,256,256]{3,2,1,0:T(8,128)} custom-call(f32[5,208,256]{2,1,0:T(8,128)S(1)} %get-tuple-element.16.adjoint, f32[5,208,256]{2,1,0:T(8,128)S(1)} %collective-permute-done.10.arrived), custom_call_target="tpu_custom_call" | custom-call | tf_op jit(solution)/shard_map/pallas_call | solution.py:177
  58.0 0.0 collective-permute-done.8.early
  58.0 2.6 %collective-permute-done.9.late = f32[5,48,256]{2,1,0:T(8,128)S(1)} collective-permute-done((f32[5,48,256]{2,1,0:T(8,128)S(1)}, f32[5,48,256]{2,1,0:T(8,128)S(1)}, u32[]{:S(2)}, u32[]{:S(2)}) %collective-permute-start.9) | collective-permute-done | bytes 245792 | tf_op jit(solution)/shard_map/ppermute | solution.py:242
  60.6 0.7 %shard_map.73 = f32[1,5,256,256]{3,2,1,0:T(8,128)} custom-call(f32[5,48,256]{2,1,0:T(8,128)S(1)} %get-tuple-element.15.adjoint, f32[5,48,256]{2,1,0:T(8,128)S(1)} %collective-permute-done.8.early, f32[5,48,256]{2,1,0:T(8,128)S(1)} %collective-permute-done.9.late, f32[1,5,256,256]{3,2,1,0:T(8,128)} %shard_map.72.begun), custom_call_target="tpu_custom_call", output_to_operand_aliasing={{}: (3, {})} | custom-call | tf_op jit(solution)/shard_map/pallas_call | solution.py:185
  (8 shorter events, 0.0 us)
Async XLA Ops:
  0.6 11.6 %copy-start.5 = (f32[5]{0:T(128)S(1)}, f32[5]{0:T(128)}, u32[]{:S(2)}) copy-start(f32[5]{0:T(128)} %viscous.3) | copy-start | bytes 64
  0.6 30.9 %collective-permute-start.3 = (f32[5,256,256]{2,1,0:T(8,128)}, f32[5,256,256]{2,1,0:T(8,128)S(1)}, u32[]{:S(2)}, u32[]{:S(2)}) collective-permute-start(f32[5,256,256]{2,1,0:T(8,128)} %bitcast.12), channel_id=1, source_target_pairs={{0,24},{8,0},{16,8},{24,16},{1,25},{9,1},{17,9},{25,17},{2,26},{10... | collective-permute-start | bytes 3932168 | tf_op jit(solution)/shard_map/ppermute | solution.py:233
  3.7 1.4 %copy-start = (f32[1,5,256,256]{3,2,1,0:T(8,128)S(1)}, f32[1,5,256,256]{3,2,1,0:T(8,128)}, u32[]{:S(2)}) copy-start(f32[1,5,256,256]{3,2,1,0:T(8,128)} %param.5) | copy-start | bytes 3932164
  5.0 7.2 %copy-start.1 = (f32[1,5,256,256]{3,2,1,0:T(8,128)S(1)}, f32[1,5,256,256]{3,2,1,0:T(8,128)}, u32[]{:S(2)}) copy-start(f32[1,5,256,256]{3,2,1,0:T(8,128)} %param.5) | copy-start | bytes 3932164
  5.0 7.2 %copy-start.3 = (f32[5,5]{1,0:T(8,128)S(1)}, f32[5,5]{1,0:T(8,128)}, u32[]{:S(2)}) copy-start(f32[5,5]{1,0:T(8,128)} %mat_pitch.3) | copy-start | bytes 304
  5.0 7.2 %copy-start.4 = (f32[5,5]{1,0:T(8,128)S(1)}, f32[5,5]{1,0:T(8,128)}, u32[]{:S(2)}) copy-start(f32[5,5]{1,0:T(8,128)} %mat_span.3) | copy-start | bytes 304
  5.3 1.8 %collective-permute-start = (f32[24,256]{1,0:T(8,128)S(1)}, f32[24,256]{1,0:T(8,128)S(1)}, u32[]{:S(2)}, u32[]{:S(2)}) collective-permute-start(f32[24,256]{1,0:T(8,128)S(1)} %shard_map.68), channel_id=1, source_target_pairs={{0,1},{1,0},{2,3},{3,2},{4,5},{5,4},{6,7},{7,6},{8,9},{9,8},{10,11... | collective-permute-start | bytes 73736 | tf_op jit(solution)/shard_map/ppermute | solution.py:200
  7.2 5.1 %collective-permute-start.1 = (f32[5,8,384]{2,1,0:T(8,128)S(1)}, f32[5,8,384]{2,1,0:T(8,128)S(1)}, u32[]{:S(2)}, u32[]{:S(2)}) collective-permute-start(f32[5,8,384]{2,1,0:T(8,128)S(1)} %select_maximum_fusion.3), channel_id=1, source_target_pairs={{0,2},{2,4},{4,6},{6,0},{1,3},{3,5},{5,7},{7,1},{8,10},{10,12},{12... | collective-permute-start | bytes 184328 | tf_op jit(solution)/shard_map/ppermute | solution.py:213
  8.5 3.7 %collective-permute-start.2 = (f32[5,8,384]{2,1,0:T(8,128)S(1)}, f32[5,8,384]{2,1,0:T(8,128)S(1)}, u32[]{:S(2)}, u32[]{:S(2)}) collective-permute-start(f32[5,8,384]{2,1,0:T(8,128)S(1)} %select_maximum_fusion.2), channel_id=1, source_target_pairs={{2,0},{4,2},{6,4},{0,6},{3,1},{5,3},{7,5},{1,7},{10,8},{12,10},{14... | collective-permute-start | bytes 184328 | tf_op jit(solution)/shard_map/ppermute | solution.py:214
  12.3 1.3 %copy-start.2 = (f32[1,5,256,256]{3,2,1,0:T(8,128)S(1)}, f32[1,5,256,256]{3,2,1,0:T(8,128)}, u32[]{:S(2)}) copy-start(f32[1,5,256,256]{3,2,1,0:T(8,128)} %param.6) | copy-start | bytes 3932164
  22.1 34.8 %collective-permute-start.10 = (f32[5,208,256]{2,1,0:T(8,128)S(1)}, f32[5,208,256]{2,1,0:T(8,128)S(1)}, u32[]{:S(2)}, u32[]{:S(2)}) collective-permute-start(f32[5,208,256]{2,1,0:T(8,128)S(1)} %get-tuple-element.10.lead), channel_id=1, source_target_pairs={{0,8},{8,16},{16,24},{24,0},{1,9},{9,17},{17,25},{25,1},{2,10},{10... | collective-permute-start | bytes 3194888 | tf_op jit(solution)/shard_map/ppermute | solution.py:233
  22.2 17.5 %collective-permute-start.7 = (f32[5,48,256]{2,1,0:T(8,128)S(1)}, f32[5,48,256]{2,1,0:T(8,128)S(1)}, u32[]{:S(2)}, u32[]{:S(2)}) collective-permute-start(f32[5,48,256]{2,1,0:T(8,128)S(1)} %get-tuple-element.11.last), channel_id=1, source_target_pairs={{0,0},{8,24},{16,16},{24,8},{1,1},{9,25},{17,17},{25,9},{2,2},{10,... | collective-permute-start | bytes 737288 | tf_op jit(solution)/shard_map/ppermute | solution.py:238
  32.7 3.5 %collective-permute-start.4 = (f32[24,256]{1,0:T(8,128)S(1)}, f32[24,256]{1,0:T(8,128)S(1)}, u32[]{:S(2)}, u32[]{:S(2)}) collective-permute-start(f32[24,256]{1,0:T(8,128)S(1)} %get-tuple-element.14), channel_id=1, source_target_pairs={{0,1},{1,0},{2,3},{3,2},{4,5},{5,4},{6,7},{7,6},{8,9},{9,8},{10,11... | collective-permute-start | bytes 73736 | tf_op jit(solution)/shard_map/ppermute | solution.py:200
  36.3 4.7 %collective-permute-start.6 = (f32[5,8,384]{2,1,0:T(8,128)S(1)}, f32[5,8,384]{2,1,0:T(8,128)S(1)}, u32[]{:S(2)}, u32[]{:S(2)}) collective-permute-start(f32[5,8,384]{2,1,0:T(8,128)S(1)} %select_maximum_fusion), channel_id=1, source_target_pairs={{2,0},{4,2},{6,4},{0,6},{3,1},{5,3},{7,5},{1,7},{10,8},{12,10},{14... | collective-permute-start | bytes 184328 | tf_op jit(solution)/shard_map/ppermute | solution.py:214
  39.7 4.9 %collective-permute-start.5 = (f32[5,8,384]{2,1,0:T(8,128)S(1)}, f32[5,8,384]{2,1,0:T(8,128)S(1)}, u32[]{:S(2)}, u32[]{:S(2)}) collective-permute-start(f32[5,8,384]{2,1,0:T(8,128)S(1)} %select_maximum_fusion.1), channel_id=1, source_target_pairs={{0,2},{2,4},{4,6},{6,0},{1,3},{3,5},{5,7},{7,1},{8,10},{10,12},{12... | collective-permute-start | bytes 184328 | tf_op jit(solution)/shard_map/ppermute | solution.py:213
  39.7 18.3 %collective-permute-start.8 = (f32[5,48,256]{2,1,0:T(8,128)S(1)}, f32[5,48,256]{2,1,0:T(8,128)S(1)}, u32[]{:S(2)}, u32[]{:S(2)}) collective-permute-start(f32[5,48,256]{2,1,0:T(8,128)S(1)} %collective-permute-done.7), channel_id=1, source_target_pairs={{0,8},{8,0},{16,24},{24,16},{2,10},{10,2},{18,26},{26,18},{4,12},{... | collective-permute-start | bytes 737288 | tf_op jit(solution)/shard_map/ppermute | solution.py:242
  53.0 7.7 %collective-permute-start.9 = (f32[5,48,256]{2,1,0:T(8,128)S(1)}, f32[5,48,256]{2,1,0:T(8,128)S(1)}, u32[]{:S(2)}, u32[]{:S(2)}) collective-permute-start(f32[5,48,256]{2,1,0:T(8,128)S(1)} %collective-permute-done.7), channel_id=1, source_target_pairs={{1,9},{9,1},{17,25},{25,17},{3,11},{11,3},{19,27},{27,19},{5,13},{... | collective-permute-start | bytes 737288 | tf_op jit(solution)/shard_map/ppermute | solution.py:242
